TPU v7x, 32 devices: a whole 2x2x4 slice. The times are simulated.
32 devices in a mesh: dp: 8 (over z, core), mp: 4 (over y, x).
Axes of the slice: x: 2, y: 2, z: 4, core: 2. Of those that a mesh axis runs over, the one named last changes fastest.
Arguments:
- tokens: bfloat16 [16384, 768], P(('dp', 'mp')), may hold values from -6 to 6
- segments: int32 [32, 512], P(('dp', 'mp')), may hold values from 0 to 3, never falling along the last dimension, each value on 1 to 256 neighbouring positions
- routes: int32 [2, 16384, 1], P(None, ('dp', 'mp')), may hold values from 0 to 7; in each aligned block of 512 rows (0 to 511, 512 to 1023, ..., all dimensions but the last counted through in order) at most 72 rows name the same one
- gain_attn: float32 [2, 768], replicated, may hold values from 0.5 to 1.5
- qkv_weight: bfloat16 [2, 768, 2304], replicated, may hold values from -0.21875 to 0.21875
- out_weight: bfloat16 [2, 768, 768], replicated, may hold values from -2.5 to 2.5
- rel_bias: float32 [2, 32, 12], replicated, may hold values from -4 to 4
- gain_ffn: float32 [2, 768], replicated, may hold values from 0.5 to 1.5
- router_weight: float32 [2, 768, 8], replicated, may hold values from -0.109375 to 0.109375
- w_in: bfloat16 [2, 8, 768, 3072], P(None, 'dp', None, 'mp'), may hold values from -0.21875 to 0.21875
- w_out: bfloat16 [2, 8, 3072, 768], P(None, 'dp', 'mp'), may hold values from -1.25 to 1.25
- cotangent: bfloat16 [16384, 768], P(('dp', 'mp')), may hold values from -6 to 6
Outputs:
- output: float32 [16384, 768], P(('dp', 'mp'))
- grad_tokens: float32 [16384, 768], P(('dp', 'mp'))
- grad_gain_attn: float32 [2, 768], replicated
- grad_qkv: float32 [2, 768, 2304], replicated
- grad_out_weight: float32 [2, 768, 768], replicated
- grad_rel_bias: float32 [2, 32, 12], replicated
- grad_gain_ffn: float32 [2, 768], replicated
- grad_router: float32 [2, 768, 8], replicated
- grad_w_in: float32 [2, 8, 768, 3072], P(None, 'dp', None, 'mp')
- grad_w_out: float32 [2, 8, 3072, 768], P(None, 'dp', 'mp')
Inputs may be any that keep to these rules, and one draw needn't show every extreme that they name: `routes`: in every layer the 512 rows of one device name no expert more than 72 times, and some device's rows name some expert exactly 72 times. `segments`: along each pack segment numbers never fall; a segment holds at most half of the 512 positions.
All inputs are finite; a program needn't handle non-finite values.
Results may differ from a plain program's by a relative error of at most 0.02.
Values may be sent and summed in bfloat16 or wider, within the bound.
No kernel may reach another device: no remote copies, remote signals or barrier semaphores. Data moves between devices by JAX's collectives and lax.ppermute only.
A program may use at most 320 MiB of HBM per device.

v0:
```python
import jax
import jax.numpy as jnp
import numpy as np
from jax import lax
from jax.sharding import PartitionSpec as P

HEAD_DIM = 64
BUCKETS = 32
MAX_DIST = 128
LAYERS = 2
LEN = 512


epsilon = 1e-06
masked_score = -1000000000.0
highest = lax.Precision.HIGHEST


def bucket_limits():
    half_count = BUCKETS // 2
    exact_count = half_count // 2
    lengths = np.arange(exact_count, 4 * MAX_DIST + 2 * LEN + 2)
    levels = (
        np.log(lengths / exact_count) / np.log(MAX_DIST / exact_count) * (half_count - exact_count)
    ).astype(np.int64)
    levels = np.minimum(levels, half_count - exact_count - 1)
    limits = []
    for target in range(1, half_count - exact_count):
        limits.append(int(lengths[np.argmax(levels >= target)]))
    return limits


def bucket_of(distance):
    half_count = BUCKETS // 2
    exact_count = half_count // 2
    magnitude = jnp.abs(distance)
    counted = jnp.full(distance.shape, exact_count, jnp.int32)
    for limit_value in bucket_limits():
        counted = counted + (magnitude >= limit_value).astype(jnp.int32)
    return jnp.where(distance > 0, half_count, 0) + jnp.where(
        magnitude < exact_count, magnitude, counted
    )


def distance_onehot():
    distance = jnp.arange(-(LEN - 1), LEN, dtype=jnp.int32)
    buckets = bucket_of(distance)
    return (buckets[:, None] == jnp.arange(BUCKETS, dtype=jnp.int32)[None, :]).astype(jnp.float32)


def rms_apply(values, gain):
    factor = lax.rsqrt(jnp.mean(values * values, axis=-1, keepdims=True) + epsilon)
    return values * factor * gain


def router_gates(normed, weights, onehot):
    logits = jnp.dot(normed, weights, precision=highest)
    shifted = logits - jnp.max(logits, axis=-1, keepdims=True)
    powers = jnp.exp(shifted)
    probability = powers / jnp.sum(powers, axis=-1, keepdims=True)
    return jnp.sum(probability * onehot, axis=-1)


def diagonal_rows(dist_table, first_row, block_rows):
    span_width = LEN + block_rows - 1
    window_start = LEN - block_rows - first_row
    window = dist_table[:, window_start : window_start + span_width]
    tiled = jnp.tile(window, (1, block_rows))
    sheared = tiled[:, block_rows - 1 : block_rows - 1 + block_rows * (span_width - 1)]
    return sheared.reshape(dist_table.shape[0], block_rows, span_width - 1)[:, :, :LEN]


def diagonal_sums(score_grad):
    head_count = score_grad.shape[0]
    block_rows = score_grad.shape[1]
    span_width = LEN + block_rows - 1
    padded = jnp.pad(score_grad, ((0, 0), (0, 0), (0, span_width - 1 - LEN)))
    flat = padded.reshape(head_count, block_rows * (span_width - 1))
    flat = jnp.pad(flat, ((0, 0), (block_rows - 1, 1)))
    window = jnp.sum(flat.reshape(head_count, block_rows, span_width), axis=1, dtype=jnp.float32)
    return window


def block_scores(query_rows, key_heads, seg_rows, seg_all, bias_rows):
    scores = (
        jnp.einsum("ihd,jhd->hij", query_rows, key_heads, preferred_element_type=jnp.float32)
        * HEAD_DIM ** (-0.5)
        + bias_rows
    )
    same_segment = seg_rows[:, None] == seg_all[None, :]
    return jnp.where(same_segment[None], scores, masked_score)


def attention_forward(qkv_rows, seg_pack, dist_table):
    head_count = dist_table.shape[0]
    block_rows = min(512, LEN)
    heads_view = qkv_rows.reshape(LEN, 3, head_count, HEAD_DIM)
    queries = heads_view[:, 0]
    key_heads = heads_view[:, 1]
    value_heads = heads_view[:, 2]
    scores = block_scores(
        queries, key_heads, seg_pack, seg_pack, diagonal_rows(dist_table, 0, block_rows)
    )
    row_max = jnp.max(scores, axis=-1, keepdims=True)
    powers = jnp.exp(scores - row_max)
    row_total = jnp.sum(powers, axis=-1, keepdims=True)
    probability = (powers / row_total).astype(jnp.bfloat16)
    mixed_rows = jnp.einsum(
        "hij,jhd->ihd", probability, value_heads, preferred_element_type=jnp.float32
    )
    mixed_parts = mixed_rows.reshape(block_rows, head_count * HEAD_DIM)
    lse_parts = (row_max + jnp.log(row_total))[:, :, 0]
    return (mixed_parts.astype(jnp.bfloat16), lse_parts)


def attention_backward(qkv_rows, seg_pack, dist_table, lse_pack, grad_rows):
    head_count = dist_table.shape[0]
    block_rows = min(512, LEN)
    score_scale = HEAD_DIM ** (-0.5)
    heads_view = qkv_rows.reshape(LEN, 3, head_count, HEAD_DIM)
    queries = heads_view[:, 0]
    key_heads = heads_view[:, 1]
    value_heads = heads_view[:, 2]
    grad_heads = grad_rows.reshape(LEN, head_count, HEAD_DIM)
    key_grad = jnp.zeros((LEN, head_count, HEAD_DIM), jnp.float32)
    value_grad = jnp.zeros((LEN, head_count, HEAD_DIM), jnp.float32)
    table_grad = jnp.zeros(dist_table.shape, jnp.float32)
    scores = block_scores(
        queries, key_heads, seg_pack, seg_pack, diagonal_rows(dist_table, 0, block_rows)
    )
    probability = jnp.exp(scores - lse_pack[:, 0:block_rows, None])
    prob_grad = jnp.einsum(
        "ihd,jhd->hij", grad_heads, value_heads, preferred_element_type=jnp.float32
    )
    delta = jnp.sum(probability * prob_grad, axis=-1, keepdims=True)
    score_grad = (probability * (prob_grad - delta)).astype(jnp.bfloat16)
    table_grad = table_grad + diagonal_sums(score_grad)
    query_parts = (
        jnp.einsum("hij,jhd->ihd", score_grad, key_heads, preferred_element_type=jnp.float32)
        * score_scale
    )
    key_grad = (
        key_grad
        + jnp.einsum("hij,ihd->jhd", score_grad, queries, preferred_element_type=jnp.float32)
        * score_scale
    )
    value_grad = value_grad + jnp.einsum(
        "hij,ihd->jhd",
        probability.astype(jnp.bfloat16),
        grad_heads,
        preferred_element_type=jnp.float32,
    )
    stacked = jnp.stack([query_parts, key_grad, value_grad], axis=1)
    return (stacked.reshape(LEN, 3 * head_count * HEAD_DIM).astype(jnp.bfloat16), table_grad)


def body(
    tokens,
    segments,
    routes,
    gain_attn,
    qkv_weight,
    out_weight,
    rel_bias,
    gain_ffn,
    router_weight,
    w_in,
    w_out,
    cotangent,
):
    tok_count = tokens.shape[0]
    model_width = tokens.shape[1]
    local_experts = w_in.shape[1]
    expert_total = local_experts * lax.axis_size("dp")
    capacity = (tok_count * 9 + 8 * expert_total - 1) // (8 * expert_total)
    dist_onehot = distance_onehot()
    expert_ids = jnp.arange(expert_total, dtype=jnp.int32)
    values = tokens.astype(jnp.float32)
    stored = []
    for layer_index in range(LAYERS):
        normed_attn = rms_apply(values, gain_attn[layer_index]).astype(jnp.bfloat16)
        projected = jnp.dot(
            normed_attn, qkv_weight[layer_index], preferred_element_type=jnp.float32
        ).astype(jnp.bfloat16)
        dist_table = jnp.dot(dist_onehot, rel_bias[layer_index], precision=highest).T
        lse_list = []
        pack_index = 0
        mixed_pack, lse_pack = attention_forward(projected, segments[pack_index], dist_table)
        lse_list.append(lse_pack)
        mixed = mixed_pack
        middle = values + jnp.dot(
            mixed, out_weight[layer_index], preferred_element_type=jnp.float32
        )
        normed_ffn = rms_apply(middle, gain_ffn[layer_index]).astype(jnp.bfloat16)
        chosen = routes[layer_index, :, 0]
        onehot_int = (chosen[:, None] == expert_ids[None, :]).astype(jnp.int32)
        slot_index = jnp.sum(jnp.cumsum(onehot_int, axis=0) * onehot_int, axis=-1) - 1
        onehot_float = onehot_int.astype(jnp.float32)
        gate_values = router_gates(
            normed_ffn.astype(jnp.float32), router_weight[layer_index], onehot_float
        )
        buffer = (
            jnp.zeros((capacity, expert_total, model_width), jnp.bfloat16)
            .at[slot_index, chosen]
            .set(normed_ffn)
        )
        arrived = lax.all_to_all(buffer, "dp", split_axis=1, concat_axis=0, tiled=True)
        w_in_layer = w_in[layer_index]
        w_out_layer = w_out[layer_index]
        rows_all = lax.all_gather(arrived, "mp", axis=0, tiled=True)
        hidden = jnp.einsum(
            "red,edf->ref", rows_all, w_in_layer, preferred_element_type=jnp.float32
        )
        active = jax.nn.gelu(hidden).astype(jnp.bfloat16)
        summed = lax.psum_scatter(
            jnp.einsum(
                "ref,efd->red", active, w_out_layer, preferred_element_type=jnp.float32
            ).astype(jnp.bfloat16),
            "mp",
            scatter_dimension=0,
            tiled=True,
        )
        expert_keep = (rows_all, hidden)
        back = lax.all_to_all(summed, "dp", split_axis=0, concat_axis=1, tiled=True)
        returned = back[slot_index, chosen]
        stored.append(
            (
                values,
                normed_attn,
                projected,
                mixed,
                lse_list,
                dist_table,
                middle,
                normed_ffn,
                chosen,
                slot_index,
                onehot_float,
                gate_values,
                returned,
                expert_keep,
            )
        )
        values = middle + gate_values[:, None] * returned.astype(jnp.float32)
    gradient = cotangent.astype(jnp.float32)
    layer_results = []
    for layer_index in reversed(range(LAYERS)):
        (
            layer_input,
            normed_attn,
            projected,
            mixed,
            lse_list,
            dist_table,
            middle,
            normed_ffn,
            chosen,
            slot_index,
            onehot_float,
            gate_values,
            returned,
            expert_keep,
        ) = stored[layer_index]
        w_in_layer = w_in[layer_index]
        w_out_layer = w_out[layer_index]
        gate_grad = jnp.sum(gradient * returned.astype(jnp.float32), axis=-1)
        expert_grad = (gate_values[:, None] * gradient).astype(jnp.bfloat16)
        grad_buffer = (
            jnp.zeros((capacity, expert_total, model_width), jnp.bfloat16)
            .at[slot_index, chosen]
            .set(expert_grad)
        )
        grad_arrived = lax.all_to_all(grad_buffer, "dp", split_axis=1, concat_axis=0, tiled=True)
        rows_all, hidden = expert_keep
        grad_rows_all = lax.all_gather(grad_arrived, "mp", axis=0, tiled=True)
        act_grad = jnp.einsum(
            "red,efd->ref", grad_rows_all, w_out_layer, preferred_element_type=jnp.float32
        )
        active, gelu_pull = jax.vjp(jax.nn.gelu, hidden)
        hidden_grad = gelu_pull(act_grad)[0].astype(jnp.bfloat16)
        grad_w_out_layer = jnp.einsum(
            "ref,red->efd",
            active.astype(jnp.bfloat16),
            grad_rows_all,
            preferred_element_type=jnp.float32,
        )
        grad_w_in_layer = jnp.einsum(
            "red,ref->edf", rows_all, hidden_grad, preferred_element_type=jnp.float32
        )
        sent_grad = lax.psum_scatter(
            jnp.einsum("ref,edf->red", hidden_grad, w_in_layer, preferred_element_type=jnp.float32),
            "mp",
            scatter_dimension=0,
            tiled=True,
        )
        grad_back = lax.all_to_all(
            sent_grad.astype(jnp.bfloat16), "dp", split_axis=0, concat_axis=1, tiled=True
        )
        expert_part = grad_back[slot_index, chosen].astype(jnp.float32)
        router_layer = router_weight[layer_index]
        unused_gates, router_pull = jax.vjp(
            lambda normed, weights: router_gates(normed, weights, onehot_float),
            normed_ffn.astype(jnp.float32),
            router_layer,
        )
        router_normed_grad, grad_router_layer = router_pull(gate_grad)
        normed_grad = router_normed_grad + expert_part
        unused_norm, norm_pull = jax.vjp(rms_apply, middle, gain_ffn[layer_index])
        middle_norm_grad, grad_gain_ffn_layer = norm_pull(normed_grad)
        middle_grad = gradient + middle_norm_grad
        att_grad = middle_grad.astype(jnp.bfloat16)
        grad_out_layer = jnp.einsum(
            "td,te->de", mixed, att_grad, preferred_element_type=jnp.float32
        )
        mixed_grad = jnp.einsum(
            "te,de->td", att_grad, out_weight[layer_index], preferred_element_type=jnp.float32
        ).astype(jnp.bfloat16)
        table_grad = jnp.zeros(dist_table.shape, jnp.float32)
        pack_index = 0
        proj_pack, table_pack = attention_backward(
            projected, segments[pack_index], dist_table, lse_list[pack_index], mixed_grad
        )
        table_grad = table_grad + table_pack
        grad_rel_layer = jnp.dot(dist_onehot.T, table_grad.T, precision=highest)
        grad_qkv_layer = jnp.einsum(
            "td,te->de", normed_attn, proj_pack, preferred_element_type=jnp.float32
        )
        normed_attn_grad = jnp.einsum(
            "te,de->td", proj_pack, qkv_weight[layer_index], preferred_element_type=jnp.float32
        )
        unused_input, input_pull = jax.vjp(rms_apply, layer_input, gain_attn[layer_index])
        input_norm_grad, grad_gain_attn_layer = input_pull(normed_attn_grad)
        gradient = middle_grad + input_norm_grad
        layer_results.append(
            (
                grad_gain_attn_layer,
                grad_qkv_layer,
                grad_out_layer,
                grad_rel_layer,
                grad_gain_ffn_layer,
                grad_router_layer,
                grad_w_in_layer,
                grad_w_out_layer,
            )
        )
    layer_results = layer_results[::-1]
    grad_gain_attn = jnp.stack([entry[0] for entry in layer_results])
    grad_qkv = jnp.stack([entry[1] for entry in layer_results])
    grad_out_weight = jnp.stack([entry[2] for entry in layer_results])
    grad_rel_bias = jnp.stack([entry[3] for entry in layer_results])
    grad_gain_ffn = jnp.stack([entry[4] for entry in layer_results])
    grad_router = jnp.stack([entry[5] for entry in layer_results])
    grad_w_in = jnp.stack([entry[6] for entry in layer_results])
    grad_w_out = jnp.stack([entry[7] for entry in layer_results])
    grad_gain_attn, grad_qkv, grad_out_weight, grad_rel_bias, grad_gain_ffn, grad_router = lax.psum(
        (grad_gain_attn, grad_qkv, grad_out_weight, grad_rel_bias, grad_gain_ffn, grad_router),
        ("dp", "mp"),
    )
    return (
        values,
        gradient,
        grad_gain_attn,
        grad_qkv,
        grad_out_weight,
        grad_rel_bias,
        grad_gain_ffn,
        grad_router,
        grad_w_in,
        grad_w_out,
    )


def solution(mesh):
    return jax.shard_map(
        body,
        mesh=mesh,
        in_specs=(
            P(("dp", "mp"), None),
            P(("dp", "mp"), None),
            P(None, ("dp", "mp"), None),
            P(),
            P(),
            P(),
            P(),
            P(),
            P(),
            P(None, "dp", None, "mp"),
            P(None, "dp", "mp", None),
            P(("dp", "mp"), None),
        ),
        out_specs=(
            P(("dp", "mp"), None),
            P(("dp", "mp"), None),
            P(),
            P(),
            P(),
            P(),
            P(),
            P(),
            P(None, "dp", None, "mp"),
            P(None, "dp", "mp", None),
        ),
        check_vma=False,
    )
```

profile of v0, /device:TPU:0, one launch (start us, length us, event | category | flops | bytes accessed | tf_op | source)
XLA Modules:
  0.0 1785.1 jit_solution(2624858879631590853)
XLA Ops:
  11.2 5.7 convolution_convert_fusion.3
  20.3 11.5 tile.8
  31.8 38.0 %tile.9 = f32[12,523776]{1,0:T(8,128)} reshape(f32[12,512,1023]{2,1,0:T(8,128)} %tile.8) | data formatting | bytes 50282496 | tf_op jit(solution)/shard_map/tile | solution.py:68
  69.8 25.5 %slice.171 = f32[12,523264]{1,0:T(8,128)} slice(f32[12,523776]{1,0:T(8,128)} %tile.9), slice={[0:12], [511:523775]} | slice | bytes 50233344 | tf_op jit(solution)/shard_map/slice | solution.py:69
  95.3 53.6 %reshape.492 = f32[12,512,1022]{2,1,0:T(8,128)} reshape(f32[12,523264]{1,0:T(8,128)} %slice.171) | data formatting | bytes 50233344 | tf_op jit(solution)/shard_map/reshape | solution.py:70
  148.9 10.9 slice.172
  159.8 12.6 copy.166
  172.6 6.3 fusion.212
  191.8 28.5 %scatter_fusion = bf16[72,8,768]{2,1,0:T(8,128)(2,1)S(1)} fusion(bf16[72,8,768]{2,1,0:T(8,128)(2,1)S(1)} %broadcast.365.clone, s32[512]{0:T(512)S(1)} %bitcast.451, bf16[512,768]{1,0:T(8,128)(2,1)S(1)} %multiply_convert_fusion.5), kind=kCustom, calls=%fused_computation.4 | custom fusion | bytes 2363392 | tf_op jit(solution)/shard_map/scatter | solution.py:205
  220.6 29.2 %all_to_all.144 = bf16[72,8,768]{2,0,1:T(8,128)(2,1)} all-to-all(bf16[72,8,768]{2,0,1:T(8,128)(2,1)S(1)} %copy.126), channel_id=1, replica_groups=mesh['dp'=8,'mp'=4] {'dp'}, dimensions={1} | all-to-all | bytes 1769472 | tf_op jit(solution)/shard_map/all_to_all | solution.py:207
  249.9 46.3 %all-gather.5.cloned.1.call-done = bf16[2304,1,768]{2,0,1:T(8,128)(2,1)} async-done(((bf16[576,1,768]{2,0,1:T(8,128)(2,1)}), bf16[2304,1,768]{2,0,1:T(8,128)(2,1)}) %all-gather.5.cloned.1.call-update) | async-done | bytes 3538960 | tf_op jit(solution)/shard_map/all_gather | solution.py:210
  304.6 7.0 fusion.34
  311.6 47.4 %reduce-scatter.5.cloned.1.call-done = bf16[576,1,768]{2,0,1:T(8,128)(2,1)} async-done(((bf16[2304,1,768]{2,0,1:T(8,128)(2,1)}), bf16[576,1,768]{2,0,1:T(8,128)(2,1)}) %reduce-scatter.5.cloned.1.call-update) | async-done | bytes 884752 | tf_op jit(solution)/shard_map/reduce_scatter | solution.py:215
  368.1 11.5 tile.10
  379.7 38.4 %tile.11 = f32[12,523776]{1,0:T(8,128)} reshape(f32[12,512,1023]{2,1,0:T(8,128)} %tile.10) | data formatting | bytes 50282496 | tf_op jit(solution)/shard_map/tile | solution.py:68
  418.1 25.5 %slice.177 = f32[12,523264]{1,0:T(8,128)} slice(f32[12,523776]{1,0:T(8,128)} %tile.11), slice={[0:12], [511:523775]} | slice | bytes 50233344 | tf_op jit(solution)/shard_map/slice | solution.py:69
  443.5 42.2 %reshape.499 = f32[12,512,1022]{2,1,0:T(8,128)} reshape(f32[12,523264]{1,0:T(8,128)} %slice.177) | data formatting | bytes 50233344 | tf_op jit(solution)/shard_map/reshape | solution.py:70
  485.7 10.9 slice.178
  496.6 12.6 copy.168
  528.1 7.6 fusion.214
  546.6 28.5 %scatter_fusion.1 = bf16[72,8,768]{2,1,0:T(8,128)(2,1)S(1)} fusion(bf16[72,8,768]{2,1,0:T(8,128)(2,1)S(1)} %broadcast.365.clone.1, s32[512]{0:T(512)S(1)} %bitcast.453, bf16[512,768]{1,0:T(8,128)(2,1)S(1)} %multiply_convert_fusion.3), kind=kCustom, calls=%fused_computation.5 | custom fusion | bytes 2363392 | tf_op jit(solution)/shard_map/scatter | solution.py:205
  575.3 28.0 %all_to_all.145 = bf16[72,8,768]{2,0,1:T(8,128)(2,1)} all-to-all(bf16[72,8,768]{2,0,1:T(8,128)(2,1)S(1)} %copy.133), channel_id=1, replica_groups=mesh['dp'=8,'mp'=4] {'dp'}, dimensions={1} | all-to-all | bytes 1769472 | tf_op jit(solution)/shard_map/all_to_all | solution.py:207
  603.4 45.3 %all-gather.7.cloned.1.call-done = bf16[2304,1,768]{2,0,1:T(8,128)(2,1)} async-done(((bf16[576,1,768]{2,0,1:T(8,128)(2,1)}), bf16[2304,1,768]{2,0,1:T(8,128)(2,1)}) %all-gather.7.cloned.1.call-update) | async-done | bytes 3538960 | tf_op jit(solution)/shard_map/all_gather | solution.py:210
  648.6 5.6 fusion.48
  657.1 5.7 fusion.35
  662.8 47.4 %reduce-scatter.7.cloned.1.call-done = bf16[576,1,768]{2,0,1:T(8,128)(2,1)} async-done(((bf16[2304,1,768]{2,0,1:T(8,128)(2,1)}), bf16[576,1,768]{2,0,1:T(8,128)(2,1)}) %reduce-scatter.7.cloned.1.call-update) | async-done | bytes 884752 | tf_op jit(solution)/shard_map/reduce_scatter | solution.py:215
  719.2 22.2 %all-to-all-done.3 = bf16[8,2,27648]{2,1,0:T(2,128)(2,1)S(1)} async-done(((bf16[8,2,27648]{2,1,0:T(2,128)(2,1)}), bf16[8,2,27648]{2,1,0:T(2,128)(2,1)S(1)}, u32[]{:S(2)}, u32[]{:S(2)}) %all-to-all-start.3) | async-done | bytes 884768 | tf_op jit(solution)/shard_map/all_to_all | solution.py:224
  746.4 7.1 gather_fusion.1
  757.5 46.5 %scatter_fusion.2 = bf16[72,8,768]{2,1,0:T(8,128)(2,1)S(1)} fusion(bf16[72,8,768]{2,1,0:T(8,128)(2,1)S(1)} %broadcast.365.clone.2, s32[512]{0:T(512)S(1)} %bitcast.454, bf16[512,768]{1,0:T(8,128)(2,1)} %fusion.90), kind=kCustom, calls=%fused_computation.6 | custom fusion | bytes 2363392 | tf_op jit(solution)/shard_map/scatter | solution.py:271
  804.2 26.2 %all_to_all.146 = bf16[72,8,768]{2,0,1:T(8,128)(2,1)} all-to-all(bf16[72,8,768]{2,0,1:T(8,128)(2,1)S(1)} %copy.136), channel_id=1, replica_groups=mesh['dp'=8,'mp'=4] {'dp'}, dimensions={1} | all-to-all | bytes 1769472 | tf_op jit(solution)/shard_map/all_to_all | solution.py:273
  830.5 45.2 %all-gather.9.cloned.1.call-done = bf16[2304,1,768]{2,0,1:T(8,128)(2,1)} async-done(((bf16[576,1,768]{2,0,1:T(8,128)(2,1)}), bf16[2304,1,768]{2,0,1:T(8,128)(2,1)}) %all-gather.9.cloned.1.call-update) | async-done | bytes 3538960 | tf_op jit(solution)/shard_map/all_gather | solution.py:275
  875.7 9.5 fusion.36
  892.0 76.9 %reduce-scatter.9.cloned.1.call-done = f32[576,1,768]{2,0,1:T(8,128)} async-done(((f32[2304,1,768]{2,0,1:T(8,128)}), f32[576,1,768]{2,0,1:T(8,128)}) %reduce-scatter.9.cloned.1.call-update) | async-done | bytes 1769488 | tf_op jit(solution)/shard_map/reduce_scatter | solution.py:290
  979.8 23.0 %all-to-all-done.5 = bf16[8,2,27648]{2,1,0:T(2,128)(2,1)S(1)} async-done(((bf16[8,2,27648]{2,1,0:T(2,128)(2,1)}), bf16[8,2,27648]{2,1,0:T(2,128)(2,1)S(1)}, u32[]{:S(2)}, u32[]{:S(2)}) %all-to-all-start.5) | async-done | bytes 884768 | tf_op jit(solution)/shard_map/all_to_all | solution.py:296
  1007.7 7.2 gather_fusion.2
  1024.5 10.7 multiply_reduce_fusion.1
  1037.4 7.4 multiply_convert_fusion.1
  1059.4 46.5 %scatter_fusion.3 = bf16[72,8,768]{2,1,0:T(8,128)(2,1)S(1)} fusion(bf16[72,8,768]{2,1,0:T(8,128)(2,1)S(1)} %broadcast.365, s32[512]{0:T(512)S(1)} %bitcast.452, bf16[512,768]{1,0:T(8,128)(2,1)} %multiply_convert_fusion.2), kind=kCustom, calls=%fused_computation.7 | custom fusion | bytes 2363392 | tf_op jit(solution)/shard_map/scatter | solution.py:271
  1106.1 26.2 %all_to_all.147 = bf16[72,8,768]{2,0,1:T(8,128)(2,1)} all-to-all(bf16[72,8,768]{2,0,1:T(8,128)(2,1)S(1)} %copy.143), channel_id=1, replica_groups=mesh['dp'=8,'mp'=4] {'dp'}, dimensions={1} | all-to-all | bytes 1769472 | tf_op jit(solution)/shard_map/all_to_all | solution.py:273
  1133.0 7.7 fusion.71
  1140.7 7.9 fusion.74
  1148.7 8.7 copy.170
  1157.4 9.2 pad.16.clone
  1166.6 41.2 %reshape.514 = bf16[12,523264]{1,0:T(8,128)(2,1)} reshape(bf16[12,512,1022]{2,1,0:T(8,128)(2,1)} %pad.16.clone) | data formatting | bytes 25116672 | tf_op jit(solution)/shard_map/reshape | solution.py:78
  1207.9 9.3 fusion.37
  1224.1 19.4 %pad_convert_fusion = f32[12,523776]{1,0:T(8,128)} fusion(bf16[12,523264]{1,0:T(8,128)(2,1)} %reshape.514), kind=kLoop, calls=%fused_computation.8 | loop fusion | flops 6285312 | bytes 37699584 | tf_op jit(solution)/shard_map/convert_element_type | solution.py:80
  1243.6 42.2 %reshape.518 = f32[12,512,1023]{2,1,0:T(8,128)} reshape(f32[12,523776]{1,0:T(8,128)} %pad_convert_fusion) | data formatting | bytes 50282496 | tf_op jit(solution)/shard_map/convert_element_type | solution.py:80
  1285.8 9.5 reduce_sum.330
  1312.8 6.3 fusion.68
  1319.1 5.8 fusion.79
  1329.3 6.5 all-to-all-done.7
  1350.9 11.6 multiply_reduce_fusion
  1363.3 7.0 multiply_convert_fusion
  1378.2 8.8 copy.169
  1394.0 9.2 pad.14.clone
  1403.2 41.1 %reshape.513 = bf16[12,523264]{1,0:T(8,128)(2,1)} reshape(bf16[12,512,1022]{2,1,0:T(8,128)(2,1)} %pad.14.clone) | data formatting | bytes 25116672 | tf_op jit(solution)/shard_map/reshape | solution.py:78
  1448.4 11.2 pad_maximum_fusion
  1459.7 19.2 %pad_convert_fusion.1 = f32[12,523776]{1,0:T(8,128)} fusion(bf16[12,523264]{1,0:T(8,128)(2,1)} %reshape.513), kind=kLoop, calls=%fused_computation.9 | loop fusion | flops 6285312 | bytes 37699584 | tf_op jit(solution)/shard_map/convert_element_type | solution.py:80
  1478.9 54.8 %reshape.517 = f32[12,512,1023]{2,1,0:T(8,128)} reshape(f32[12,523776]{1,0:T(8,128)} %pad_convert_fusion.1) | data formatting | bytes 50282496 | tf_op jit(solution)/shard_map/convert_element_type | solution.py:80
  1533.7 9.2 reduce_sum.329
  1542.9 6.4 fusion.85
  1549.7 40.6 %all-reduce.4 = (f32[2,768]{1,0:T(2,128)}, f32[2,32,12]{1,2,0:T(8,128)S(1)}, f32[2,768]{1,0:T(2,128)}, f32[2,768,8]{1,2,0:T(8,128)}) all-reduce(f32[2,768]{1,0:T(2,128)S(1)} %get-tuple-element.126, f32[2,32,12]{1,2,0:T(8,128)S(1)} %pad_maximum_fusion.5, ...), channel_id=1, replica_groups=mesh['dp'=8,'mp'=4] {'dp','mp'}, use_global_device_ids=true, to_apply=%region_44.45 | all-reduce | flops 16128 | bytes 129024 | tf_op jit(solution)/shard_map/psum | solution.py:355
  1594.0 168.2 %all-reduce.8.cloned.1.call-done = (f32[2,768,2304]{2,1,0:T(8,128)}, f32[2,768,768]{2,1,0:T(8,128)}) async-done(((f32[2,768,2304]{2,1,0:T(8,128)}, f32[2,768,768]{2,1,0:T(8,128)}), (f32[2,768,2304]{2,1,0:T(8,128)}, f32[2,768,768]{2,1,0:T(8,128)})) %all-reduce.8.cloned.1.call-update) | async-done | bytes 18874384 | tf_op jit(solution)/shard_map/psum | solution.py:355
  1762.2 11.2 copy.195
  (373 shorter events, 210.5 us)
Async XLA Ops:
  7.2 289.0 %all-gather.5.cloned.1.call-start = ((), (), s32[]{:S(2)}) async-start(), calls=%async_computation.12 | async-start | bytes 4423680 | tf_op jit(solution)/shard_map/all_gather | solution.py:210
  7.2 360.5 %copy-start.87 = (s32[1023]{0:T(1024)}, s32[1023]{0:T(1024)S(1)}, u32[]{:S(2)}) copy-start(s32[1023]{0:T(1024)S(1)} %fusion.168) | copy-start | bytes 12280
  19.8 160.9 %copy-start.13 = (bf16[512,2304]{0,1:T(8,128)(2,1)}, bf16[512,2304]{0,1:T(8,128)(2,1)S(1)}, u32[]{:S(2)}) copy-start(bf16[512,2304]{0,1:T(8,128)(2,1)S(1)} %copy.122) | copy-start | bytes 7077892
  159.8 12.6 copy-start.83
  186.1 5.0 copy-start.42
  187.1 33.3 %copy-start.73 = (f32[512]{0:T(512)}, f32[512]{0:T(512)S(1)}, u32[]{:S(2)}) copy-start(f32[512]{0:T(512)S(1)} %fusion.181) | copy-start | bytes 6148
  187.8 32.6 %copy-start.67 = (f32[768]{0:T(1024)}, f32[768]{0:T(1024)S(1)}, u32[]{:S(2)}) copy-start(f32[768]{0:T(1024)S(1)} %get-tuple-element.71) | copy-start | bytes 9220
  187.8 32.6 %copy-start.62 = (s32[1,512,1]{1,2,0:T(1,128)}, s32[1,512,1]{1,2,0:T(1,128)S(1)}, u32[]{:S(2)}) copy-start(s32[1,512,1]{1,2,0:T(1,128)S(1)} %get-tuple-element.100) | copy-start | bytes 6148
  187.8 322.1 %copy-start.58 = (s32[1,512,1]{1,2,0:T(1,128)}, s32[1,512,1]{1,2,0:T(1,128)S(1)}, u32[]{:S(2)}) copy-start(s32[1,512,1]{1,2,0:T(1,128)S(1)} %get-tuple-element.101) | copy-start | bytes 6148
  191.1 318.1 %copy-start.22 = (bf16[512,768]{1,0:T(8,128)(2,1)}, bf16[512,768]{1,0:T(8,128)(2,1)S(1)}, u32[]{:S(2)}) copy-start(bf16[512,768]{1,0:T(8,128)(2,1)S(1)} %multiply_convert_fusion.5) | copy-start | bytes 2359300
  191.8 28.7 %copy-start.7 = (s32[512,1]{0,1:T(1,128)}, s32[512,1]{0,1:T(1,128)S(1)}, u32[]{:S(2)}) copy-start(s32[512,1]{0,1:T(1,128)S(1)} %get-tuple-element.98) | copy-start | bytes 6148
  191.8 319.8 %copy-start.4 = (s32[512,1]{0,1:T(1,128)}, s32[512,1]{0,1:T(1,128)S(1)}, u32[]{:S(2)}) copy-start(s32[512,1]{0,1:T(1,128)S(1)} %get-tuple-element.99) | copy-start | bytes 6148
  249.9 109.1 %reduce-scatter.5.cloned.1.call-start = ((), (), s32[]{:S(2)}) async-start(), calls=%async_computation.13 | async-start | bytes 4423680 | tf_op jit(solution)/shard_map/reduce_scatter | solution.py:215
  363.0 147.5 %all-to-all-start.1 = ((bf16[8,2,27648]{2,1,0:T(2,128)(2,1)}), bf16[8,2,27648]{2,1,0:T(2,128)(2,1)S(1)}, u32[]{:S(2)}, u32[]{:S(2)}) async-start(bf16[8,2,27648]{2,1,0:T(2,128)(2,1)} %reshape.573), calls=%async_computation.2 | async-start | bytes 1769472 | tf_op jit(solution)/shard_map/all_to_all | solution.py:224
  367.6 281.0 %all-gather.7.cloned.1.call-start = ((), (), s32[]{:S(2)}) async-start(), calls=%async_computation.14 | async-start | bytes 4423680 | tf_op jit(solution)/shard_map/all_gather | solution.py:210
  496.6 12.6 copy-start.50
  510.5 5.7 copy-start.79
  516.2 7.7 copy-start.30
  518.3 5.5 copy-start.77
  518.3 5.5 copy-start.69
  603.3 106.9 %reduce-scatter.7.cloned.1.call-start = ((), (), s32[]{:S(2)}) async-start(), calls=%async_computation.15 | async-start | bytes 4423680 | tf_op jit(solution)/shard_map/reduce_scatter | solution.py:215
  648.6 8.4 copy-start.91
  662.8 55.6 %copy-start.51 = (f32[2,768,8]{1,2,0:T(8,128)S(1)}, f32[2,768,8]{1,2,0:T(8,128)}, u32[]{:S(2)}) copy-start(f32[2,768,8]{1,2,0:T(8,128)} %param.20) | copy-start | bytes 147460
  713.8 27.7 %all-to-all-start.3 = ((bf16[8,2,27648]{2,1,0:T(2,128)(2,1)}), bf16[8,2,27648]{2,1,0:T(2,128)(2,1)S(1)}, u32[]{:S(2)}, u32[]{:S(2)}) async-start(bf16[8,2,27648]{2,1,0:T(2,128)(2,1)} %reshape.575), calls=%async_computation.5 | async-start | bytes 1769472 | tf_op jit(solution)/shard_map/all_to_all | solution.py:224
  718.4 157.3 %all-gather.9.cloned.1.call-start = ((), (), s32[]{:S(2)}) async-start(), calls=%async_computation.16 | async-start | bytes 4423680 | tf_op jit(solution)/shard_map/all_gather | solution.py:275
  719.2 27.2 %copy-start.6 = (s32[512,1]{0,1:T(1,128)S(1)}, s32[512,1]{0,1:T(1,128)}, u32[]{:S(2)}) copy-start(s32[512,1]{0,1:T(1,128)} %get-tuple-element.87) | copy-start | bytes 6148
  746.4 8.8 copy-start.63
  830.4 138.5 %reduce-scatter.9.cloned.1.call-start = ((), (), s32[]{:S(2)}) async-start(), calls=%async_computation.17 | async-start | bytes 8847360 | tf_op jit(solution)/shard_map/reduce_scatter | solution.py:290
  875.7 11.3 copy-start.92
  975.1 27.7 %all-to-all-start.5 = ((bf16[8,2,27648]{2,1,0:T(2,128)(2,1)}), bf16[8,2,27648]{2,1,0:T(2,128)(2,1)S(1)}, u32[]{:S(2)}, u32[]{:S(2)}) async-start(bf16[8,2,27648]{2,1,0:T(2,128)(2,1)} %reshape.577), calls=%async_computation.8 | async-start | bytes 1769472 | tf_op jit(solution)/shard_map/all_to_all | solution.py:296
  979.7 228.2 %all-gather.11.cloned.1.call-start = ((), (), s32[]{:S(2)}) async-start(), calls=%async_computation.18 | async-start | bytes 4423680 | tf_op jit(solution)/shard_map/all_gather | solution.py:275
  1024.5 10.8 slice-start.3
  1024.5 11.4 slice-start.4
  1024.5 12.8 slice-start.5
  1037.4 7.4 copy-start.15
  1051.8 5.2 copy-start.24
  1052.2 4.8 copy-start.17
  1052.2 4.8 copy-start.31
  1105.9 26.6 %copy-start.65 = (f32[512]{0:T(512)S(1)}, f32[512]{0:T(512)}, u32[]{:S(2)}) copy-start(f32[512]{0:T(512)} %copy-done.64) | copy-start | bytes 6148
  1106.0 26.6 %copy-start.49 = (f32[12,512]{1,0:T(8,128)S(1)}, f32[12,512]{1,0:T(8,128)}, u32[]{:S(2)}) copy-start(f32[12,512]{1,0:T(8,128)} %copy-done.48) | copy-start | bytes 73732
  1106.0 26.6 %copy-start.57 = (f32[12,512]{1,0:T(8,128)S(1)}, f32[12,512]{1,0:T(8,128)}, u32[]{:S(2)}) copy-start(f32[12,512]{1,0:T(8,128)} %copy-done.56) | copy-start | bytes 73732
  1132.3 172.5 %reduce-scatter.11.cloned.1.call-start = ((), (), s32[]{:S(2)}) async-start(), calls=%async_computation.19 | async-start | bytes 8847360 | tf_op jit(solution)/shard_map/reduce_scatter | solution.py:290
  1133.0 7.7 copy-start.89
  1207.9 11.1 copy-start.93
  1224.0 19.5 %copy-start.41 = (f32[512,8]{0,1:T(8,128)S(1)}, f32[512,8]{0,1:T(8,128)}, u32[]{:S(2)}) copy-start(f32[512,8]{0,1:T(8,128)} %copy-done.40) | copy-start | bytes 49156
  1224.0 19.5 %copy-start.59 = (s32[1,512,1]{1,2,0:T(1,128)S(1)}, s32[1,512,1]{1,2,0:T(1,128)}, u32[]{:S(2)}) copy-start(s32[1,512,1]{1,2,0:T(1,128)} %copy-done.58) | copy-start | bytes 6148
  1224.1 19.5 %copy-start.61 = (f32[512]{0:T(512)S(1)}, f32[512]{0:T(512)}, u32[]{:S(2)}) copy-start(f32[512]{0:T(512)} %copy-done.60) | copy-start | bytes 6148
  1285.8 9.6 copy-start.23
  1285.8 10.0 copy-start.88
  1285.8 10.4 copy-start.35
  1308.9 26.9 %all-to-all-start.7 = ((bf16[8,2,27648]{2,1,0:T(2,128)(2,1)}), bf16[8,2,27648]{2,1,0:T(2,128)(2,1)S(1)}, u32[]{:S(2)}, u32[]{:S(2)}) async-start(bf16[8,2,27648]{2,1,0:T(2,128)(2,1)} %reshape.579), calls=%async_computation.11 | async-start | bytes 1769472 | tf_op jit(solution)/shard_map/all_to_all | solution.py:296
  1312.7 449.4 %all-reduce.8.cloned.1.call-start = ((), (), s32[]{:S(2)}) async-start(), calls=%async_computation.20 | async-start | bytes 37748736 | tf_op jit(solution)/shard_map/psum | solution.py:355
  1312.8 6.3 copy-start.90
  1319.1 5.9 copy-start.38
  1319.1 5.9 copy-start.39
  1329.3 7.6 copy-start.5
  1350.8 11.6 slice-start
  1350.8 11.6 slice-start.1
  1350.9 12.5 slice-start.2
  1378.2 8.8 copy-start.36
  1378.2 8.8 copy-start.37
  1403.2 41.1 %copy-start.26 = (f32[1,768,768]{2,1,0:T(8,128)S(1)}, f32[1,768,768]{2,1,0:T(8,128)}, u32[]{:S(2)}) copy-start(f32[1,768,768]{2,1,0:T(8,128)} %convolution_bitcast_fusion.4) | copy-start | bytes 7077892
  1542.9 48.1 %copy-start.76 = (f32[512]{0:T(512)S(1)}, f32[512]{0:T(512)}, u32[]{:S(2)}) copy-start(f32[512]{0:T(512)} %copy-done.75) | copy-start | bytes 6148
  1542.9 48.1 %copy-start.21 = (f32[512,768]{1,0:T(8,128)S(1)}, f32[512,768]{1,0:T(8,128)}, u32[]{:S(2)}) copy-start(f32[512,768]{1,0:T(8,128)} %copy-done.20) | copy-start | bytes 4718596
  (53 other events, 132.7 us)
Sparse Core Ops, SparseCore 0:
  250.0 46.1 all-gather.4
  311.7 47.2 reduce-scatter.4
  603.4 45.1 all-gather.6
  662.9 47.2 reduce-scatter.6
  830.6 45.0 all-gather.8
  892.1 76.7 reduce-scatter.8
  1132.5 45.1 all-gather.10
  1224.2 75.7 reduce-scatter.10
  1459.8 302.3 all-reduce.7
where the time goes:
time: 1800 us; the launch traced here: 1790 us
  local copies, waits for them, and re-layouts  757 us (42%)
  waiting for transfers between devices  529 us (29%)
  matrix products  188 us (10%)
  blocking collectives  150 us (8%)
  other arithmetic  127 us (7%)
  starting transfers between devices  18.2 us (1%)
    psum x1, waiting for transfers between devices, body(): lax.psum((grad_gain_attn, grad_qkv, grad_out_weight, grad_rel_bias, grad_...  168 us
    unnamed x227, local copies, waits for them, and re-layouts  103 us
    another operation x4, local copies, waits for them, and re-layouts, diagonal_rows(): tiled = jnp.tile(window, (1, block_rows))  99.4 us
    convert_element_type x2, local copies, waits for them, and re-layouts, diagonal_sums(): jnp.sum(flat.reshape(head_count, block_rows, span_width), axis=1, dtype=j...  97 us
    reshape x2, local copies, waits for them, and re-layouts, diagonal_rows(): sheared.reshape(dist_table.shape[0], block_rows, span_width - 1)[:, :, :LEN]  95.8 us
    reduce_scatter x2, waiting for transfers between devices, body(): lax.psum_scatter(jnp.einsum('ref,efd->red', active, w_out_layer, preferre...  94.8 us
    scatter x4, local copies, waits for them, and re-layouts, body(): grad_buffer = jnp.zeros((capacity, expert_total, model_width), jnp.bfloat...  93.4 us
    all_gather x2, waiting for transfers between devices, body(): rows_all = lax.all_gather(arrived, 'mp', axis=0, tiled=True)  91.5 us
  transfers between devices with their start and end apart: 13, of which 10 were waited for; matrix products, arithmetic and copies ran while one was open for 23% of the time, Pallas kernels for 0%

commit v1 on v0

v1 whole, which is shorter than its diff:
```python
import functools

import jax
import jax.numpy as jnp
import numpy as np
from jax import lax
from jax.experimental import pallas as pl
from jax.experimental.pallas import tpu as pltpu
from jax.sharding import PartitionSpec as P

HEAD_DIM = 64
BUCKETS = 32
MAX_DIST = 128
LAYERS = 2
LEN = 512

SIDE = 128
SPAN = 256
WINDOW_ROWS = 8
GROUP_HEADS = 4
GROUP = GROUP_HEADS * HEAD_DIM
PAIR = 2 * HEAD_DIM
VMEM_BYTES = 56 * 1024 * 1024

epsilon = 1e-06
masked_score = -1000000000.0
highest = lax.Precision.HIGHEST
f32 = jnp.float32
bf16 = jnp.bfloat16

NT = (((1,), (1,)), ((), ()))
TN = (((0,), (0,)), ((), ()))


def bucket_limits():
    half_count = BUCKETS // 2
    exact_count = half_count // 2
    lengths = np.arange(exact_count, 4 * MAX_DIST + 2 * LEN + 2)
    levels = (
        np.log(lengths / exact_count) / np.log(MAX_DIST / exact_count) * (half_count - exact_count)
    ).astype(np.int64)
    levels = np.minimum(levels, half_count - exact_count - 1)
    limits = []
    for target in range(1, half_count - exact_count):
        limits.append(int(lengths[np.argmax(levels >= target)]))
    return limits


def bucket_of(distance):
    half_count = BUCKETS // 2
    exact_count = half_count // 2
    magnitude = np.abs(distance)
    counted = np.full(distance.shape, exact_count, np.int32)
    for limit_value in bucket_limits():
        counted = counted + (magnitude >= limit_value).astype(np.int32)
    return np.where(distance > 0, half_count, 0) + np.where(
        magnitude < exact_count, magnitude, counted
    )


def window_buckets():
    place = np.arange(SPAN)
    shift = np.where(place < SIDE, -place, SPAN - place)
    rows = [bucket_of(offset * SIDE + shift) for offset in (-1, 0, 1)]
    for row in rows:
        row[SIDE] = -1
    far = bucket_of(np.array([-2 * SIDE + SIDE - 1, 2 * SIDE - SIDE + 1]))
    rows += [np.full(SPAN, far[0]), np.full(SPAN, far[1])]
    rows += [np.full(SPAN, -1)] * (WINDOW_ROWS - len(rows))
    return np.stack(rows).astype(np.int32)


def window_onehot():
    return (
        jnp.asarray(window_buckets().reshape(-1))[:, None]
        == jnp.arange(BUCKETS, dtype=jnp.int32)[None, :]
    ).astype(f32)


def params(**extra):
    return pltpu.CompilerParams(vmem_limit_bytes=VMEM_BYTES, **extra)


def dot(a, b, dims=None, precision=None):
    if dims is None:
        return jnp.dot(a, b, preferred_element_type=f32, precision=precision)
    return lax.dot_general(a, b, dims, preferred_element_type=f32, precision=precision)


def rms_factor(values):
    return lax.rsqrt(jnp.mean(values * values, axis=-1, keepdims=True) + epsilon)


def half_mask(half):
    lane = lax.broadcasted_iota(jnp.int32, (1, PAIR), 1)
    inside = (lane >= half * HEAD_DIM) & (lane < (half + 1) * HEAD_DIM)
    return inside.astype(f32)


def bias_blocks(windows):
    blocks = {}
    for row, offset in enumerate((-1, 0, 1)):
        spread = jnp.broadcast_to(windows[row : row + 1, :], (SIDE, SPAN))
        blocks[offset] = pltpu.roll(spread, 0, 1, stride=1, stride_axis=0)[:, :SIDE]
    blocks[-2] = jnp.broadcast_to(windows[3:4, :SIDE], (SIDE, SIDE))
    blocks[2] = jnp.broadcast_to(windows[4:5, :SIDE], (SIDE, SIDE))
    return blocks


def offset_of(key_block, query_block):
    return max(-2, min(2, key_block - query_block))


def bias_part(blocks, first_query, width):
    columns = []
    for query_block in range(first_query // SIDE, (first_query + width) // SIDE):
        columns.append(
            jnp.concatenate(
                [blocks[offset_of(key_block, query_block)] for key_block in range(LEN // SIDE)],
                axis=0,
            )
        )
    return jnp.concatenate(columns, axis=1)


def diagonal_sums(block):
    padded = jnp.concatenate([block, jnp.zeros((SIDE, SPAN - SIDE), f32)], axis=1)
    total = padded[:8]
    for first in range(8, SIDE, 8):
        total = total + pltpu.roll(padded[first : first + 8], SPAN - first, 1)
    row = lax.broadcasted_iota(jnp.int32, (8, SPAN), 0)
    for bit in (1, 2, 4):
        total = jnp.where((row & bit) != 0, pltpu.roll(total, SPAN - bit, 1), total)
    return jnp.sum(total, axis=0, keepdims=True)


def mask_of(seg_col, seg_row):
    return jnp.where(seg_col == seg_row, 0.0, masked_score).astype(f32)


def place_matrix(rowid_row, count):
    rows = lax.broadcasted_iota(jnp.int32, (count, rowid_row.shape[1]), 0)
    return (rows == rowid_row).astype(bf16)


def take_matrix(rowid_col, count):
    lanes = lax.broadcasted_iota(jnp.int32, (rowid_col.shape[0], count), 1)
    return (lanes == rowid_col).astype(bf16)


def route_onehot(route_col, experts):
    lanes = lax.broadcasted_iota(jnp.int32, (route_col.shape[0], experts), 1)
    return (lanes == route_col).astype(f32)


QUERY_SPAN = 256


def attend_kernel(combine, refs):
    refs = list(refs)
    take = lambda count: [refs.pop(0) for _ in range(count)]
    if combine:
        middle_prev, prob_prev, back_prev, rowcol_prev, route_prev = take(5)
    else:
        (tokens,) = take(1)
    gain_attn, wq, wk, wv, wout, windows, seg_row, seg_col = take(8)
    gain_ffn, router, rowid_row = take(3)
    if combine:
        (x_out,) = take(1)
    proj, mixed, lse, middle, prob, buffer = take(6)
    normed_s, x_s, acc_s, mask_s = take(4)
    step = pl.program_id(0)

    @pl.when(step == 0)
    def _():
        if combine:
            chosen = route_onehot(route_prev[...], prob_prev.shape[1])
            gate = jnp.sum(prob_prev[...] * chosen, axis=-1, keepdims=True)
            returned = dot(take_matrix(rowcol_prev[...], back_prev.shape[0]), back_prev[...])
            x = middle_prev[...] + gate * returned
            x_out[...] = x
        else:
            x = tokens[...].astype(f32)
        x_s[...] = x
        normed_s[...] = (x * rms_factor(x) * gain_attn[...]).astype(bf16)
        acc_s[...] = jnp.zeros_like(acc_s)
        mask_s[...] = mask_of(seg_col[...], seg_row[...])

    normed = normed_s[...]
    q = dot(normed, wq[...]).astype(bf16)
    k = dot(normed, wk[...]).astype(bf16)
    v = dot(normed, wv[...]).astype(bf16)
    proj[0] = q
    proj[1] = k
    proj[2] = v
    for pair in range(GROUP_HEADS // 2):
        lanes = slice(pair * PAIR, (pair + 1) * PAIR)
        q2 = q[:, lanes].astype(f32) * HEAD_DIM ** (-0.5)
        k2 = k[:, lanes]
        v2t = v[:, lanes].T
        outs = []
        for half in range(2):
            head = pair * 2 + half
            qm = (q2 * half_mask(half)).astype(bf16)
            vt = v2t[half * HEAD_DIM : (half + 1) * HEAD_DIM, :]
            blocks = bias_blocks(windows[head])
            parts = []
            for first in range(0, LEN, QUERY_SPAN):
                span = slice(first, first + QUERY_SPAN)
                scores = dot(k2, qm[span], NT)
                scores = scores + bias_part(blocks, first, QUERY_SPAN) + mask_s[:, span]
                top = jnp.max(scores, axis=0, keepdims=True)
                powers = jnp.exp(scores - top)
                total = jnp.sum(powers, axis=0, keepdims=True)
                parts.append(dot(vt, powers.astype(bf16)) * (1.0 / total))
                lse[0, head : head + 1, span] = top + jnp.log(total)
            outs.append(jnp.concatenate(parts, axis=1))
        mixed[:, lanes] = jnp.concatenate(outs, axis=0).T.astype(bf16)
    acc_s[...] += dot(mixed[...], wout[...])

    @pl.when(step == pl.num_programs(0) - 1)
    def _():
        mid = x_s[...] + acc_s[...]
        middle[...] = mid
        nf = (mid * rms_factor(mid) * gain_ffn[...]).astype(bf16)
        logits = dot(nf.astype(f32), router[...], precision=highest)
        powers = jnp.exp(logits - jnp.max(logits, axis=-1, keepdims=True))
        prob[...] = powers / jnp.sum(powers, axis=-1, keepdims=True)
        buffer[...] = dot(place_matrix(rowid_row[...], buffer.shape[0]), nf).astype(bf16)


def whole(array):
    zeros = (0,) * array.ndim
    return pl.BlockSpec(array.shape, lambda g: zeros)


def whole_shape(shape):
    zeros = (0,) * len(shape)
    return pl.BlockSpec(shape, lambda g: zeros)


def qkv_specs(width):
    per = width // GROUP
    return [
        pl.BlockSpec((width, GROUP), functools.partial(lambda part, g: (0, part * per + g), part))
        for part in range(3)
    ]


def attend(source, gain_attn, qkv_w, out_w, windows, seg_row, seg_col, gain_ffn, router, rowid_row):
    combine = len(source) > 1
    width = qkv_w.shape[0]
    groups = width // GROUP
    experts = router.shape[1]
    count = rowid_row.rows
    ins = list(source) + [gain_attn, qkv_w, qkv_w, qkv_w, out_w, windows, seg_row, seg_col]
    ins += [gain_ffn, router, rowid_row.array]
    specs = [whole(a) for a in source] + [whole(gain_attn)] + qkv_specs(width)
    specs += [pl.BlockSpec((GROUP, width), lambda g: (g, 0))]
    specs += [pl.BlockSpec((GROUP_HEADS, WINDOW_ROWS, SPAN), lambda g: (g, 0, 0))]
    specs += [whole(seg_row), whole(seg_col), whole(gain_ffn), whole(router), whole(rowid_row.array)]
    shapes = [
        ((3, LEN, width), bf16, pl.BlockSpec((3, LEN, GROUP), lambda g: (0, 0, g))),
        ((LEN, width), bf16, pl.BlockSpec((LEN, GROUP), lambda g: (0, g))),
        ((groups, 8, LEN), f32, pl.BlockSpec((1, 8, LEN), lambda g: (g, 0, 0))),
        ((LEN, width), f32, whole_shape((LEN, width))),
        ((LEN, experts), f32, whole_shape((LEN, experts))),
        ((count, width), bf16, whole_shape((count, width))),
    ]
    if combine:
        shapes = [((LEN, width), f32, whole_shape((LEN, width)))] + shapes
    return pl.pallas_call(
        lambda *refs: attend_kernel(combine, refs),
        grid=(groups,),
        in_specs=specs,
        out_specs=[s[2] for s in shapes],
        out_shape=[jax.ShapeDtypeStruct(s[0], s[1]) for s in shapes],
        scratch_shapes=[
            pltpu.VMEM((LEN, width), bf16),
            pltpu.VMEM((LEN, width), f32),
            pltpu.VMEM((LEN, width), f32),
            pltpu.VMEM((LEN, LEN), f32),
        ],
        compiler_params=params(),
        cost_estimate=pl.CostEstimate(
            flops=8 * LEN * width * width + 4 * LEN * LEN * width,
            bytes_accessed=16 * LEN * width + 8 * width * width,
            transcendentals=LEN * LEN * width // HEAD_DIM,
        ),
        name="attend",
    )(*ins)


def attend_back_kernel(first_layer, refs):
    refs = list(refs)
    take = lambda count: [refs.pop(0) for _ in range(count)]
    gradient, gback, rowcol, gate_grad, prob, route_col, middle, gain_ffn, router = take(9)
    x_ref, gain_attn, wq, wk, wv, wout, proj, mixed, lse, windows, seg_row, seg_col = take(12)
    if not first_layer:
        back_prev, rowrow_prev, rowcol_prev, prob_prev, route_prev = take(5)
    grad_in, gq, gk, gv, gout, gwin, gain_attn_g, gain_ffn_g, grouter = take(9)
    if not first_layer:
        buffer_prev, gate_grad_prev = take(2)
    normt_s, mg_s, att_s, acc_s, mask_s = take(5)
    step = pl.program_id(0)

    @pl.when(step == 0)
    def _():
        g = gradient[...].astype(f32)
        expert_part = dot(take_matrix(rowcol[...], gback.shape[0]), gback[...])
        probability = prob[...]
        chosen = route_onehot(route_col[...], prob.shape[1])
        gate = jnp.sum(probability * chosen, axis=-1, keepdims=True)
        logit_grad = gate_grad[...] * gate * (chosen - probability)
        mid = middle[...]
        r = rms_factor(mid)
        scaled = mid * r
        nf = (scaled * gain_ffn[...]).astype(bf16).astype(f32)
        grouter[...] = dot(logit_grad, nf, TN, precision=highest)
        ffn_in = expert_part + dot(logit_grad, router[...], NT, precision=highest)
        u = ffn_in * gain_ffn[...]
        mg = g + r * (u - scaled * (r * jnp.mean(u * mid, axis=-1, keepdims=True)))
        gain_ffn_g[...] = jnp.sum(ffn_in * scaled, axis=0, keepdims=True)
        mg_s[...] = mg
        att_s[...] = mg.astype(bf16)
        x = x_ref[...].astype(f32)
        normed = (x * rms_factor(x) * gain_attn[...]).astype(bf16)
        normt_s[...] = normed.T
        acc_s[...] = jnp.zeros_like(acc_s)
        mask_s[...] = mask_of(seg_col[...], seg_row[...])

    att = att_s[...]
    gout[...] = dot(mixed[...], att, TN).astype(gout.dtype)
    mixed_grad = dot(att, wout[...], NT).astype(bf16)
    dqs, dks, dvs = [], [], []
    for pair in range(GROUP_HEADS // 2):
        lanes = slice(pair * PAIR, (pair + 1) * PAIR)
        q2 = proj[0, :, lanes].astype(f32) * HEAD_DIM ** (-0.5)
        k2 = proj[1, :, lanes]
        v2 = proj[2, :, lanes]
        k2t = k2.T
        o2 = mixed_grad[:, lanes].astype(f32)
        dk = jnp.zeros((LEN, PAIR), f32)
        dv = jnp.zeros((LEN, PAIR), f32)
        dqts = []
        for half in range(2):
            head = pair * 2 + half
            qm = (q2 * half_mask(half)).astype(bf16)
            om = (o2 * half_mask(half)).astype(bf16)
            kt = k2t[half * HEAD_DIM : (half + 1) * HEAD_DIM, :]
            blocks = bias_blocks(windows[head])
            sums = {}
            parts = []
            for first in range(0, LEN, QUERY_SPAN):
                span = slice(first, first + QUERY_SPAN)
                scores = dot(k2, qm[span], NT)
                scores = scores + bias_part(blocks, first, QUERY_SPAN) + mask_s[:, span]
                powers = jnp.exp(scores - lse[0, head : head + 1, span])
                prob_grad = dot(v2, om[span], NT)
                weighted = powers * prob_grad
                delta = jnp.sum(weighted, axis=0, keepdims=True)
                score_grad = weighted - powers * delta
                for kb in range(LEN // SIDE):
                    for qb in range(QUERY_SPAN // SIDE):
                        piece = score_grad[kb * SIDE : (kb + 1) * SIDE, qb * SIDE : (qb + 1) * SIDE]
                        offset = offset_of(kb, qb + first // SIDE)
                        sums[offset] = sums[offset] + piece if offset in sums else piece
                sg = score_grad.astype(bf16)
                dv = dv + dot(powers.astype(bf16), om[span])
                dk = dk + dot(sg, qm[span])
                parts.append(dot(kt, sg))
            dqts.append(jnp.concatenate(parts, axis=1))
            for row, offset in enumerate((-1, 0, 1)):
                gwin[head, row : row + 1, :] = diagonal_sums(sums[offset])
            for row, offset in ((3, -2), (4, 2)):
                gwin[head, row : row + 1, :SIDE] = jnp.sum(sums[offset], axis=0, keepdims=True)
                gwin[head, row : row + 1, SIDE:] = jnp.zeros((1, SPAN - SIDE), f32)
            gwin[head, 5:WINDOW_ROWS, :] = jnp.zeros((WINDOW_ROWS - 5, SPAN), f32)
        dqs.append((jnp.concatenate(dqts, axis=0) * HEAD_DIM ** (-0.5)).T)
        dks.append(dk)
        dvs.append(dv)
    total = acc_s[...]
    for ref, weight, pieces in ((gq, wq, dqs), (gk, wk, dks), (gv, wv, dvs)):
        part = jnp.concatenate(pieces, axis=1).astype(bf16)
        ref[...] = dot(normt_s[...], part).astype(ref.dtype)
        total = total + dot(part, weight[...], NT)
    acc_s[...] = total

    @pl.when(step == pl.num_programs(0) - 1)
    def _():
        x = x_ref[...].astype(f32)
        r = rms_factor(x)
        scaled = x * r
        attn_in = acc_s[...]
        u = attn_in * gain_attn[...]
        g = mg_s[...] + r * (u - scaled * (r * jnp.mean(u * x, axis=-1, keepdims=True)))
        gain_attn_g[...] = jnp.sum(attn_in * scaled, axis=0, keepdims=True)
        grad_in[...] = g
        if not first_layer:
            send_back(
                g, back_prev, rowrow_prev, rowcol_prev, prob_prev, route_prev, buffer_prev, gate_grad_prev
            )


def send_back(g, back, rowrow, rowcol, prob, route_col, buffer, gate_grad):
    returned = dot(take_matrix(rowcol[...], back.shape[0]), back[...])
    gate = jnp.sum(
        prob[...] * route_onehot(route_col[...], prob.shape[1]), axis=-1, keepdims=True
    )
    gate_grad[...] = jnp.sum(g * returned, axis=-1, keepdims=True)
    expert_grad = (gate * g).astype(bf16)
    buffer[...] = dot(place_matrix(rowrow[...], buffer.shape[0]), expert_grad).astype(bf16)
    return gate * returned


def attend_back(state, gradient, gback, gate_grad, previous, common):
    first_layer = previous is None
    width = common["out_w"].shape[0]
    groups = width // GROUP
    experts = common["router"].shape[1]
    ins, specs = [], []

    def add(array, spec=None):
        ins.append(array)
        specs.append(whole(array) if spec is None else spec)

    for array in (gradient, gback, state["rowcol"], gate_grad, state["prob"], state["route_col"]):
        add(array)
    for array in (state["middle"], common["gain_ffn"], common["router"], state["x"]):
        add(array)
    add(common["gain_attn"])
    for spec in qkv_specs(width):
        add(common["qkv_w"], spec)
    add(common["out_w"], pl.BlockSpec((GROUP, width), lambda g: (g, 0)))
    add(state["proj"], pl.BlockSpec((3, LEN, GROUP), lambda g: (0, 0, g)))
    add(state["mixed"], pl.BlockSpec((LEN, GROUP), lambda g: (0, g)))
    add(state["lse"], pl.BlockSpec((1, 8, LEN), lambda g: (g, 0, 0)))
    add(common["windows"], pl.BlockSpec((GROUP_HEADS, WINDOW_ROWS, SPAN), lambda g: (g, 0, 0)))
    add(common["seg_row"])
    add(common["seg_col"])
    if not first_layer:
        for name in ("back", "rowrow", "rowcol", "prob", "route_col"):
            add(previous[name])
    column = pl.BlockSpec((width, GROUP), lambda g: (0, g))
    shapes = [
        ((LEN, width), f32, whole_shape((LEN, width))),
        ((width, width), bf16, column),
        ((width, width), bf16, column),
        ((width, width), bf16, column),
        ((width, width), bf16, pl.BlockSpec((GROUP, width), lambda g: (g, 0))),
        (
            common["windows"].shape,
            f32,
            pl.BlockSpec((GROUP_HEADS, WINDOW_ROWS, SPAN), lambda g: (g, 0, 0)),
        ),
        ((1, width), f32, whole_shape((1, width))),
        ((1, width), f32, whole_shape((1, width))),
        ((experts, width), f32, whole_shape((experts, width))),
    ]
    if not first_layer:
        count = previous["back"].shape[0]
        shapes += [
            ((count, width), bf16, whole_shape((count, width))),
            ((LEN, 1), f32, whole_shape((LEN, 1))),
        ]
    return pl.pallas_call(
        lambda *refs: attend_back_kernel(first_layer, refs),
        grid=(groups,),
        in_specs=specs,
        out_specs=[s[2] for s in shapes],
        out_shape=[jax.ShapeDtypeStruct(s[0], s[1]) for s in shapes],
        scratch_shapes=[
            pltpu.VMEM((width, LEN), bf16),
            pltpu.VMEM((LEN, width), f32),
            pltpu.VMEM((LEN, width), bf16),
            pltpu.VMEM((LEN, width), f32),
            pltpu.VMEM((LEN, LEN), f32),
        ],
        compiler_params=params(),
        cost_estimate=pl.CostEstimate(
            flops=16 * LEN * width * width + 10 * LEN * LEN * width,
            bytes_accessed=30 * LEN * width + 16 * width * width,
            transcendentals=LEN * LEN * width // HEAD_DIM,
        ),
        name="attend_back",
    )(*ins)


def turn_kernel(middle, cotangent, back, rowrow, rowcol, prob, route_col, output, buffer, gate_grad):
    g = cotangent[...].astype(f32)
    added = send_back(g, back, rowrow, rowcol, prob, route_col, buffer, gate_grad)
    output[...] = middle[...] + added


def turn(state, cotangent):
    width = cotangent.shape[1]
    count = state["back"].shape[0]
    return pl.pallas_call(
        turn_kernel,
        out_shape=[
            jax.ShapeDtypeStruct((LEN, width), f32),
            jax.ShapeDtypeStruct((count, width), bf16),
            jax.ShapeDtypeStruct((LEN, 1), f32),
        ],
        compiler_params=params(),
        cost_estimate=pl.CostEstimate(
            flops=4 * LEN * count * width, bytes_accessed=14 * LEN * width, transcendentals=0
        ),
        name="turn",
    )(
        state["middle"],
        cotangent,
        state["back"],
        state["rowrow"],
        state["rowcol"],
        state["prob"],
        state["route_col"],
    )


GELU_A = float(np.sqrt(2.0 / np.pi))
GELU_B = 0.044715


def gelu_tanh(hidden):
    return jnp.tanh(GELU_A * (hidden + GELU_B * (hidden * hidden * hidden)))


def gelu_of(hidden, curve):
    return 0.5 * hidden * (1.0 + curve)


def gelu_slope(hidden, curve):
    inner = GELU_A * (1.0 + (3.0 * GELU_B) * (hidden * hidden))
    return 0.5 * (1.0 + curve) + 0.5 * hidden * (1.0 - curve * curve) * inner


def expert_kernel(rows, w_in, w_out, out, acc):
    step = pl.program_id(0)

    @pl.when(step == 0)
    def _():
        acc[...] = jnp.zeros_like(acc)

    hidden = dot(rows[...], w_in[0])
    active = gelu_of(hidden, gelu_tanh(hidden)).astype(bf16)
    acc[...] += dot(active, w_out[0])

    @pl.when(step == pl.num_programs(0) - 1)
    def _():
        out[...] = acc[...].astype(bf16)


def expert(rows, w_in_all, w_out_all):
    parts, width, part = w_in_all.shape
    count = rows.shape[0]
    return pl.pallas_call(
        expert_kernel,
        grid=(parts,),
        in_specs=[
            whole(rows),
            pl.BlockSpec((1, width, part), lambda b: (b, 0, 0)),
            pl.BlockSpec((1, part, width), lambda b: (b, 0, 0)),
        ],
        out_specs=whole(rows),
        out_shape=jax.ShapeDtypeStruct(rows.shape, bf16),
        scratch_shapes=[pltpu.VMEM(rows.shape, f32)],
        compiler_params=params(),
        cost_estimate=pl.CostEstimate(
            flops=4 * count * width * parts * part,
            bytes_accessed=4 * count * width + 4 * width * parts * part,
            transcendentals=count * parts * part,
        ),
        name="expert",
    )(rows, w_in_all, w_out_all)


def expert_back_kernel(rows, grads, w_in, w_out, out, acc):
    step = pl.program_id(0)

    @pl.when(step == 0)
    def _():
        acc[...] = jnp.zeros_like(acc)

    hidden = dot(rows[...], w_in[0])
    act_grad = dot(grads[...], w_out[0], NT)
    pre_grad = (act_grad * gelu_slope(hidden, gelu_tanh(hidden))).astype(bf16)
    acc[...] += dot(pre_grad, w_in[0], NT)

    @pl.when(step == pl.num_programs(0) - 1)
    def _():
        out[...] = acc[...].astype(bf16)


def expert_back(rows, grads, w_in_all, w_out_all):
    parts, width, part = w_in_all.shape
    count = rows.shape[0]
    return pl.pallas_call(
        expert_back_kernel,
        grid=(parts,),
        in_specs=[
            whole(rows),
            whole(grads),
            pl.BlockSpec((1, width, part), lambda b: (b, 0, 0)),
            pl.BlockSpec((1, part, width), lambda b: (b, 0, 0)),
        ],
        out_specs=whole(rows),
        out_shape=jax.ShapeDtypeStruct(rows.shape, bf16),
        scratch_shapes=[pltpu.VMEM(rows.shape, f32)],
        compiler_params=params(),
        cost_estimate=pl.CostEstimate(
            flops=6 * count * width * parts * part,
            bytes_accessed=6 * count * width + 4 * width * parts * part,
            transcendentals=count * parts * part,
        ),
        name="expert_back",
    )(rows, grads, w_in_all, w_out_all)


def weight_grad_kernel(rows, grads, w_in, w_out, g_in, g_out):
    step = pl.program_id(0)

    @pl.when(step == 0)
    def _():
        g_in[...] = jnp.zeros_like(g_in)
        g_out[...] = jnp.zeros_like(g_out)

    hidden = dot(rows[...], w_in[...])
    curve = gelu_tanh(hidden)
    active = gelu_of(hidden, curve).astype(bf16)
    act_grad = dot(grads[...], w_out[...], NT)
    pre_grad = (act_grad * gelu_slope(hidden, curve)).astype(bf16)
    g_out[...] += dot(active, grads[...], TN)
    g_in[...] += dot(rows[...], pre_grad, TN)


def weight_grad(rows_all, grads_all, w_in, w_out, parts):
    width, part = w_in.shape
    count = rows_all.shape[0] // parts
    block = pl.BlockSpec((count, width), lambda b: (b, 0))
    return pl.pallas_call(
        weight_grad_kernel,
        grid=(parts,),
        in_specs=[block, block, whole(w_in), whole(w_out)],
        out_specs=[whole(w_in), whole(w_out)],
        out_shape=[
            jax.ShapeDtypeStruct(w_in.shape, f32),
            jax.ShapeDtypeStruct(w_out.shape, f32),
        ],
        compiler_params=params(),
        cost_estimate=pl.CostEstimate(
            flops=8 * rows_all.shape[0] * width * part,
            bytes_accessed=4 * rows_all.shape[0] * width + 12 * width * part,
            transcendentals=rows_all.shape[0] * part,
        ),
        name="weight_grad",
    )(rows_all, grads_all, w_in, w_out)


class Places:
    def __init__(self, array, rows):
        self.array = array
        self.rows = rows


def swap(rows, experts):
    count, width = rows.shape
    split = rows.reshape(experts, count // experts, width)
    return lax.all_to_all(split, "dp", split_axis=0, concat_axis=0, tiled=True).reshape(count, width)


def gather_parts(array):
    return lax.all_gather(array, "mp", axis=0, tiled=True)


def body(
    tokens,
    segments,
    routes,
    gain_attn,
    qkv_weight,
    out_weight,
    rel_bias,
    gain_ffn,
    router_weight,
    w_in,
    w_out,
    cotangent,
):
    tok_count, width = tokens.shape
    experts = w_in.shape[1] * lax.axis_size("dp")
    parts = lax.axis_size("mp")
    capacity = (tok_count * 9 + 8 * experts - 1) // (8 * experts)
    count = experts * capacity
    heads = width // HEAD_DIM

    onehot = window_onehot()
    windows = [
        jnp.dot(onehot, rel_bias[layer], precision=highest).T.reshape(heads, WINDOW_ROWS, SPAN)
        for layer in range(LAYERS)
    ]
    chosen = routes[:, :, 0]
    chosen_onehot = (
        chosen[:, :, None] == jnp.arange(experts, dtype=jnp.int32)[None, None, :]
    ).astype(jnp.int32)
    slots = jnp.sum(jnp.cumsum(chosen_onehot, axis=1) * chosen_onehot, axis=-1) - 1
    rowid = chosen * capacity + slots
    seg_row = segments.reshape(1, LEN)
    seg_col = segments.reshape(LEN, 1)

    w_all = [(gather_parts(w_in[layer]), gather_parts(w_out[layer])) for layer in range(LAYERS)]
    states = []
    source = (tokens,)
    for layer in range(LAYERS):
        common = dict(
            gain_attn=gain_attn[layer : layer + 1],
            gain_ffn=gain_ffn[layer : layer + 1],
            qkv_w=qkv_weight[layer],
            out_w=out_weight[layer],
            router=router_weight[layer],
            windows=windows[layer],
            seg_row=seg_row,
            seg_col=seg_col,
        )
        state = dict(
            common=common,
            rowrow=rowid[layer].reshape(1, tok_count),
            rowcol=rowid[layer].reshape(tok_count, 1),
            route_col=routes[layer],
        )
        results = attend(
            source,
            common["gain_attn"],
            common["qkv_w"],
            common["out_w"],
            common["windows"],
            seg_row,
            seg_col,
            common["gain_ffn"],
            common["router"],
            Places(state["rowrow"], count),
        )
        if layer > 0:
            state["x"] = results[0]
            results = results[1:]
        else:
            state["x"] = tokens
        for name, value in zip(("proj", "mixed", "lse", "middle", "prob"), results):
            state[name] = value
        rows = swap(results[5], experts)
        state["rows"] = rows
        state["back"] = swap(expert(rows, *w_all[layer]), experts)
        states.append(state)
        source = tuple(state[name] for name in ("middle", "prob", "back", "rowcol", "route_col"))

    rows_all = [gather_parts(state["rows"]) for state in states]
    output, buffer, gate_grad = turn(states[-1], cotangent)
    gradient = cotangent
    per_layer = [None] * LAYERS
    for layer in reversed(range(LAYERS)):
        state = states[layer]
        grads = swap(buffer, experts)
        sent = expert_back(state["rows"], grads, *w_all[layer])
        gback = swap(sent, experts)
        grads_all = gather_parts(grads)
        g_in, g_out = weight_grad(rows_all[layer], grads_all, w_in[layer, 0], w_out[layer, 0], parts)
        previous = states[layer - 1] if layer > 0 else None
        results = attend_back(state, gradient, gback, gate_grad, previous, state["common"])
        gradient, gq, gk, gv, gout, gwin, gain_a, gain_f, grouter = results[:9]
        if layer > 0:
            buffer, gate_grad = results[9:]
        big = lax.psum((gq, gk, gv, gout), ("dp", "mp"))
        small = (
            gain_a,
            gain_f,
            grouter,
            jnp.dot(
                onehot.T, gwin.reshape(heads, WINDOW_ROWS * SPAN).T, precision=highest
            ),
        )
        per_layer[layer] = (big, small, g_in, g_out)
    small = lax.psum([entry[1] for entry in per_layer], ("dp", "mp"))
    grad_qkv = jnp.stack(
        [jnp.concatenate(entry[0][:3], axis=1).astype(f32) for entry in per_layer]
    )
    grad_out = jnp.stack([entry[0][3].astype(f32) for entry in per_layer])
    grad_gain_attn = jnp.concatenate([entry[0] for entry in small], axis=0)
    grad_gain_ffn = jnp.concatenate([entry[1] for entry in small], axis=0)
    grad_router = jnp.stack([entry[2].T for entry in small])
    grad_rel = jnp.stack([entry[3] for entry in small])
    grad_w_in = jnp.stack([entry[2] for entry in per_layer])[:, None]
    grad_w_out = jnp.stack([entry[3] for entry in per_layer])[:, None]
    return (
        output,
        gradient,
        grad_gain_attn,
        grad_qkv,
        grad_out,
        grad_rel,
        grad_gain_ffn,
        grad_router,
        grad_w_in,
        grad_w_out,
    )


def solution(mesh):
    return jax.shard_map(
        body,
        mesh=mesh,
        in_specs=(
            P(("dp", "mp"), None),
            P(("dp", "mp"), None),
            P(None, ("dp", "mp"), None),
            P(),
            P(),
            P(),
            P(),
            P(),
            P(),
            P(None, "dp", None, "mp"),
            P(None, "dp", "mp", None),
            P(("dp", "mp"), None),
        ),
        out_specs=(
            P(("dp", "mp"), None),
            P(("dp", "mp"), None),
            P(),
            P(),
            P(),
            P(),
            P(),
            P(),
            P(None, "dp", None, "mp"),
            P(None, "dp", "mp", None),
        ),
        check_vma=False,
    )
```

time: 1800 us -> 710 us (0.39)
  local copies, waits for them, and re-layouts: 757 us -> 28.2 us
  waiting for transfers between devices: 529 us -> 229 us
  Pallas kernels: 0 us -> 188 us
  matrix products: 188 us -> 2.6 us
  other arithmetic: 127 us -> 21 us
  blocking collectives: 150 us -> 208 us
    pallas_call x0 -> x11, Pallas kernels: none -> 188 us  [the longest x2 60 us: attend_back(): pl.pallas_call(lambda *refs: attend_back_kernel(first_layer, refs), grid=...]
    dot_general x46 -> x4, matrix products: 188 us -> 2.6 us  [the longest x2 1.44 us: body(): jnp.dot(onehot, rel_bias[layer], precision=highest)]
    reshape x8 -> x3, local copies, waits for them, and re-layouts: 178 us -> 2.16 us  [the longest x2 1.3 us: body(): jnp.dot(onehot, rel_bias[layer], precision=highest)]
    reduce_scatter x4 -> x0, waiting for transfers between devices: 172 us -> none  [the longest x2 94.8 us: body(): lax.psum_scatter(jnp.einsum('ref,efd->red', active, w_out_layer, preferre...]
    scatter x8 -> x0, local copies, waits for them, and re-layouts: 151 us -> none  [the longest x4 93.4 us: body(): grad_buffer = jnp.zeros((capacity, expert_total, model_width), jnp.bfloat...]
    convert_element_type x6 -> x0, local copies, waits for them, and re-layouts: 107 us -> none  [the longest x2 97 us: diagonal_sums(): jnp.sum(flat.reshape(head_count, block_rows, span_width), axis=1, dtype=j...]
    another operation x11 -> x4, local copies, waits for them, and re-layouts: 99.9 us -> 2.33 us  [the longest x3 2.32 us: body(): rowid[layer].reshape(tok_count, 1)]
    unnamed x227 -> x64, local copies, waits for them, and re-layouts: 103 us -> 6.37 us
  transfers between devices with their start and end apart: 13 -> 11, of which waited for: 10 -> 5; matrix products, arithmetic and copies ran while one was open for 23% -> 5% of each run, Pallas kernels for 0% -> 27%
where the time goes in v1:
time: 710 us; the launch traced here: 701 us
  waiting for transfers between devices  229 us (32%)
  blocking collectives  208 us (29%)
  Pallas kernels  188 us (26%)
  local copies, waits for them, and re-layouts  28.2 us (4%)
  other arithmetic  21 us (3%)
  between operations  14.4 us (2%)
  starting transfers between devices  10.6 us (1%)
    all_to_all x6, blocking collectives, swap(): lax.all_to_all(split, 'dp', split_axis=0, concat_axis=0, tiled=True)  166 us
    psum x1, waiting for transfers between devices, body(): big = lax.psum((gq, gk, gv, gout), ('dp', 'mp'))  102 us
    all_gather x8, waiting for transfers between devices, gather_parts(): return lax.all_gather(array, 'mp', axis=0, tiled=True)  84.1 us
    pallas_call x2, Pallas kernels, attend_back(): pl.pallas_call(lambda *refs: attend_back_kernel(first_layer, refs), grid=...  60 us
    psum x1, blocking collectives, body(): small = lax.psum([entry[1] for entry in per_layer], ('dp', 'mp'))  41.9 us
    pallas_call x2, Pallas kernels, attend(): pl.pallas_call(lambda *refs: attend_kernel(combine, refs), grid=(groups,)...  40.7 us
    all_to_all x2, waiting for transfers between devices, swap(): lax.all_to_all(split, 'dp', split_axis=0, concat_axis=0, tiled=True)  39.8 us
    pallas_call x2, Pallas kernels, weight_grad(): pl.pallas_call(weight_grad_kernel, grid=(parts,), in_specs=[block, block,...  37.2 us
  transfers between devices with their start and end apart: 11, of which 5 were waited for; matrix products, arithmetic and copies ran while one was open for 5% of the time, Pallas kernels for 27%

profile of v1, /device:TPU:0, one launch (start us, length us, event | category | flops | bytes accessed | tf_op | source)
XLA Modules:
  0.0 701.2 jit_solution(6862031732123296761)
XLA Ops:
  7.2 6.2 slice_bitcast_fusion.10
  13.5 0.7 all-gather.23.cloned.1.call-update
  14.3 0.7 all-gather.25.cloned.1.call-update
  15.0 0.5 all-gather.27.cloned.1.call-update
  15.6 2.3 reduce-window.6
  17.8 0.3 slice_reduce_fusion
  18.3 0.6 slice_bitcast_fusion.6
  18.9 0.9 copy.51.refs_8_.refs_12_.refs_20_
  19.8 0.9 copy.72
  20.7 0.7 fusion.1
  21.5 0.6 slice.98.refs_6_.refs_18_
  22.1 0.6 fusion.10
  22.7 1.7 slice_bitcast_fusion.2
  24.4 6.9 slice_bitcast_fusion
  31.3 19.5 %attend.2 = (bf16[3,512,768]{2,1,0:T(8,128)(2,1)}, bf16[512,768]{1,0:T(8,128)(2,1)}, f32[3,8,512]{2,1,0:T(8,128)}, f32[512,768]{1,0:T(8,128)}, f32[512,8]{1,0:T(8,128)}, /*index=5*/bf16[576,768]{1,0:T(8,128)(2,1)}) custom-call(bf16[512,768]{1,0:T(8,128)(2,1)} %refs_9_.1, f32[1,768]{1,0:T(1,128)} %get-tuple-element.162.refs_1_.refs_10_, ...), custom_call_target="tpu_custom_call" | custom-call | flops 3221225472 | bytes 11010048 | tf_op jit(solution)/shard_map/attend/pallas_call | solution.py:272
  50.8 29.2 %all_to_all.40 = bf16[8,72,768]{2,1,0:T(8,128)(2,1)} all-to-all(bf16[8,72,768]{2,1,0:T(8,128)(2,1)} %bitcast.146), channel_id=1, replica_groups=mesh['dp'=8,'mp'=4] {'dp'}, dimensions={0} | all-to-all | bytes 1769472 | tf_op jit(solution)/shard_map/all_to_all | solution.py:669
  79.9 52.9 %all-gather.23.cloned.1.call-done = bf16[4,1,768,768]{3,2,1,0:T(8,128)(2,1)} async-done(((bf16[1,1,768,768]{3,2,1,0:T(8,128)(2,1)}), bf16[4,1,768,768]{3,2,1,0:T(8,128)(2,1)}) %all-gather.23.cloned.1.call-update) | async-done | bytes 4718608 | tf_op jit(solution)/shard_map/all_gather | solution.py:673
  132.8 9.9 %expert.2 = bf16[576,768]{1,0:T(8,128)(2,1)} custom-call(bf16[576,768]{1,0:T(8,128)(2,1)} %bitcast.112, bf16[4,768,768]{2,1,0:T(8,128)(2,1)} %bitcast.163, bf16[4,768,768]{2,1,0:T(8,128)(2,1)} %bitcast.165), custom_call_target="tpu_custom_call" | custom-call | flops 5435817984 | bytes 11206656 | tf_op jit(solution)/shard_map/expert/pallas_call | solution.py:557
  142.8 4.6 all-to-all-start.1
  147.4 0.5 all-gather.17.cloned.1.call-start
  147.9 0.9 copy.54.refs_3_.refs_23_.refs_2_
  148.7 0.9 copy.55.refs_4_.refs_25_.refs_5_
  149.6 0.9 copy.74
  150.5 0.7 fusion
  151.3 0.7 slice.99.refs_10_.refs_18_
  152.0 18.5 %all-to-all-done.1 = bf16[8,72,768]{2,1,0:T(8,128)(2,1)S(1)} async-done(((bf16[8,72,768]{2,1,0:T(8,128)(2,1)}), bf16[8,72,768]{2,1,0:T(8,128)(2,1)S(1)}, u32[]{:S(2)}, u32[]{:S(2)}) %all-to-all-start.1) | async-done | bytes 884768 | tf_op jit(solution)/shard_map/all_to_all | solution.py:669
  170.5 0.9 copy-done.1
  171.4 21.3 %attend.3 = (f32[512,768]{1,0:T(8,128)}, bf16[3,512,768]{2,1,0:T(8,128)(2,1)}, bf16[512,768]{1,0:T(8,128)(2,1)}, f32[3,8,512]{2,1,0:T(8,128)}, f32[512,768]{1,0:...) custom-call(f32[512,768]{1,0:T(8,128)} %get-tuple-element.50.refs_0_.refs_6_, ...), custom_call_target="tpu_custom_call" | custom-call | flops 3221225472 | bytes 11010048 | tf_op jit(solution)/shard_map/attend/pallas_call | solution.py:272
  192.7 27.3 %all_to_all.41 = bf16[8,72,768]{2,1,0:T(8,128)(2,1)} all-to-all(bf16[8,72,768]{2,1,0:T(8,128)(2,1)} %bitcast.145), channel_id=1, replica_groups=mesh['dp'=8,'mp'=4] {'dp'}, dimensions={0} | all-to-all | bytes 1769472 | tf_op jit(solution)/shard_map/all_to_all | solution.py:669
  220.0 31.2 %all-gather.27.cloned.1.call-done = bf16[4,1,768,768]{3,2,1,0:T(8,128)(2,1)} async-done(((bf16[1,1,768,768]{3,2,1,0:T(8,128)(2,1)}), bf16[4,1,768,768]{3,2,1,0:T(8,128)(2,1)}) %all-gather.27.cloned.1.call-update) | async-done | bytes 4718608 | tf_op jit(solution)/shard_map/all_gather | solution.py:673
  251.2 9.9 %expert.3 = bf16[576,768]{1,0:T(8,128)(2,1)} custom-call(bf16[576,768]{1,0:T(8,128)(2,1)} %bitcast.116, bf16[4,768,768]{2,1,0:T(8,128)(2,1)} %bitcast.167, bf16[4,768,768]{2,1,0:T(8,128)(2,1)} %bitcast.169), custom_call_target="tpu_custom_call" | custom-call | flops 5435817984 | bytes 11206656 | tf_op jit(solution)/shard_map/expert/pallas_call | solution.py:557
  261.1 4.6 all-to-all-start.3
  265.7 0.9 copy.57.rowcol.refs_2_
  266.6 0.9 copy.58.route_col.refs_5_
  267.5 21.3 %all-to-all-done.3 = bf16[8,72,768]{2,1,0:T(8,128)(2,1)S(1)} async-done(((bf16[8,72,768]{2,1,0:T(8,128)(2,1)}), bf16[8,72,768]{2,1,0:T(8,128)(2,1)S(1)}, u32[]{:S(2)}, u32[]{:S(2)}) %all-to-all-start.3) | async-done | bytes 884768 | tf_op jit(solution)/shard_map/all_to_all | solution.py:669
  288.8 1.0 copy-done
  289.7 4.6 turn.1
  294.4 27.3 %all_to_all.42 = bf16[8,72,768]{2,1,0:T(8,128)(2,1)} all-to-all(bf16[8,72,768]{2,1,0:T(8,128)(2,1)} %bitcast.147), channel_id=1, replica_groups=mesh['dp'=8,'mp'=4] {'dp'}, dimensions={0} | all-to-all | bytes 1769472 | tf_op jit(solution)/shard_map/all_to_all | solution.py:669
  321.7 0.7 all-gather.13.cloned.1.call-update
  322.4 0.2 all-gather.15.cloned.1.call-start
  322.7 12.9 %expert_back.2 = bf16[576,768]{1,0:T(8,128)(2,1)} custom-call(bf16[576,768]{1,0:T(8,128)(2,1)} %bitcast.117, bf16[576,768]{1,0:T(8,128)(2,1)} %bitcast.119, bf16[4,768,768]{2,1,0:T(8,128)(2,1)} %bitcast.168, bf16[4,768,768]{2,1,0:T(8,128)(2,1)} %bitcast.170), custom_call_target="tpu_custom_call" | custom-call | flops 8153726976 | bytes 12091392 | tf_op jit(solution)/shard_map/expert_back/pallas_call | solution.py:598
  335.5 27.3 %all_to_all.43 = bf16[8,72,768]{2,1,0:T(8,128)(2,1)} all-to-all(bf16[8,72,768]{2,1,0:T(8,128)(2,1)} %bitcast.148), channel_id=1, replica_groups=mesh['dp'=8,'mp'=4] {'dp'}, dimensions={0} | all-to-all | bytes 1769472 | tf_op jit(solution)/shard_map/all_to_all | solution.py:669
  362.8 30.9 %attend_back.2 = (f32[512,768]{1,0:T(8,128)}, bf16[768,768]{1,0:T(8,128)(2,1)}, bf16[768,768]{1,0:T(8,128)(2,1)}, bf16[768,768]{1,0:T(8,128)(2,1)}, bf16[768,768...) custom-call(bf16[512,768]{1,0:T(8,128)(2,1)} %refs_0_.3, ...), custom_call_target="tpu_custom_call" | custom-call | flops 6845104128 | bytes 21233664 | tf_op jit(solution)/shard_map/attend_back/pallas_call | solution.py:466
  393.7 27.3 %all_to_all.44 = bf16[8,72,768]{2,1,0:T(8,128)(2,1)} all-to-all(bf16[8,72,768]{2,1,0:T(8,128)(2,1)} %bitcast.141), channel_id=1, replica_groups=mesh['dp'=8,'mp'=4] {'dp'}, dimensions={0} | all-to-all | bytes 1769472 | tf_op jit(solution)/shard_map/all_to_all | solution.py:669
  421.1 0.4 all-reduce.4.cloned.1.call-start
  421.5 12.8 %expert_back.3 = bf16[576,768]{1,0:T(8,128)(2,1)} custom-call(bf16[576,768]{1,0:T(8,128)(2,1)} %bitcast.114, bf16[576,768]{1,0:T(8,128)(2,1)} %bitcast.121, bf16[4,768,768]{2,1,0:T(8,128)(2,1)} %bitcast.164, bf16[4,768,768]{2,1,0:T(8,128)(2,1)} %bitcast.166), custom_call_target="tpu_custom_call" | custom-call | flops 8153726976 | bytes 12091392 | tf_op jit(solution)/shard_map/expert_back/pallas_call | solution.py:598
  434.4 27.3 %all_to_all.45 = bf16[8,72,768]{2,1,0:T(8,128)(2,1)} all-to-all(bf16[8,72,768]{2,1,0:T(8,128)(2,1)} %bitcast.149), channel_id=1, replica_groups=mesh['dp'=8,'mp'=4] {'dp'}, dimensions={0} | all-to-all | bytes 1769472 | tf_op jit(solution)/shard_map/all_to_all | solution.py:669
  461.6 29.0 %attend_back.3 = (f32[512,768]{1,0:T(8,128)}, bf16[768,768]{1,0:T(8,128)(2,1)}, bf16[768,768]{1,0:T(8,128)(2,1)}, bf16[768,768]{1,0:T(8,128)(2,1)}, bf16[768,768...) custom-call(f32[512,768]{1,0:T(8,128)} %get-tuple-element.63.refs_0_, ...), custom_call_target="tpu_custom_call" | custom-call | flops 6845104128 | bytes 21233664 | tf_op jit(solution)/shard_map/attend_back/pallas_call | solution.py:466
  490.8 0.8 copy-done.12
  491.6 0.6 convolution_bitcast_fusion
  492.3 0.6 convolution_bitcast_fusion.1
  493.0 41.9 %all-reduce = (f32[1,768]{1,0:T(1,128)S(1)}, f32[1,768]{1,0:T(1,128)S(1)}, f32[1,32,12]{1,2,0:T(8,128)S(1)}, f32[1,32,12]{1,2,0:T(8,128)S(1)}, f32[1,768]{1,0:T(...) all-reduce(f32[1,768]{1,0:T(1,128)S(1)} %copy-done.22, ...), channel_id=1, replica_groups=mesh['dp'=8,'mp'=4] {'dp','mp'}, use_global_device_ids=true, to_apply=%region_4.5 | all-reduce | flops 16128 | bytes 129024 | tf_op jit(solution)/shard_map/psum | solution.py:782
  534.9 0.6 copy.67
  535.5 0.6 pad_maximum_fusion.3
  536.1 0.6 pad_maximum_fusion.2
  536.7 0.6 pad_maximum_fusion
  537.3 18.5 %weight_grad.3 = (f32[768,768]{1,0:T(8,128)}, f32[768,768]{1,0:T(8,128)}) custom-call(bf16[2304,768]{1,0:T(8,128)(2,1)} %all-gather.17.cloned.1.call-done.rows, bf16[2304,768]{1,0:T(8,128)(2,1)} %all-gather.19.cloned.1.call-done.grads, bf16[768,768]{1,0:T(8,128)(2,1)} %get-tuple-element.166.w_in, bf16[768,768]{1,0:T(8,128)(2,1)} %get-tuple-element.139.w_out), custom_call_target="tpu_custom_call" | custom-call | flops 10871635968 | bytes 14155776 | tf_op jit(solution)/shard_map/weight_grad/pallas_call | solution.py:641
  555.9 18.6 %weight_grad.2 = (f32[768,768]{1,0:T(8,128)}, f32[768,768]{1,0:T(8,128)}) custom-call(bf16[2304,768]{1,0:T(8,128)(2,1)} %all-gather.13.cloned.1.call-done.rows, bf16[2304,768]{1,0:T(8,128)(2,1)} %all-gather.15.cloned.1.call-done.grads, bf16[768,768]{1,0:T(8,128)(2,1)} %get-tuple-element.167.w_in, bf16[768,768]{1,0:T(8,128)(2,1)} %get-tuple-element.138.w_out), custom_call_target="tpu_custom_call" | custom-call | flops 10871635968 | bytes 14155776 | tf_op jit(solution)/shard_map/weight_grad/pallas_call | solution.py:641
  574.6 4.3 maximum_bitcast_fusion.1
  578.9 2.5 maximum_bitcast_fusion
  581.4 102.2 %all-reduce.4.cloned.1.call-done = (bf16[1,768,768]{2,1,0:T(8,128)(2,1)}, bf16[1,768,768]{2,1,0:T(8,128)(2,1)}, bf16[1,768,768]{2,1,0:T(8,128)(2,1)}, bf16[1,768...) async-done(((bf16[1,768,768]{2,1,0:T(8,128)(2,1)}, ...) | async-done | bytes 9437200 | tf_op jit(solution)/shard_map/psum | solution.py:772
  683.6 4.5 maximum_convert_fusion.1
  688.1 0.9 copy-done.11
  689.1 5.4 maximum_convert_fusion
  (83 shorter events, 0.9 us)
Async XLA Ops:
  7.2 72.7 %all-gather.21.cloned.1.call-start = ((), (), s32[]{:S(2)}) async-start(), calls=%async_computation.12 | async-start | bytes 5898240 | tf_op jit(solution)/shard_map/all_gather | solution.py:673
  13.4 2.2 copy-start.14
  13.4 5.5 copy-start.18
  13.4 6.4 copy-start.15
  13.4 7.3 %copy-start.19 = (f32[2,32,12]{1,0,2:T(2,128)S(1)}, f32[2,32,12]{1,0,2:T(2,128)}, u32[]{:S(2)}) copy-start(f32[2,32,12]{1,0,2:T(2,128)} %param.19) | copy-start | bytes 9220
  13.4 7.3 %copy-start.26 = (s32[2048]{0:T(1024)S(1)}, s32[2048]{0:T(1024)}, u32[]{:S(2)}) copy-start(s32[2048]{0:T(1024)} %constant.13.clone) | copy-start | bytes 24580
  13.4 119.4 %all-gather.23.cloned.1.call-start = ((), (), s32[]{:S(2)}) async-start(), calls=%async_computation.13 | async-start | bytes 5898240 | tf_op jit(solution)/shard_map/all_gather | solution.py:673
  14.2 7.9 %copy-start.20 = (f32[2,768]{1,0:T(2,128)S(1)}, f32[2,768]{1,0:T(2,128)}, u32[]{:S(2)}) copy-start(f32[2,768]{1,0:T(2,128)} %param.20) | copy-start | bytes 18436
  14.2 7.9 %copy-start.21 = (f32[2,768]{1,0:T(2,128)S(1)}, f32[2,768]{1,0:T(2,128)}, u32[]{:S(2)}) copy-start(f32[2,768]{1,0:T(2,128)} %param.16) | copy-start | bytes 18436
  14.2 8.5 %copy-start.2 = (bf16[2,768,768]{2,1,0:T(8,128)(2,1)S(1)}, bf16[2,768,768]{2,1,0:T(8,128)(2,1)}, u32[]{:S(2)}) copy-start(bf16[2,768,768]{2,1,0:T(8,128)(2,1)} %param.18) | copy-start | bytes 7077892
  14.2 205.8 %all-gather.25.cloned.1.call-start = ((), (), s32[]{:S(2)}) async-start(), calls=%async_computation.14 | async-start | bytes 5898240 | tf_op jit(solution)/shard_map/all_gather | solution.py:673
  15.0 236.2 %all-gather.27.cloned.1.call-start = ((), (), s32[]{:S(2)}) async-start(), calls=%async_computation.15 | async-start | bytes 5898240 | tf_op jit(solution)/shard_map/all_gather | solution.py:673
  142.8 27.7 %all-to-all-start.1 = ((bf16[8,72,768]{2,1,0:T(8,128)(2,1)}), bf16[8,72,768]{2,1,0:T(8,128)(2,1)S(1)}, u32[]{:S(2)}, u32[]{:S(2)}) async-start(bf16[8,72,768]{2,1,0:T(8,128)(2,1)} %bitcast.143), calls=%async_computation.1 | async-start | bytes 1769472 | tf_op jit(solution)/shard_map/all_to_all | solution.py:669
  147.4 390.0 %all-gather.17.cloned.1.call-start = ((), (), s32[]{:S(2)}) async-start(), calls=%async_computation.10 | async-start | bytes 4423680 | tf_op jit(solution)/shard_map/all_gather | solution.py:673
  170.5 0.9 copy-start.1
  261.1 27.7 %all-to-all-start.3 = ((bf16[8,72,768]{2,1,0:T(8,128)(2,1)}), bf16[8,72,768]{2,1,0:T(8,128)(2,1)S(1)}, u32[]{:S(2)}, u32[]{:S(2)}) async-start(bf16[8,72,768]{2,1,0:T(8,128)(2,1)} %bitcast.144), calls=%async_computation.3 | async-start | bytes 1769472 | tf_op jit(solution)/shard_map/all_to_all | solution.py:669
  265.7 271.6 %all-gather.19.cloned.1.call-start = ((), (), s32[]{:S(2)}) async-start(), calls=%async_computation.11 | async-start | bytes 4423680 | tf_op jit(solution)/shard_map/all_gather | solution.py:673
  288.8 1.0 copy-start
  321.7 234.2 %all-gather.13.cloned.1.call-start = ((), (), s32[]{:S(2)}) async-start(), calls=%async_computation.8 | async-start | bytes 4423680 | tf_op jit(solution)/shard_map/all_gather | solution.py:673
  322.4 233.4 %all-gather.15.cloned.1.call-start = ((), (), s32[]{:S(2)}) async-start(), calls=%async_computation.9 | async-start | bytes 4423680 | tf_op jit(solution)/shard_map/all_gather | solution.py:673
  421.1 262.5 %all-reduce.4.cloned.1.call-start = ((), (), s32[]{:S(2)}) async-start(), calls=%async_computation.16 | async-start | bytes 18874368 | tf_op jit(solution)/shard_map/psum | solution.py:772
  490.7 0.9 copy-start.12
  490.7 1.5 copy-start.13
  490.7 2.2 copy-start.16
  490.7 2.2 copy-start.17
  490.7 2.2 copy-start.22
  490.7 2.2 copy-start.23
  490.7 2.2 copy-start.24
  490.8 2.2 copy-start.25
  555.9 18.7 %copy-start.4 = (f32[768,768]{1,0:T(8,128)S(1)}, f32[768,768]{1,0:T(8,128)}, u32[]{:S(2)}) copy-start(f32[768,768]{1,0:T(8,128)} %get-tuple-element.89) | copy-start | bytes 7077892
  574.5 4.3 copy-start.3
  574.5 4.3 copy-start.5
  683.6 4.5 copy-start.6
  683.6 4.5 copy-start.7
  683.6 4.5 copy-start.8
  683.6 4.5 copy-start.9
  683.6 4.5 copy-start.10
  683.6 5.4 copy-start.11
Sparse Core Ops, SparseCore 0:
  13.5 59.7 all-gather.20
  75.7 57.0 all-gather.22
  134.7 57.0 all-gather.24
  194.1 57.0 all-gather.26
  252.9 47.2 all-gather.16
  321.8 45.1 all-gather.18
  368.9 47.2 all-gather.12
  421.2 45.2 all-gather.14
  490.9 192.6 all-reduce.3

commit v2 on v1

v2 whole, which is shorter than its diff:
```python
import functools

import jax
import jax.numpy as jnp
import numpy as np
from jax import lax
from jax.experimental import pallas as pl
from jax.experimental.pallas import tpu as pltpu
from jax.sharding import PartitionSpec as P

HEAD_DIM = 64
BUCKETS = 32
MAX_DIST = 128
LAYERS = 2
LEN = 512

SIDE = 128
SPAN = 256
WINDOW_ROWS = 8
GROUP_HEADS = 4
GROUP = GROUP_HEADS * HEAD_DIM
PAIR = 2 * HEAD_DIM
VMEM_BYTES = 56 * 1024 * 1024
QUICK = pl.CostEstimate(flops=1000000, bytes_accessed=1000000, transcendentals=0)

epsilon = 1e-06
masked_score = -1000000000.0
highest = lax.Precision.HIGHEST
f32 = jnp.float32
bf16 = jnp.bfloat16

NT = (((1,), (1,)), ((), ()))
TN = (((0,), (0,)), ((), ()))


def bucket_limits():
    half_count = BUCKETS // 2
    exact_count = half_count // 2
    lengths = np.arange(exact_count, 4 * MAX_DIST + 2 * LEN + 2)
    levels = (
        np.log(lengths / exact_count) / np.log(MAX_DIST / exact_count) * (half_count - exact_count)
    ).astype(np.int64)
    levels = np.minimum(levels, half_count - exact_count - 1)
    limits = []
    for target in range(1, half_count - exact_count):
        limits.append(int(lengths[np.argmax(levels >= target)]))
    return limits


def bucket_of(distance):
    half_count = BUCKETS // 2
    exact_count = half_count // 2
    magnitude = np.abs(distance)
    counted = np.full(distance.shape, exact_count, np.int32)
    for limit_value in bucket_limits():
        counted = counted + (magnitude >= limit_value).astype(np.int32)
    return np.where(distance > 0, half_count, 0) + np.where(
        magnitude < exact_count, magnitude, counted
    )


def window_buckets():
    place = np.arange(SPAN)
    shift = np.where(place < SIDE, -place, SPAN - place)
    rows = [bucket_of(offset * SIDE + shift) for offset in (-1, 0, 1)]
    for row in rows:
        row[SIDE] = -1
    far = bucket_of(np.array([-2 * SIDE + SIDE - 1, 2 * SIDE - SIDE + 1]))
    rows += [np.full(SPAN, far[0]), np.full(SPAN, far[1])]
    rows += [np.full(SPAN, -1)] * (WINDOW_ROWS - len(rows))
    return np.stack(rows).astype(np.int32)


def window_onehot():
    return (
        jnp.asarray(window_buckets().reshape(-1))[:, None]
        == jnp.arange(BUCKETS, dtype=jnp.int32)[None, :]
    ).astype(f32)


def params(**extra):
    return pltpu.CompilerParams(vmem_limit_bytes=VMEM_BYTES, **extra)


def dot(a, b, dims=None, precision=None):
    if dims is None:
        return jnp.dot(a, b, preferred_element_type=f32, precision=precision)
    return lax.dot_general(a, b, dims, preferred_element_type=f32, precision=precision)


def rms_factor(values):
    return lax.rsqrt(jnp.mean(values * values, axis=-1, keepdims=True) + epsilon)


def half_mask(half):
    lane = lax.broadcasted_iota(jnp.int32, (1, PAIR), 1)
    inside = (lane >= half * HEAD_DIM) & (lane < (half + 1) * HEAD_DIM)
    return inside.astype(f32)


def bias_blocks(windows):
    blocks = {}
    for row, offset in enumerate((-1, 0, 1)):
        spread = jnp.broadcast_to(windows[row : row + 1, :], (SIDE, SPAN))
        blocks[offset] = pltpu.roll(spread, 0, 1, stride=1, stride_axis=0)[:, :SIDE]
    blocks[-2] = jnp.broadcast_to(windows[3:4, :SIDE], (SIDE, SIDE))
    blocks[2] = jnp.broadcast_to(windows[4:5, :SIDE], (SIDE, SIDE))
    return blocks


def offset_of(key_block, query_block):
    return max(-2, min(2, key_block - query_block))


def bias_part(blocks, first_query, width):
    columns = []
    for query_block in range(first_query // SIDE, (first_query + width) // SIDE):
        columns.append(
            jnp.concatenate(
                [blocks[offset_of(key_block, query_block)] for key_block in range(LEN // SIDE)],
                axis=0,
            )
        )
    return jnp.concatenate(columns, axis=1)


def diagonal_sums(block):
    padded = jnp.concatenate([block, jnp.zeros((SIDE, SPAN - SIDE), f32)], axis=1)
    total = padded[:8]
    for first in range(8, SIDE, 8):
        total = total + pltpu.roll(padded[first : first + 8], SPAN - first, 1)
    row = lax.broadcasted_iota(jnp.int32, (8, SPAN), 0)
    for bit in (1, 2, 4):
        total = jnp.where((row & bit) != 0, pltpu.roll(total, SPAN - bit, 1), total)
    return jnp.sum(total, axis=0, keepdims=True)


def mask_of(seg_col, seg_row):
    return jnp.where(seg_col == seg_row, 0.0, masked_score).astype(f32)


def place_matrix(rowid_row, count):
    rows = lax.broadcasted_iota(jnp.int32, (count, rowid_row.shape[1]), 0)
    return (rows == rowid_row).astype(bf16)


def take_matrix(rowid_col, count):
    lanes = lax.broadcasted_iota(jnp.int32, (rowid_col.shape[0], count), 1)
    return (lanes == rowid_col).astype(bf16)


def route_onehot(route_col, experts):
    lanes = lax.broadcasted_iota(jnp.int32, (route_col.shape[0], experts), 1)
    return (lanes == route_col).astype(f32)


def join(refs):
    return jnp.concatenate([ref[...].astype(f32) for ref in refs], axis=0).astype(bf16)


def cut(values, refs):
    count = values.shape[0] // len(refs)
    for index, ref in enumerate(refs):
        ref[...] = values[index * count : (index + 1) * count].astype(ref.dtype)


QUERY_SPAN = 256
SMALL_ROWS = 128


def attend_kernel(layer, experts, refs):
    refs = list(refs)
    take = lambda count: [refs.pop(0) for _ in range(count)]
    combine = layer > 0
    if combine:
        middle_prev, prob_prev, rowcol_prev, route_prev = take(4)
        back_prev = take(experts)
    else:
        (tokens,) = take(1)
    gain_attn, wq, wk, wv, wout, windows, seg_row, seg_col = take(8)
    gain_ffn, router, rowid_row = take(3)
    if combine:
        (x_out,) = take(1)
    proj, mixed, lse, middle, prob = take(5)
    buffer = take(experts)
    normed_s, x_s, acc_s, mask_s = take(4)
    step = pl.program_id(0)

    @pl.when(step == 0)
    def _():
        if combine:
            chosen = route_onehot(route_prev[0], experts)
            gate = jnp.sum(prob_prev[...] * chosen, axis=-1, keepdims=True)
            rows = join(back_prev)
            returned = dot(take_matrix(rowcol_prev[0], rows.shape[0]), rows)
            x = middle_prev[...] + gate * returned
            x_out[...] = x
        else:
            x = tokens[...].astype(f32)
        x_s[...] = x
        normed_s[...] = (x * rms_factor(x) * gain_attn[layer : layer + 1, :]).astype(bf16)
        acc_s[...] = jnp.zeros_like(acc_s)
        mask_s[...] = mask_of(seg_col[...], seg_row[...])

    normed = normed_s[...]
    q = dot(normed, wq[0]).astype(bf16)
    k = dot(normed, wk[0]).astype(bf16)
    v = dot(normed, wv[0]).astype(bf16)
    proj[0] = q
    proj[1] = k
    proj[2] = v
    for pair in range(GROUP_HEADS // 2):
        lanes = slice(pair * PAIR, (pair + 1) * PAIR)
        q2 = q[:, lanes].astype(f32) * HEAD_DIM ** (-0.5)
        k2 = k[:, lanes]
        v2t = v[:, lanes].T
        outs = []
        for half in range(2):
            head = pair * 2 + half
            qm = (q2 * half_mask(half)).astype(bf16)
            vt = v2t[half * HEAD_DIM : (half + 1) * HEAD_DIM, :]
            blocks = bias_blocks(windows[0, head])
            parts = []
            for first in range(0, LEN, QUERY_SPAN):
                span = slice(first, first + QUERY_SPAN)
                scores = dot(k2, qm[span], NT)
                scores = scores + bias_part(blocks, first, QUERY_SPAN) + mask_s[:, span]
                top = jnp.max(scores, axis=0, keepdims=True)
                powers = jnp.exp(scores - top)
                total = jnp.sum(powers, axis=0, keepdims=True)
                parts.append(dot(vt, powers.astype(bf16)) * (1.0 / total))
                lse[0, head : head + 1, span] = top + jnp.log(total)
            outs.append(jnp.concatenate(parts, axis=1))
        mixed[:, lanes] = jnp.concatenate(outs, axis=0).T.astype(bf16)
    acc_s[...] += dot(mixed[...], wout[0])

    @pl.when(step == pl.num_programs(0) - 1)
    def _():
        mid = x_s[...] + acc_s[...]
        middle[...] = mid
        nf = (mid * rms_factor(mid) * gain_ffn[layer : layer + 1, :]).astype(bf16)
        logits = dot(nf.astype(f32), router[0], precision=highest)
        powers = jnp.exp(logits - jnp.max(logits, axis=-1, keepdims=True))
        prob[...] = powers / jnp.sum(powers, axis=-1, keepdims=True)
        cut(dot(place_matrix(rowid_row[0], experts * buffer[0].shape[0]), nf), buffer)


def whole(array):
    zeros = (0,) * array.ndim
    return pl.BlockSpec(array.shape, lambda g: zeros)


def whole_shape(shape):
    zeros = (0,) * len(shape)
    return pl.BlockSpec(shape, lambda g: zeros)


def of_layer(array, layer):
    place = (layer,) + (0,) * (array.ndim - 1)
    return pl.BlockSpec((1,) + array.shape[1:], lambda g: place)


def qkv_specs(width, layer):
    per = width // GROUP
    return [
        pl.BlockSpec(
            (1, width, GROUP), functools.partial(lambda part, g: (layer, 0, part * per + g), part)
        )
        for part in range(3)
    ]


def group_specs(width, layer):
    return (
        pl.BlockSpec((1, GROUP, width), lambda g: (layer, g, 0)),
        pl.BlockSpec((1, GROUP_HEADS, WINDOW_ROWS, SPAN), lambda g: (layer, g, 0, 0)),
    )


def attend(layer, source, common):
    qkv_w, router = common["qkv_w"], common["router"]
    width = qkv_w.shape[1]
    groups = width // GROUP
    experts = router.shape[2]
    out_spec, window_spec = group_specs(width, layer)
    ins, specs = [], []

    def add(array, spec=None):
        ins.append(array)
        specs.append(whole(array) if spec is None else spec)

    if layer > 0:
        add(source["middle"])
        add(source["prob"])
        for name in ("rowcol", "route"):
            add(common[name], of_layer(common[name], layer - 1))
        for block in source["back"]:
            add(block)
    else:
        add(source)
    add(common["gain_attn"])
    for spec in qkv_specs(width, layer):
        add(qkv_w, spec)
    add(common["out_w"], out_spec)
    add(common["windows"], window_spec)
    add(common["seg_row"])
    add(common["seg_col"])
    add(common["gain_ffn"])
    add(router, of_layer(router, layer))
    add(common["rowrow"], of_layer(common["rowrow"], layer))
    block = (common["capacity"], width)
    shapes = [
        ((3, LEN, width), bf16, pl.BlockSpec((3, LEN, GROUP), lambda g: (0, 0, g))),
        ((LEN, width), bf16, pl.BlockSpec((LEN, GROUP), lambda g: (0, g))),
        ((groups, 8, LEN), f32, pl.BlockSpec((1, 8, LEN), lambda g: (g, 0, 0))),
        ((LEN, width), f32, whole_shape((LEN, width))),
        ((LEN, experts), f32, whole_shape((LEN, experts))),
    ] + [(block, bf16, whole_shape(block))] * experts
    if layer > 0:
        shapes = [((LEN, width), f32, whole_shape((LEN, width)))] + shapes
    return pl.pallas_call(
        lambda *refs: attend_kernel(layer, experts, refs),
        grid=(groups,),
        in_specs=specs,
        out_specs=[s[2] for s in shapes],
        out_shape=[jax.ShapeDtypeStruct(s[0], s[1]) for s in shapes],
        scratch_shapes=[
            pltpu.VMEM((LEN, width), bf16),
            pltpu.VMEM((LEN, width), f32),
            pltpu.VMEM((LEN, width), f32),
            pltpu.VMEM((LEN, LEN), f32),
        ],
        compiler_params=params(),
        cost_estimate=QUICK,
        name="attend",
    )(*ins)


def attend_back_kernel(layer, experts, refs):
    refs = list(refs)
    take = lambda count: [refs.pop(0) for _ in range(count)]
    first_layer = layer == 0
    gradient, rowcol, gate_grad, prob, route_col, middle, gain_ffn, router = take(8)
    gback = take(experts)
    x_ref, gain_attn, wq, wk, wv, wout, proj, mixed, lse, windows, seg_row, seg_col, onehot = take(13)
    if not first_layer:
        rowrow_prev, rowcol_prev, prob_prev, route_prev = take(4)
        back_prev = take(experts)
    grad_in, big = take(2)
    if not first_layer:
        (gate_grad_prev,) = take(1)
        buffer_prev = take(experts)
    normt_s, mg_s, att_s, acc_s, mask_s, small_s, rel_s = take(7)
    step = pl.program_id(0)
    width = att_s.shape[1]
    places = dict(
        q=0, k=width, small=2 * width, v=2 * width + SMALL_ROWS, out=3 * width + SMALL_ROWS
    )
    columns = pl.ds(pl.multiple_of(step * GROUP, GROUP), GROUP)

    @pl.when(step == 0)
    def _():
        g = gradient[...].astype(f32)
        rows = join(gback)
        expert_part = dot(take_matrix(rowcol[0], rows.shape[0]), rows)
        probability = prob[...]
        chosen = route_onehot(route_col[0], experts)
        gate = jnp.sum(probability * chosen, axis=-1, keepdims=True)
        logit_grad = gate_grad[...] * gate * (chosen - probability)
        mid = middle[...]
        r = rms_factor(mid)
        scaled = mid * r
        gain = gain_ffn[layer : layer + 1, :]
        nf = (scaled * gain).astype(bf16).astype(f32)
        small_s[...] = jnp.zeros_like(small_s)
        small_s[:experts] = dot(logit_grad, nf, TN, precision=highest)
        ffn_in = expert_part + dot(logit_grad, router[0], NT, precision=highest)
        u = ffn_in * gain
        mg = g + r * (u - scaled * (r * jnp.mean(u * mid, axis=-1, keepdims=True)))
        small_s[experts + 1 : experts + 2] = jnp.sum(ffn_in * scaled, axis=0, keepdims=True)
        mg_s[...] = mg
        att_s[...] = mg.astype(bf16)
        x = x_ref[...].astype(f32)
        normed = (x * rms_factor(x) * gain_attn[layer : layer + 1, :]).astype(bf16)
        normt_s[...] = normed.T
        acc_s[...] = jnp.zeros_like(acc_s)
        mask_s[...] = mask_of(seg_col[...], seg_row[...])

    att = att_s[...]
    out_rows = pl.ds(pl.multiple_of(places["out"] + step * GROUP, SMALL_ROWS), GROUP)
    big[out_rows, :] = dot(mixed[...], att, TN).astype(big.dtype)
    mixed_grad = dot(att, wout[0], NT).astype(bf16)
    dqs, dks, dvs, rel_rows = [], [], [], []
    for pair in range(GROUP_HEADS // 2):
        lanes = slice(pair * PAIR, (pair + 1) * PAIR)
        q2 = proj[0, :, lanes].astype(f32) * HEAD_DIM ** (-0.5)
        k2 = proj[1, :, lanes]
        v2 = proj[2, :, lanes]
        k2t = k2.T
        o2 = mixed_grad[:, lanes].astype(f32)
        dk = jnp.zeros((LEN, PAIR), f32)
        dv = jnp.zeros((LEN, PAIR), f32)
        dqts = []
        for half in range(2):
            head = pair * 2 + half
            qm = (q2 * half_mask(half)).astype(bf16)
            om = (o2 * half_mask(half)).astype(bf16)
            kt = k2t[half * HEAD_DIM : (half + 1) * HEAD_DIM, :]
            blocks = bias_blocks(windows[0, head])
            sums = {}
            parts = []
            for first in range(0, LEN, QUERY_SPAN):
                span = slice(first, first + QUERY_SPAN)
                scores = dot(k2, qm[span], NT)
                scores = scores + bias_part(blocks, first, QUERY_SPAN) + mask_s[:, span]
                powers = jnp.exp(scores - lse[0, head : head + 1, span])
                prob_grad = dot(v2, om[span], NT)
                weighted = powers * prob_grad
                delta = jnp.sum(weighted, axis=0, keepdims=True)
                score_grad = weighted - powers * delta
                for kb in range(LEN // SIDE):
                    for qb in range(QUERY_SPAN // SIDE):
                        piece = score_grad[kb * SIDE : (kb + 1) * SIDE, qb * SIDE : (qb + 1) * SIDE]
                        offset = offset_of(kb, qb + first // SIDE)
                        sums[offset] = sums[offset] + piece if offset in sums else piece
                sg = score_grad.astype(bf16)
                dv = dv + dot(powers.astype(bf16), om[span])
                dk = dk + dot(sg, qm[span])
                parts.append(dot(kt, sg))
            dqts.append(jnp.concatenate(parts, axis=1))
            rel_rows.append(
                [diagonal_sums(sums[offset]) for offset in (-1, 0, 1)]
                + [
                    jnp.concatenate(
                        [jnp.sum(sums[offset], axis=0, keepdims=True)] + [jnp.zeros((1, SPAN - SIDE), f32)],
                        axis=1,
                    )
                    for offset in (-2, 2)
                ]
            )
        dqs.append((jnp.concatenate(dqts, axis=0) * HEAD_DIM ** (-0.5)).T)
        dks.append(dk)
        dvs.append(dv)
    total = acc_s[...]
    for name, weight, pieces in (("q", wq, dqs), ("k", wk, dks), ("v", wv, dvs)):
        part = jnp.concatenate(pieces, axis=1).astype(bf16)
        first = places[name]
        big[first : first + width, columns] = dot(normt_s[...], part).astype(big.dtype)
        total = total + dot(part, weight[0], NT)
    acc_s[...] = total
    for group in range(width // GROUP):

        @pl.when(step == group)
        def _(group=group):
            for index, rows in enumerate(rel_rows):
                at = group * GROUP_HEADS + index
                for kind, row in enumerate(rows):
                    rel_s[kind, at : at + 1, :] = row

    @pl.when(step == pl.num_programs(0) - 1)
    def _():
        x = x_ref[...].astype(f32)
        r = rms_factor(x)
        scaled = x * r
        attn_in = acc_s[...]
        u = attn_in * gain_attn[layer : layer + 1, :]
        g = mg_s[...] + r * (u - scaled * (r * jnp.mean(u * x, axis=-1, keepdims=True)))
        small_s[experts : experts + 1] = jnp.sum(attn_in * scaled, axis=0, keepdims=True)
        heads = width // HEAD_DIM
        bucket_sums = jnp.zeros((heads, BUCKETS), f32)
        for kind in range(5):
            bucket_sums = bucket_sums + dot(
                rel_s[kind], onehot[kind * SPAN : (kind + 1) * SPAN], precision=highest
            )
        small_s[experts + 2 : experts + 2 + heads, :BUCKETS] = bucket_sums
        big[places["small"] : places["small"] + SMALL_ROWS, :] = small_s[...].astype(big.dtype)
        big[places["out"] + width :, :] = jnp.zeros((SMALL_ROWS, width), big.dtype)
        grad_in[...] = g
        if not first_layer:
            send_back(
                g, back_prev, rowrow_prev, rowcol_prev, prob_prev, route_prev, buffer_prev, gate_grad_prev
            )


def send_back(g, back, rowrow, rowcol, prob, route_col, buffer, gate_grad):
    rows = join(back)
    returned = dot(take_matrix(rowcol[0], rows.shape[0]), rows)
    chosen = route_onehot(route_col[0], prob.shape[1])
    gate = jnp.sum(prob[...] * chosen, axis=-1, keepdims=True)
    gate_grad[...] = jnp.sum(g * returned, axis=-1, keepdims=True)
    expert_grad = (gate * g).astype(bf16)
    cut(dot(place_matrix(rowrow[0], rows.shape[0]), expert_grad), buffer)
    return gate * returned


def attend_back(layer, states, gradient, gback, gate_grad, common):
    state = states[layer]
    qkv_w, router = common["qkv_w"], common["router"]
    width = qkv_w.shape[1]
    groups = width // GROUP
    experts = router.shape[2]
    out_spec, window_spec = group_specs(width, layer)
    ins, specs = [], []

    def add(array, spec=None):
        ins.append(array)
        specs.append(whole(array) if spec is None else spec)

    add(gradient)
    add(common["rowcol"], of_layer(common["rowcol"], layer))
    add(gate_grad)
    add(state["prob"])
    add(common["route"], of_layer(common["route"], layer))
    add(state["middle"])
    add(common["gain_ffn"])
    add(router, of_layer(router, layer))
    for block in gback:
        add(block)
    add(state["x"])
    add(common["gain_attn"])
    for spec in qkv_specs(width, layer):
        add(qkv_w, spec)
    add(common["out_w"], out_spec)
    add(state["proj"], pl.BlockSpec((3, LEN, GROUP), lambda g: (0, 0, g)))
    add(state["mixed"], pl.BlockSpec((LEN, GROUP), lambda g: (0, g)))
    add(state["lse"], pl.BlockSpec((1, 8, LEN), lambda g: (g, 0, 0)))
    add(common["windows"], window_spec)
    add(common["seg_row"])
    add(common["seg_col"])
    add(common["onehot"])
    payload = (4 * width + 2 * SMALL_ROWS, width)
    shapes = [((LEN, width), f32), (payload, bf16)]
    if layer > 0:
        for name in ("rowrow", "rowcol"):
            add(common[name], of_layer(common[name], layer - 1))
        add(states[layer - 1]["prob"])
        add(common["route"], of_layer(common["route"], layer - 1))
        for block in states[layer - 1]["back"]:
            add(block)
        shapes += [((LEN, 1), f32)] + [((common["capacity"], width), bf16)] * experts
    return pl.pallas_call(
        lambda *refs: attend_back_kernel(layer, experts, refs),
        grid=(groups,),
        in_specs=specs,
        out_specs=[whole_shape(s[0]) for s in shapes],
        out_shape=[jax.ShapeDtypeStruct(s[0], s[1]) for s in shapes],
        scratch_shapes=[
            pltpu.VMEM((width, LEN), bf16),
            pltpu.VMEM((LEN, width), f32),
            pltpu.VMEM((LEN, width), bf16),
            pltpu.VMEM((LEN, width), f32),
            pltpu.VMEM((LEN, LEN), f32),
            pltpu.VMEM((SMALL_ROWS, width), f32),
            pltpu.VMEM((5, width // HEAD_DIM, SPAN), f32),
        ],
        compiler_params=params(),
        cost_estimate=QUICK,
        name="attend_back",
    )(*ins)


def turn_kernel(experts, refs):
    middle, cotangent, rowrow, rowcol, prob, route_col = refs[:6]
    back = refs[6 : 6 + experts]
    output, gate_grad = refs[6 + experts : 8 + experts]
    buffer = refs[8 + experts :]
    g = cotangent[...].astype(f32)
    added = send_back(g, back, rowrow, rowcol, prob, route_col, buffer, gate_grad)
    output[...] = middle[...] + added


def turn(layer, state, cotangent, common):
    width = cotangent.shape[1]
    experts = len(state["back"])
    ins = [state["middle"], cotangent, common["rowrow"], common["rowcol"], state["prob"]]
    ins += [common["route"]] + list(state["back"])
    specs = [whole(array) for array in ins]
    for index in (2, 3, 5):
        specs[index] = of_layer(ins[index], layer)
    shapes = [((LEN, width), f32), ((LEN, 1), f32)]
    shapes += [((common["capacity"], width), bf16)] * experts
    return pl.pallas_call(
        lambda *refs: turn_kernel(experts, refs),
        grid=(1,),
        in_specs=specs,
        out_specs=[whole_shape(s[0]) for s in shapes],
        out_shape=[jax.ShapeDtypeStruct(s[0], s[1]) for s in shapes],
        compiler_params=params(),
        cost_estimate=QUICK,
        name="turn",
    )(*ins)


GELU_A = float(np.sqrt(2.0 / np.pi))
GELU_B = 0.044715


def gelu_tanh(hidden):
    return jnp.tanh(GELU_A * (hidden + GELU_B * (hidden * hidden * hidden)))


def gelu_of(hidden, curve):
    return 0.5 * hidden * (1.0 + curve)


def gelu_slope(hidden, curve):
    inner = GELU_A * (1.0 + (3.0 * GELU_B) * (hidden * hidden))
    return 0.5 * (1.0 + curve) + 0.5 * hidden * (1.0 - curve * curve) * inner


def expert_kernel(experts, refs):
    blocks = refs[:experts]
    w_in, w_out, rows = refs[experts : experts + 3]
    outs = refs[experts + 3 : -1]
    acc = refs[-1]
    step = pl.program_id(0)

    @pl.when(step == 0)
    def _():
        rows[...] = join(blocks)
        acc[...] = jnp.zeros_like(acc)

    hidden = dot(rows[...], w_in[...])
    active = gelu_of(hidden, gelu_tanh(hidden)).astype(bf16)
    acc[...] += dot(active, w_out[...])

    @pl.when(step == pl.num_programs(0) - 1)
    def _():
        cut(acc[...], outs)


def weight_specs(weights):
    if len(weights) == 1:
        width = weights[0].shape[1]
        return [
            pl.BlockSpec((width, width), lambda b: (2 * b, 0)),
            pl.BlockSpec((width, width), lambda b: (2 * b + 1, 0)),
        ]
    parts = weights[0].shape[0] // weights[1].shape[1]
    return [
        pl.BlockSpec((array.shape[0] // parts, array.shape[1]), lambda b: (b, 0))
        for array in weights
    ]


def expert(blocks, weights, parts):
    experts = len(blocks)
    capacity, width = blocks[0].shape
    count = experts * capacity
    rows_shape = jax.ShapeDtypeStruct((count, width), bf16)
    specs = [whole(block) for block in blocks]
    hidden = weights[-1].shape[0] // (2 if len(weights) == 1 else 1)
    results = pl.pallas_call(
        lambda *refs: expert_kernel(experts, refs),
        grid=(parts,),
        in_specs=specs + weight_specs(weights),
        out_specs=[whole_shape((count, width))] + specs,
        out_shape=[rows_shape] + [jax.ShapeDtypeStruct(b.shape, bf16) for b in blocks],
        scratch_shapes=[pltpu.VMEM((count, width), f32)],
        compiler_params=params(),
        cost_estimate=QUICK,
        name="expert",
    )(*blocks, *(weights * 2)[:2])
    return results[0], results[1:]


def expert_back_kernel(experts, refs):
    rows = refs[0]
    blocks = refs[1 : 1 + experts]
    w_in, w_out, grads = refs[1 + experts : 4 + experts]
    outs = refs[4 + experts : -1]
    acc = refs[-1]
    step = pl.program_id(0)

    @pl.when(step == 0)
    def _():
        grads[...] = join(blocks)
        acc[...] = jnp.zeros_like(acc)

    hidden = dot(rows[...], w_in[...])
    act_grad = dot(grads[...], w_out[...], NT)
    pre_grad = (act_grad * gelu_slope(hidden, gelu_tanh(hidden))).astype(bf16)
    acc[...] += dot(pre_grad, w_in[...], NT)

    @pl.when(step == pl.num_programs(0) - 1)
    def _():
        cut(acc[...], outs)


def expert_back(rows, blocks, weights, parts):
    experts = len(blocks)
    count, width = rows.shape
    specs = [whole(block) for block in blocks]
    hidden = weights[-1].shape[0] // (2 if len(weights) == 1 else 1)
    results = pl.pallas_call(
        lambda *refs: expert_back_kernel(experts, refs),
        grid=(parts,),
        in_specs=[whole(rows)] + specs + weight_specs(weights),
        out_specs=[whole(rows)] + specs,
        out_shape=[jax.ShapeDtypeStruct(a.shape, bf16) for a in [rows] + list(blocks)],
        scratch_shapes=[pltpu.VMEM((count, width), f32)],
        compiler_params=params(),
        cost_estimate=QUICK,
        name="expert_back",
    )(rows, *blocks, *(weights * 2)[:2])
    return results[0], results[1:]


def weight_grad_kernel(order, rows, grads, w_in, w_out, *refs):
    g_in, g_out = refs[-2:]
    step = pl.program_id(0)

    @pl.when(step == 0)
    def _():
        g_in[...] = jnp.zeros_like(g_in)
        g_out[...] = jnp.zeros_like(g_out)

    hidden = dot(rows[...], w_in[0, 0])
    curve = gelu_tanh(hidden)
    active = gelu_of(hidden, curve).astype(bf16)
    act_grad = dot(grads[...], w_out[0, 0], NT)
    pre_grad = (act_grad * gelu_slope(hidden, curve)).astype(bf16)
    g_out[0, 0] += dot(active, grads[...], TN)
    g_in[0, 0] += dot(rows[...], pre_grad, TN)


def weight_grad(layer, order, rows_all, grads_all, w_in, w_out, into):
    width = w_in.shape[2]
    parts = order.shape[0]
    count = rows_all.shape[0] // parts

    def part_of(array):
        return pl.BlockSpec((1, 1) + array.shape[2:], lambda b, order: (layer, 0, 0, 0))

    specs = [part_of(w_in), part_of(w_out)]
    grid_spec = pltpu.PrefetchScalarGridSpec(
        num_scalar_prefetch=1,
        grid=(parts,),
        in_specs=[
            pl.BlockSpec((count, width), lambda b, order: (order[b], 0)),
            pl.BlockSpec((count, width), lambda b, order: (b, 0)),
        ]
        + specs
        + [pl.BlockSpec(memory_space=pl.ANY)] * len(into),
        out_specs=specs,
    )
    return pl.pallas_call(
        weight_grad_kernel,
        grid_spec=grid_spec,
        out_shape=[
            jax.ShapeDtypeStruct(w_in.shape, f32),
            jax.ShapeDtypeStruct(w_out.shape, f32),
        ],
        input_output_aliases={5 + index: index for index in range(len(into))},
        compiler_params=params(),
        cost_estimate=QUICK,
        name="weight_grad",
    )(order, rows_all, grads_all, w_in, w_out, *into)


def finish_kernel(side, first, second, qkv, out):
    kind = pl.program_id(0) % 4
    upper = (side[0] + jnp.where(kind >= 2, 1, 0)) % 2
    values = jnp.where(upper == 0, first[...].astype(f32), second[...].astype(f32))

    @pl.when(kind < 3)
    def _():
        qkv[0] = values

    @pl.when(kind == 3)
    def _():
        out[0] = values


def finish(side, first, second):
    width = first.shape[1] // LAYERS

    def rows_of(turned):
        def place(step, side):
            kind = step % 4
            lower, higher = jnp.minimum(kind, 1), jnp.maximum(kind, 2) - 2
            return jnp.where(side[0] == turned, lower, higher), step // 4

        return pl.BlockSpec((width, width), place)

    grid_spec = pltpu.PrefetchScalarGridSpec(
        num_scalar_prefetch=1,
        grid=(4 * LAYERS,),
        in_specs=[rows_of(0), rows_of(1)],
        out_specs=[
            pl.BlockSpec(
                (1, width, width), lambda step, side: (step // 4, 0, jnp.minimum(step % 4, 2))
            ),
            pl.BlockSpec((1, width, width), lambda step, side: (step // 4, 0, 0)),
        ],
    )
    return pl.pallas_call(
        finish_kernel,
        grid_spec=grid_spec,
        out_shape=[
            jax.ShapeDtypeStruct((LAYERS, width, 3 * width), f32),
            jax.ShapeDtypeStruct((LAYERS, width, width), f32),
        ],
        compiler_params=params(),
        cost_estimate=QUICK,
        name="finish",
    )(side.reshape(1), first, second)


def partner(array, axis, bit):
    pairs = [(index, index ^ bit) for index in range(lax.axis_size(axis))]
    return lax.ppermute(array, axis, pairs)


def swap(blocks):
    return [blocks[0]] + [partner(block, "dp", k) for k, block in enumerate(blocks) if k > 0]


def gather_rows(rows):
    return lax.all_gather(rows, "mp", axis=0, tiled=True)


def gather_weights(w_in, w_out, layer):
    first, second = w_in[layer, 0], w_out[layer, 0]
    if first.shape == second.shape:
        joined = jnp.concatenate([first, second], axis=0)
        return (lax.all_gather(joined, "mp", axis=0, tiled=True),)
    return tuple(lax.all_gather(part, "mp", axis=0, tiled=True) for part in (first, second))


def bit_of(step):
    axis, bit = step
    return (lax.axis_index(axis) // bit) % 2


def add_rounded(kept, received):
    return (kept.astype(f32) + received.astype(f32)).astype(kept.dtype)


def halve(array, step):
    half = array.shape[0] // 2
    mine = bit_of(step)
    kept = lax.dynamic_slice_in_dim(array, mine * half, half, 0)
    sent = lax.dynamic_slice_in_dim(array, (1 - mine) * half, half, 0)
    return kept, sent


def bits_of(axis):
    size = lax.axis_size(axis)
    return [(axis, 1 << place) for place in range(size.bit_length() - 1)]


def sum_of_cores(payload):
    core = bits_of("dp")[0]
    kept, sent = halve(payload, core)
    return add_rounded(kept, partner(sent, *core))


def sum_everywhere(total, beside):
    along_dp, along_mp = bits_of("dp"), bits_of("mp")
    core, along_z = along_dp[0], along_dp[1:]
    half_mp = len(along_mp) // 2
    inner, outer = along_mp[:half_mp], along_mp[half_mp:]
    near, far = along_z[:1], along_z[1:]
    orders = [inner + outer + near + far, outer + near + inner + far, near + inner + outer + far]
    unit = 1 << len(orders[0])
    units = total.shape[0] // unit
    sizes = [(units + 2 - index) // 3 * unit for index in range(3)]
    starts = [0, sizes[0], sizes[0] + sizes[1]]
    parts = [total[start : start + size] for start, size in zip(starts, sizes)]
    for level in range(len(orders[0])):
        steps = [order[level] for order in orders]
        halves = [halve(part, step) for part, step in zip(parts, steps)]
        received = [partner(half[1], *step) for half, step in zip(halves, steps)]
        received = lax.optimization_barrier(received)
        if level == 0:
            received, beside = lax.optimization_barrier((received, beside))
        parts = [add_rounded(half[0], other) for half, other in zip(halves, received)]
        parts = lax.optimization_barrier(parts)
    for level in reversed(range(len(orders[0]))):
        steps = [order[level] for order in orders]
        received = [partner(part, *step) for part, step in zip(parts, steps)]
        received = lax.optimization_barrier(received)
        parts = [
            jnp.where(
                bit_of(step) == 0,
                jnp.concatenate([part, other], axis=0),
                jnp.concatenate([other, part], axis=0),
            )
            for part, other, step in zip(parts, received, steps)
        ]
    mine = jnp.concatenate(parts, axis=0)
    return mine, partner(mine, *core), beside


def body(
    tokens,
    segments,
    routes,
    gain_attn,
    qkv_weight,
    out_weight,
    rel_bias,
    gain_ffn,
    router_weight,
    w_in,
    w_out,
    cotangent,
):
    tok_count, width = tokens.shape
    experts = w_in.shape[1] * lax.axis_size("dp")
    parts = lax.axis_size("mp")
    capacity = (tok_count * 9 + 8 * experts - 1) // (8 * experts)
    heads = width // HEAD_DIM

    weights = [gather_weights(w_in, w_out, layer) for layer in range(LAYERS)]
    onehot = window_onehot()
    windows = jnp.einsum("pb,lbh->lhp", onehot, rel_bias, precision=highest)
    chosen = routes[:, :, 0]
    chosen_onehot = (
        chosen[:, :, None] == jnp.arange(experts, dtype=jnp.int32)[None, None, :]
    ).astype(jnp.int32)
    slots = jnp.sum(jnp.cumsum(chosen_onehot, axis=1) * chosen_onehot, axis=-1) - 1
    rowid = (chosen ^ lax.axis_index("dp")) * capacity + slots
    common = dict(
        gain_attn=gain_attn,
        gain_ffn=gain_ffn,
        qkv_w=qkv_weight,
        out_w=out_weight,
        router=router_weight,
        windows=windows.reshape(LAYERS, heads, WINDOW_ROWS, SPAN),
        onehot=onehot,
        seg_row=segments.reshape(1, LEN),
        seg_col=segments.reshape(LEN, 1),
        rowrow=rowid[:, None, :],
        rowcol=rowid[:, :, None],
        route=routes,
        capacity=capacity,
    )

    states = []
    source = tokens
    for layer in range(LAYERS):
        results = list(attend(layer, source, common))
        state = dict(x=results.pop(0) if layer > 0 else tokens)
        for name in ("proj", "mixed", "lse", "middle", "prob"):
            state[name] = results.pop(0)
        state["rows"], outs = expert(swap(results), weights[layer], parts)
        state["back"] = swap(outs)
        states.append(state)
        source = state

    rows_all = [gather_rows(state["rows"]) for state in states]
    output, gate_grad, *blocks = turn(LAYERS - 1, states[-1], cotangent, common)
    gradient = cotangent
    totals = [None] * LAYERS
    order = jnp.arange(parts, dtype=jnp.int32)
    weight_grads = ()
    for layer in reversed(range(LAYERS)):
        last = layer == 0
        arrived = swap(blocks)
        if layer == LAYERS - 1:
            arrived, rows_all[0] = lax.optimization_barrier((arrived, rows_all[0]))
        else:
            arrived, weight_grads = lax.optimization_barrier((arrived, weight_grads))
        grads, sent = expert_back(states[layer]["rows"], arrived, weights[layer], parts)
        gback = swap(sent)
        if layer > 0:
            gback, rows_all[layer] = lax.optimization_barrier((gback, rows_all[layer]))
        grads_all = gather_rows(grads)
        results = attend_back(layer, states, gradient, gback, gate_grad, common)
        gradient, payload = results[:2]
        if layer > 0:
            gate_grad, *blocks = results[2:]
            totals[layer] = sum_of_cores(payload)
        else:
            payload, grads_all = lax.optimization_barrier((payload, grads_all))
            totals[layer] = sum_of_cores(payload)
            totals[layer], grads_all = lax.optimization_barrier((totals[layer], grads_all))
        weight_grads = weight_grad(
            layer, order, rows_all[layer], grads_all, w_in, w_out, tuple(weight_grads)
        )
    total = jnp.concatenate(totals, axis=1)
    mine, other, (grad_w_in, grad_w_out) = sum_everywhere(total, weight_grads)
    side = lax.axis_index("dp").astype(jnp.int32) % 2
    grad_qkv, grad_out = finish(side, mine, other)
    rows = jnp.where(side == 0, mine[2 * width :], other[2 * width :]).astype(f32)
    small = [rows[:, layer * width : (layer + 1) * width] for layer in range(LAYERS)]
    grad_gain_attn = jnp.stack([rows[experts] for rows in small])
    grad_gain_ffn = jnp.stack([rows[experts + 1] for rows in small])
    grad_router = jnp.stack([rows[:experts].T for rows in small])
    grad_rel = jnp.stack([rows[experts + 2 : experts + 2 + heads, :BUCKETS].T for rows in small])
    return (
        output,
        gradient,
        grad_gain_attn,
        grad_qkv,
        grad_out,
        grad_rel,
        grad_gain_ffn,
        grad_router,
        grad_w_in,
        grad_w_out,
    )


def solution(mesh):
    return jax.shard_map(
        body,
        mesh=mesh,
        in_specs=(
            P(("dp", "mp"), None),
            P(("dp", "mp"), None),
            P(None, ("dp", "mp"), None),
            P(),
            P(),
            P(),
            P(),
            P(),
            P(),
            P(None, "dp", None, "mp"),
            P(None, "dp", "mp", None),
            P(("dp", "mp"), None),
        ),
        out_specs=(
            P(("dp", "mp"), None),
            P(("dp", "mp"), None),
            P(),
            P(),
            P(),
            P(),
            P(),
            P(),
            P(None, "dp", None, "mp"),
            P(None, "dp", "mp", None),
        ),
        check_vma=False,
    )
```

time: 710 us -> 643 us (0.906)
  blocking collectives: 208 us -> 0 us
  starting transfers between devices: 10.6 us -> 111 us
  Pallas kernels: 188 us -> 219 us
  other arithmetic: 21 us -> 32.8 us
    all_to_all x6 -> x0, blocking collectives: 166 us -> none  [swap(): lax.all_to_all(split, 'dp', split_axis=0, concat_axis=0, tiled=True)]
    ppermute x0 -> x83, waiting for transfers between devices: none -> 156 us  [partner(): return lax.ppermute(array, axis, pairs)]
    ppermute x0 -> x83, starting transfers between devices: none -> 111 us  [partner(): return lax.ppermute(array, axis, pairs)]
    psum x1 -> x0, waiting for transfers between devices: 102 us -> none  [body(): big = lax.psum((gq, gk, gv, gout), ('dp', 'mp'))]
    psum x1 -> x0, blocking collectives: 41.9 us -> none  [body(): small = lax.psum([entry[1] for entry in per_layer], ('dp', 'mp'))]
    all_to_all x2 -> x0, waiting for transfers between devices: 39.8 us -> none  [swap(): lax.all_to_all(split, 'dp', split_axis=0, concat_axis=0, tiled=True)]
    pallas_call x11 -> x12, Pallas kernels: 188 us -> 219 us  [the longest x2 73.4 us: attend_back(): pl.pallas_call(lambda *refs: attend_back_kernel(layer, experts, refs), gr...]
    convert_element_type x0 -> x16, other arithmetic: none -> 16.4 us  [the longest x14 14.1 us: add_rounded(): return (kept.astype(f32) + received.astype(f32)).astype(kept.dtype)]
  transfers between devices with their start and end apart: 11 -> 89, of which waited for: 5 -> 27; matrix products, arithmetic and copies ran while one was open for 5% -> 4% of each run, Pallas kernels for 27% -> 30%
where the time goes in v2:
time: 643 us; the launch traced here: 638 us
  waiting for transfers between devices  236 us (37%)
  Pallas kernels  219 us (34%)
  starting transfers between devices  111 us (17%)
  other arithmetic  32.8 us (5%)
  local copies, waits for them, and re-layouts  22.8 us (4%)
  between operations  15.4 us (2%)
    ppermute x83, waiting for transfers between devices, partner(): return lax.ppermute(array, axis, pairs)  156 us
    ppermute x83, starting transfers between devices, partner(): return lax.ppermute(array, axis, pairs)  111 us
    all_gather x2, waiting for transfers between devices, gather_weights(): return (lax.all_gather(joined, 'mp', axis=0, tiled=True),)  80.4 us
    pallas_call x2, Pallas kernels, attend_back(): pl.pallas_call(lambda *refs: attend_back_kernel(layer, experts, refs), gr...  73.4 us
    pallas_call x2, Pallas kernels, attend(): pl.pallas_call(lambda *refs: attend_kernel(layer, experts, refs), grid=(g...  41.2 us
    pallas_call x2, Pallas kernels, weight_grad(): pl.pallas_call(weight_grad_kernel, grid_spec=grid_spec, out_shape=[jax.Sh...  38.9 us
    pallas_call x2, Pallas kernels, expert_back(): pl.pallas_call(lambda *refs: expert_back_kernel(experts, refs), grid=(par...  26.6 us
    pallas_call x2, Pallas kernels, expert(): pl.pallas_call(lambda *refs: expert_kernel(experts, refs), grid=(parts,),...  20.7 us
  transfers between devices with their start and end apart: 89, of which 27 were waited for; matrix products, arithmetic and copies ran while one was open for 4% of the time, Pallas kernels for 30%

profile of v2, /device:TPU:0, one launch (start us, length us, event | category | flops | bytes accessed | tf_op | source)
XLA Modules:
  0.0 638.2 jit_solution(13418053542849798222)
XLA Ops:
  7.2 2.6 slice_bitcast_fusion
  14.0 2.3 reduce-window.6
  22.1 20.0 %attend.2 = (bf16[3,512,768]{2,1,0:T(8,128)(2,1)}, bf16[512,768]{1,0:T(8,128)(2,1)}, f32[3,8,512]{2,1,0:T(8,128)}, f32[512,768]{1,0:T(8,128)}, f32[512,8]{1,0:T(...) custom-call(bf16[512,768]{1,0:T(8,128)(2,1)} %refs_16_.3, ...), custom_call_target="tpu_custom_call" | custom-call | flops 1000000 | bytes 1000000 | tf_op jit(solution)/shard_map/attend/pallas_call | solution.py:321
  42.5 2.5 collective-permute-start.1
  45.1 2.8 collective-permute-start.3
  47.9 3.6 collective-permute-start.5
  52.1 2.9 collective-permute-done.2.refs_3_
  55.0 8.6 %collective-permute-done.4.refs_5_ = bf16[72,768]{1,0:T(8,128)(2,1)S(1)} collective-permute-done((bf16[72,768]{1,0:T(8,128)(2,1)}, bf16[72,768]{1,0:T(8,128)(2,1)S(1)}, u32[]{:S(2)}, u32[]{:S(2)}) %collective-permute-start.4) | collective-permute-done | bytes 110624 | tf_op jit(solution)/shard_map/ppermute | solution.py:812
  63.6 47.1 %all-gather.7.cloned.1.call-done.refs_8_.refs_9_.refs_10_ = bf16[6144,768]{1,0:T(8,128)(2,1)} async-done(((bf16[1536,768]{1,0:T(8,128)(2,1)}), bf16[6144,768]{1,0:T(8,128)(2,1)}) %all-gather.7.cloned.1.call-update) | async-done | bytes 9437200 | tf_op jit(solution)/shard_map/all_gather | solution.py:827
  110.7 10.4 %expert.2 = (bf16[576,768]{1,0:T(8,128)(2,1)}, bf16[72,768]{1,0:T(8,128)(2,1)}, bf16[72,768]{1,0:T(8,128)(2,1)}, bf16[72,768]{1,0:T(8,128)(2,1)}, bf16[72,768]{1...) custom-call(bf16[72,768]{1,0:T(8,128)(2,1)} %get-tuple-element.177.r, ...), custom_call_target="tpu_custom_call" | custom-call | flops 1000000 | bytes 1000000 | tf_op jit(solution)/shard_map/expert/pallas_call | solution.py:653
  123.4 2.4 collective-permute-start.10
  126.0 3.3 collective-permute-start.12
  129.3 1.9 collective-permute-done.8.refs_6_.refs_35_
  133.1 8.4 %collective-permute-done.11.refs_9_.refs_38_ = bf16[72,768]{1,0:T(8,128)(2,1)S(1)} collective-permute-done((bf16[72,768]{1,0:T(8,128)(2,1)}, bf16[72,768]{1,0:T(8,128)(2,1)S(1)}, u32[]{:S(2)}, u32[]{:S(2)}) %collective-permute-start.11) | collective-permute-done | bytes 110624 | tf_op jit(solution)/shard_map/ppermute | solution.py:812
  142.2 21.2 %attend.3 = (f32[512,768]{1,0:T(8,128)}, bf16[3,512,768]{2,1,0:T(8,128)(2,1)}, bf16[512,768]{1,0:T(8,128)(2,1)}, f32[3,8,512]{2,1,0:T(8,128)}, f32[512,768]{1,0:...) custom-call(f32[512,768]{1,0:T(8,128)} %get-tuple-element.175.refs_0, ...), custom_call_target="tpu_custom_call" | custom-call | flops 1000000 | bytes 1000000 | tf_op jit(solution)/shard_map/attend/pallas_call | solution.py:321
  163.9 5.3 collective-permute-start.15
  169.2 3.2 collective-permute-start.17
  172.8 2.1 collective-permute-start.19
  176.1 33.3 %all-gather.9.cloned.1.call-done.refs_8_.refs_9_.refs_10_ = bf16[6144,768]{1,0:T(8,128)(2,1)} async-done(((bf16[1536,768]{1,0:T(8,128)(2,1)}), bf16[6144,768]{1,0:T(8,128)(2,1)}) %all-gather.9.cloned.1.call-update) | async-done | bytes 9437200 | tf_op jit(solution)/shard_map/all_gather | solution.py:827
  210.3 10.3 %expert.3 = (bf16[576,768]{1,0:T(8,128)(2,1)}, bf16[72,768]{1,0:T(8,128)(2,1)}, bf16[72,768]{1,0:T(8,128)(2,1)}, bf16[72,768]{1,0:T(8,128)(2,1)}, bf16[72,768]{1...) custom-call(bf16[72,768]{1,0:T(8,128)(2,1)} %get-tuple-element.195.r, ...), custom_call_target="tpu_custom_call" | custom-call | flops 1000000 | bytes 1000000 | tf_op jit(solution)/shard_map/expert/pallas_call | solution.py:653
  222.6 2.4 collective-permute-start.24
  225.2 3.3 collective-permute-start.26
  228.6 1.9 collective-permute-done.22.refs_8_
  232.4 8.4 %collective-permute-done.25.refs_11_ = bf16[72,768]{1,0:T(8,128)(2,1)S(1)} collective-permute-done((bf16[72,768]{1,0:T(8,128)(2,1)}, bf16[72,768]{1,0:T(8,128)(2,1)S(1)}, u32[]{:S(2)}, u32[]{:S(2)}) %collective-permute-start.25) | collective-permute-done | bytes 110624 | tf_op jit(solution)/shard_map/ppermute | solution.py:812
  241.5 4.8 turn.1
  246.6 5.3 collective-permute-start.29
  251.9 3.2 collective-permute-start.31
  255.5 2.1 collective-permute-start.33
  258.9 2.6 collective-permute-done.30.refs_4_
  261.4 9.1 %collective-permute-done.32.refs_6_ = bf16[72,768]{1,0:T(8,128)(2,1)S(1)} collective-permute-done((bf16[72,768]{1,0:T(8,128)(2,1)}, bf16[72,768]{1,0:T(8,128)(2,1)S(1)}, u32[]{:S(2)}, u32[]{:S(2)}) %collective-permute-start.32) | collective-permute-done | bytes 110624 | tf_op jit(solution)/shard_map/ppermute | solution.py:812
  271.3 13.3 %expert_back.2 = (bf16[576,768]{1,0:T(8,128)(2,1)}, bf16[72,768]{1,0:T(8,128)(2,1)}, bf16[72,768]{1,0:T(8,128)(2,1)}, bf16[72,768]{1,0:T(8,128)(2,1)}, bf16[72,7...) custom-call(bf16[576,768]{1,0:T(8,128)(2,1)} %get-tuple-element.213., ...), custom_call_target="tpu_custom_call" | custom-call | flops 1000000 | bytes 1000000 | tf_op jit(solution)/shard_map/expert_back/pallas_call | solution.py:695
  285.8 5.0 collective-permute-start.36
  290.8 2.1 collective-permute-start.38
  293.2 2.1 collective-permute-start.40
  298.3 2.0 collective-permute-done.37.refs_11_
  300.3 8.1 %collective-permute-done.39.refs_13_ = bf16[72,768]{1,0:T(8,128)(2,1)S(1)} collective-permute-done((bf16[72,768]{1,0:T(8,128)(2,1)}, bf16[72,768]{1,0:T(8,128)(2,1)S(1)}, u32[]{:S(2)}, u32[]{:S(2)}) %collective-permute-start.39) | collective-permute-done | bytes 110624 | tf_op jit(solution)/shard_map/ppermute | solution.py:812
  309.2 41.3 %attend_back.2 = (f32[512,768]{1,0:T(8,128)}, bf16[3328,768]{1,0:T(8,128)(2,1)}, f32[512,1]{1,0:T(8,128)}, bf16[72,768]{1,0:T(8,128)(2,1)}, bf16[72,768]{1,0:T(8...) custom-call(bf16[512,768]{1,0:T(8,128)(2,1)} %refs_0_.3, ...), custom_call_target="tpu_custom_call" | custom-call | flops 1000000 | bytes 1000000 | tf_op jit(solution)/shard_map/attend_back/pallas_call | solution.py:541
  351.1 4.6 collective-permute-start.43
  355.7 2.2 collective-permute-start.45
  358.2 2.1 collective-permute-start.47
  360.3 2.8 collective-permute-done.43.refs_3_
  363.6 19.4 %weight_grad.2 = (f32[2,1,768,768]{3,2,1,0:T(8,128)}, f32[2,1,768,768]{3,2,1,0:T(8,128)}) custom-call(s32[4]{0:T(128)} %iota.14.order, bf16[2304,768]{1,0:T(8,128)(2,1)} %all-gather.13.cloned.1.call-done.rows, bf16[2304,768]{1,0:T(8,128)(2,1)} %all-gather.15.cloned.1.call-done.grads, bf16[2,1,768,768]{3,2,1,0:T(8,128)(2,1)} %w_in.3, ...), custom_call_target="tpu_custom_call" | custom-call | flops 1000000 | bytes 1000000 | tf_op jit(solution)/shard_map/weight_grad/pallas_call | solution.py:747
  383.8 13.3 %expert_back.3 = (bf16[576,768]{1,0:T(8,128)(2,1)}, bf16[72,768]{1,0:T(8,128)(2,1)}, bf16[72,768]{1,0:T(8,128)(2,1)}, bf16[72,768]{1,0:T(8,128)(2,1)}, bf16[72,7...) custom-call(bf16[576,768]{1,0:T(8,128)(2,1)} %get-tuple-element.222., ...), custom_call_target="tpu_custom_call" | custom-call | flops 1000000 | bytes 1000000 | tf_op jit(solution)/shard_map/expert_back/pallas_call | solution.py:695
  397.2 2.0 constant_dynamic-slice_fusion.11
  405.6 3.8 collective-permute-done.50.refs_10_
  413.0 7.9 %collective-permute-done.53.refs_13_ = bf16[72,768]{1,0:T(8,128)(2,1)S(1)} collective-permute-done((bf16[72,768]{1,0:T(8,128)(2,1)S(1)}, bf16[72,768]{1,0:T(8,128)(2,1)S(1)}, u32[]{:S(2)}, u32[]{:S(2)}) %collective-permute-start.53) | collective-permute-done | bytes 110624 | tf_op jit(solution)/shard_map/ppermute | solution.py:812
  421.7 32.2 %attend_back.3 = (f32[512,768]{1,0:T(8,128)}, bf16[3328,768]{1,0:T(8,128)(2,1)}) custom-call(f32[512,768]{1,0:T(8,128)} %get-tuple-element.251.refs_0_, s32[2,512,1]{2,1,0:T(8,128)} %get-tuple-element.384.refs_2_.refs_3_.refs_1_.refs_30_, f32[512,1]{1,0:T(8,128)} %get-tuple-element.252.refs_2_, f32[512,8]{1,0:T(8,128)} %get-tuple-element.176.refs_1_.refs_31_.refs_3_, ...), custom_call_target="tpu_custom_call" | custom-call | flops 1000000 | bytes 1000000 | tf_op jit(solution)/shard_map/attend_back/pallas_call | solution.py:541
  453.9 3.4 constant_dynamic-slice_fusion.12
  457.4 3.3 add_convert_fusion
  462.4 2.4 add_convert_fusion.1
  469.3 4.6 collective-permute-start.60
  474.4 19.5 %weight_grad.3 = (f32[2,1,768,768]{3,2,1,0:T(8,128)}, f32[2,1,768,768]{3,2,1,0:T(8,128)}) custom-call(s32[4]{0:T(128)} %iota.15.order, bf16[2304,768]{1,0:T(8,128)(2,1)} %all-gather.11.cloned.1.call-done.rows, bf16[2304,768]{1,0:T(8,128)(2,1)} %all-gather.17.cloned.1.call-done.grads, ...), custom_call_target="tpu_custom_call", output_to_operand_aliasing={{0}: (5, {}), {1}: (6, {})} | custom-call | flops 1000000 | bytes 1000000 | tf_op jit(solution)/shard_map/weight_grad/pallas_call | solution.py:747
  503.0 9.4 %collective-permute-done.63 = bf16[136,1536]{1,0:T(8,128)(2,1)} collective-permute-done((bf16[136,1536]{1,0:T(8,128)(2,1)}, bf16[136,1536]{1,0:T(8,128)(2,1)}, u32[]{:S(2)}, u32[]{:S(2)}) %collective-permute-start.63) | collective-permute-done | bytes 417824 | tf_op jit(solution)/shard_map/ppermute | solution.py:812
  520.0 5.1 collective-permute-done.66
  530.1 11.1 %collective-permute-done.69 = bf16[34,1536]{1,0:T(8,128)(2,1)S(1)} collective-permute-done((bf16[34,1536]{1,0:T(8,128)(2,1)S(1)}, bf16[34,1536]{1,0:T(8,128)(2,1)S(1)}, u32[]{:S(2)}, u32[]{:S(2)}) %collective-permute-start.69) | collective-permute-done | bytes 104480 | tf_op jit(solution)/shard_map/ppermute | solution.py:812
  541.5 2.9 collective-permute-start.71
  544.5 15.2 %collective-permute-done.72 = bf16[34,1536]{1,0:T(8,128)(2,1)S(1)} collective-permute-done((bf16[34,1536]{1,0:T(8,128)(2,1)S(1)}, bf16[34,1536]{1,0:T(8,128)(2,1)S(1)}, u32[]{:S(2)}, u32[]{:S(2)}) %collective-permute-start.72) | collective-permute-done | bytes 104480 | tf_op jit(solution)/shard_map/ppermute | solution.py:812
  560.1 2.0 collective-permute-start.75
  562.2 5.2 collective-permute-done.75
  571.9 9.0 %collective-permute-done.78 = bf16[136,1536]{1,0:T(8,128)(2,1)S(1)} collective-permute-done((bf16[136,1536]{1,0:T(8,128)(2,1)S(1)}, bf16[136,1536]{1,0:T(8,128)(2,1)S(1)}, u32[]{:S(2)}, u32[]{:S(2)}) %collective-permute-start.78) | collective-permute-done | bytes 417824 | tf_op jit(solution)/shard_map/ppermute | solution.py:812
  584.3 16.3 %collective-permute-done.81 = bf16[272,1536]{1,0:T(8,128)(2,1)S(1)} collective-permute-done((bf16[272,1536]{1,0:T(8,128)(2,1)S(1)}, bf16[272,1536]{1,0:T(8,128)(2,1)S(1)}, u32[]{:S(2)}, u32[]{:S(2)}) %collective-permute-start.81) | collective-permute-done | bytes 835616 | tf_op jit(solution)/shard_map/ppermute | solution.py:812
  602.7 2.7 pad_maximum_fusion.first
  605.4 8.8 %collective-permute-done.82.second = bf16[1664,1536]{1,0:T(8,128)(2,1)} collective-permute-done((bf16[1664,1536]{1,0:T(8,128)(2,1)}, bf16[1664,1536]{1,0:T(8,128)(2,1)}, u32[]{:S(2)}, u32[]{:S(2)}) %collective-permute-start.82) | collective-permute-done | bytes 5111840 | tf_op jit(solution)/shard_map/ppermute | solution.py:812
  617.7 13.4 %finish.1 = (f32[2,768,2304]{2,1,0:T(8,128)}, f32[2,768,768]{2,1,0:T(8,128)}) custom-call(s32[1]{0:T(128)} %bitcast.11.side, bf16[1664,1536]{1,0:T(8,128)(2,1)} %pad_maximum_fusion.first, bf16[1664,1536]{1,0:T(8,128)(2,1)} %collective-permute-done.82.second), custom_call_target="tpu_custom_call" | custom-call | flops 1000000 | bytes 1000000 | tf_op jit(solution)/shard_map/finish/pallas_call | solution.py:797
  (359 shorter events, 87.1 us)
Async XLA Ops:
  7.2 103.5 %all-gather.7.cloned.1.call-start = ((), (), s32[]{:S(2)}) async-start(), calls=%async_computation | async-start | bytes 11796480 | tf_op jit(solution)/shard_map/all_gather | solution.py:827
  11.5 198.0 %all-gather.9.cloned.1.call-start = ((), (), s32[]{:S(2)}) async-start(), calls=%async_computation.1 | async-start | bytes 11796480 | tf_op jit(solution)/shard_map/all_gather | solution.py:827
  13.1 257.5 %all-gather.11.cloned.1.call-start = ((), (), s32[]{:S(2)}) async-start(), calls=%async_computation.2 | async-start | bytes 4423680 | tf_op jit(solution)/shard_map/all_gather | solution.py:820
  45.0 10.0 %collective-permute-start.2 = (bf16[72,768]{1,0:T(8,128)(2,1)}, bf16[72,768]{1,0:T(8,128)(2,1)S(1)}, u32[]{:S(2)}, u32[]{:S(2)}) collective-permute-start(bf16[72,768]{1,0:T(8,128)(2,1)} %get-tuple-element.180), channel_id=1, source_target_pairs={{0,12},{4,8},{8,4},{12,0},{16,28},{20,24},{24,20},{28,16},{1,13},{... | collective-permute-start | bytes 331784 | tf_op jit(solution)/shard_map/ppermute | solution.py:812
  45.1 9.9 %collective-permute-start.3 = (bf16[72,768]{1,0:T(8,128)(2,1)}, bf16[72,768]{1,0:T(8,128)(2,1)S(1)}, u32[]{:S(2)}, u32[]{:S(2)}) collective-permute-start(bf16[72,768]{1,0:T(8,128)(2,1)} %get-tuple-element.181), channel_id=1, source_target_pairs={{0,16},{4,20},{8,24},{12,28},{16,0},{20,4},{24,8},{28,12},{1,17},{... | collective-permute-start | bytes 331784 | tf_op jit(solution)/shard_map/ppermute | solution.py:812
  47.9 15.7 %collective-permute-start.4 = (bf16[72,768]{1,0:T(8,128)(2,1)}, bf16[72,768]{1,0:T(8,128)(2,1)S(1)}, u32[]{:S(2)}, u32[]{:S(2)}) collective-permute-start(bf16[72,768]{1,0:T(8,128)(2,1)} %get-tuple-element.182), channel_id=1, source_target_pairs={{0,20},{4,16},{8,28},{12,24},{16,4},{20,0},{24,12},{28,8},{1,21},{... | collective-permute-start | bytes 331784 | tf_op jit(solution)/shard_map/ppermute | solution.py:812
  47.9 15.7 %collective-permute-start.5 = (bf16[72,768]{1,0:T(8,128)(2,1)}, bf16[72,768]{1,0:T(8,128)(2,1)S(1)}, u32[]{:S(2)}, u32[]{:S(2)}) collective-permute-start(bf16[72,768]{1,0:T(8,128)(2,1)} %get-tuple-element.183), channel_id=1, source_target_pairs={{0,24},{4,28},{8,16},{12,20},{16,8},{20,12},{24,0},{28,4},{1,25},{... | collective-permute-start | bytes 331784 | tf_op jit(solution)/shard_map/ppermute | solution.py:812
  51.5 12.1 %collective-permute-start.6 = (bf16[72,768]{1,0:T(8,128)(2,1)}, bf16[72,768]{1,0:T(8,128)(2,1)S(1)}, u32[]{:S(2)}, u32[]{:S(2)}) collective-permute-start(bf16[72,768]{1,0:T(8,128)(2,1)} %get-tuple-element.184), channel_id=1, source_target_pairs={{0,28},{4,24},{8,20},{12,16},{16,12},{20,8},{24,4},{28,0},{1,29},{... | collective-permute-start | bytes 331784 | tf_op jit(solution)/shard_map/ppermute | solution.py:812
  121.1 187.3 %all-gather.13.cloned.1.call-start = ((), (), s32[]{:S(2)}) async-start(), calls=%async_computation.3 | async-start | bytes 4423680 | tf_op jit(solution)/shard_map/all_gather | solution.py:820
  123.1 10.0 %collective-permute-start.9 = (bf16[72,768]{1,0:T(8,128)(2,1)}, bf16[72,768]{1,0:T(8,128)(2,1)S(1)}, u32[]{:S(2)}, u32[]{:S(2)}) collective-permute-start(bf16[72,768]{1,0:T(8,128)(2,1)} %get-tuple-element.188), channel_id=1, source_target_pairs={{0,12},{4,8},{8,4},{12,0},{16,28},{20,24},{24,20},{28,16},{1,13},{... | collective-permute-start | bytes 331784 | tf_op jit(solution)/shard_map/ppermute | solution.py:812
  123.4 9.7 %collective-permute-start.10 = (bf16[72,768]{1,0:T(8,128)(2,1)}, bf16[72,768]{1,0:T(8,128)(2,1)S(1)}, u32[]{:S(2)}, u32[]{:S(2)}) collective-permute-start(bf16[72,768]{1,0:T(8,128)(2,1)} %get-tuple-element.189), channel_id=1, source_target_pairs={{0,16},{4,20},{8,24},{12,28},{16,0},{20,4},{24,8},{28,12},{1,17},{... | collective-permute-start | bytes 331784 | tf_op jit(solution)/shard_map/ppermute | solution.py:812
  125.8 15.7 %collective-permute-start.11 = (bf16[72,768]{1,0:T(8,128)(2,1)}, bf16[72,768]{1,0:T(8,128)(2,1)S(1)}, u32[]{:S(2)}, u32[]{:S(2)}) collective-permute-start(bf16[72,768]{1,0:T(8,128)(2,1)} %get-tuple-element.190), channel_id=1, source_target_pairs={{0,20},{4,16},{8,28},{12,24},{16,4},{20,0},{24,12},{28,8},{1,21},{... | collective-permute-start | bytes 331784 | tf_op jit(solution)/shard_map/ppermute | solution.py:812
  126.0 15.5 %collective-permute-start.12 = (bf16[72,768]{1,0:T(8,128)(2,1)}, bf16[72,768]{1,0:T(8,128)(2,1)S(1)}, u32[]{:S(2)}, u32[]{:S(2)}) collective-permute-start(bf16[72,768]{1,0:T(8,128)(2,1)} %get-tuple-element.191), channel_id=1, source_target_pairs={{0,24},{4,28},{8,16},{12,20},{16,8},{20,12},{24,0},{28,4},{1,25},{... | collective-permute-start | bytes 331784 | tf_op jit(solution)/shard_map/ppermute | solution.py:812
  131.2 10.3 %collective-permute-start.13 = (bf16[72,768]{1,0:T(8,128)(2,1)}, bf16[72,768]{1,0:T(8,128)(2,1)S(1)}, u32[]{:S(2)}, u32[]{:S(2)}) collective-permute-start(bf16[72,768]{1,0:T(8,128)(2,1)} %get-tuple-element.192), channel_id=1, source_target_pairs={{0,28},{4,24},{8,20},{12,16},{16,12},{20,8},{24,4},{28,0},{1,29},{... | collective-permute-start | bytes 331784 | tf_op jit(solution)/shard_map/ppermute | solution.py:812
  163.9 11.0 %collective-permute-start.15 = (bf16[72,768]{1,0:T(8,128)(2,1)}, bf16[72,768]{1,0:T(8,128)(2,1)S(1)}, u32[]{:S(2)}, u32[]{:S(2)}) collective-permute-start(bf16[72,768]{1,0:T(8,128)(2,1)} %get-tuple-element.197), channel_id=1, source_target_pairs={{0,8},{4,12},{8,0},{12,4},{16,24},{20,28},{24,16},{28,20},{1,9},{5... | collective-permute-start | bytes 331784 | tf_op jit(solution)/shard_map/ppermute | solution.py:812
  169.2 40.2 %collective-permute-start.16 = (bf16[72,768]{1,0:T(8,128)(2,1)}, bf16[72,768]{1,0:T(8,128)(2,1)S(1)}, u32[]{:S(2)}, u32[]{:S(2)}) collective-permute-start(bf16[72,768]{1,0:T(8,128)(2,1)} %get-tuple-element.198), channel_id=1, source_target_pairs={{0,12},{4,8},{8,4},{12,0},{16,28},{20,24},{24,20},{28,16},{1,13},{... | collective-permute-start | bytes 331784 | tf_op jit(solution)/shard_map/ppermute | solution.py:812
  169.2 40.2 %collective-permute-start.17 = (bf16[72,768]{1,0:T(8,128)(2,1)}, bf16[72,768]{1,0:T(8,128)(2,1)S(1)}, u32[]{:S(2)}, u32[]{:S(2)}) collective-permute-start(bf16[72,768]{1,0:T(8,128)(2,1)} %get-tuple-element.199), channel_id=1, source_target_pairs={{0,16},{4,20},{8,24},{12,28},{16,0},{20,4},{24,8},{28,12},{1,17},{... | collective-permute-start | bytes 331784 | tf_op jit(solution)/shard_map/ppermute | solution.py:812
  172.5 37.0 %collective-permute-start.18 = (bf16[72,768]{1,0:T(8,128)(2,1)}, bf16[72,768]{1,0:T(8,128)(2,1)S(1)}, u32[]{:S(2)}, u32[]{:S(2)}) collective-permute-start(bf16[72,768]{1,0:T(8,128)(2,1)} %get-tuple-element.200), channel_id=1, source_target_pairs={{0,20},{4,16},{8,28},{12,24},{16,4},{20,0},{24,12},{28,8},{1,21},{... | collective-permute-start | bytes 331784 | tf_op jit(solution)/shard_map/ppermute | solution.py:812
  172.8 36.6 %collective-permute-start.19 = (bf16[72,768]{1,0:T(8,128)(2,1)}, bf16[72,768]{1,0:T(8,128)(2,1)S(1)}, u32[]{:S(2)}, u32[]{:S(2)}) collective-permute-start(bf16[72,768]{1,0:T(8,128)(2,1)} %get-tuple-element.201), channel_id=1, source_target_pairs={{0,24},{4,28},{8,16},{12,20},{16,8},{20,12},{24,0},{28,4},{1,25},{... | collective-permute-start | bytes 331784 | tf_op jit(solution)/shard_map/ppermute | solution.py:812
  174.9 34.6 %collective-permute-start.20 = (bf16[72,768]{1,0:T(8,128)(2,1)}, bf16[72,768]{1,0:T(8,128)(2,1)S(1)}, u32[]{:S(2)}, u32[]{:S(2)}) collective-permute-start(bf16[72,768]{1,0:T(8,128)(2,1)} %get-tuple-element.202), channel_id=1, source_target_pairs={{0,28},{4,24},{8,20},{12,16},{16,12},{20,8},{24,4},{28,0},{1,29},{... | collective-permute-start | bytes 331784 | tf_op jit(solution)/shard_map/ppermute | solution.py:812
  220.6 142.4 %all-gather.15.cloned.1.call-start = ((), (), s32[]{:S(2)}) async-start(), calls=%async_computation.4 | async-start | bytes 4423680 | tf_op jit(solution)/shard_map/all_gather | solution.py:820
  220.8 9.7 %collective-permute-start.22 = (bf16[72,768]{1,0:T(8,128)(2,1)}, bf16[72,768]{1,0:T(8,128)(2,1)S(1)}, u32[]{:S(2)}, u32[]{:S(2)}) collective-permute-start(bf16[72,768]{1,0:T(8,128)(2,1)} %get-tuple-element.205), channel_id=1, source_target_pairs={{0,8},{4,12},{8,0},{12,4},{16,24},{20,28},{24,16},{28,20},{1,9},{5... | collective-permute-start | bytes 331784 | tf_op jit(solution)/shard_map/ppermute | solution.py:812
  222.3 10.0 %collective-permute-start.23 = (bf16[72,768]{1,0:T(8,128)(2,1)}, bf16[72,768]{1,0:T(8,128)(2,1)S(1)}, u32[]{:S(2)}, u32[]{:S(2)}) collective-permute-start(bf16[72,768]{1,0:T(8,128)(2,1)} %get-tuple-element.206), channel_id=1, source_target_pairs={{0,12},{4,8},{8,4},{12,0},{16,28},{20,24},{24,20},{28,16},{1,13},{... | collective-permute-start | bytes 331784 | tf_op jit(solution)/shard_map/ppermute | solution.py:812
  222.6 9.7 %collective-permute-start.24 = (bf16[72,768]{1,0:T(8,128)(2,1)}, bf16[72,768]{1,0:T(8,128)(2,1)S(1)}, u32[]{:S(2)}, u32[]{:S(2)}) collective-permute-start(bf16[72,768]{1,0:T(8,128)(2,1)} %get-tuple-element.207), channel_id=1, source_target_pairs={{0,16},{4,20},{8,24},{12,28},{16,0},{20,4},{24,8},{28,12},{1,17},{... | collective-permute-start | bytes 331784 | tf_op jit(solution)/shard_map/ppermute | solution.py:812
  225.0 15.7 %collective-permute-start.25 = (bf16[72,768]{1,0:T(8,128)(2,1)}, bf16[72,768]{1,0:T(8,128)(2,1)S(1)}, u32[]{:S(2)}, u32[]{:S(2)}) collective-permute-start(bf16[72,768]{1,0:T(8,128)(2,1)} %get-tuple-element.208), channel_id=1, source_target_pairs={{0,20},{4,16},{8,28},{12,24},{16,4},{20,0},{24,12},{28,8},{1,21},{... | collective-permute-start | bytes 331784 | tf_op jit(solution)/shard_map/ppermute | solution.py:812
  225.2 15.5 %collective-permute-start.26 = (bf16[72,768]{1,0:T(8,128)(2,1)}, bf16[72,768]{1,0:T(8,128)(2,1)S(1)}, u32[]{:S(2)}, u32[]{:S(2)}) collective-permute-start(bf16[72,768]{1,0:T(8,128)(2,1)} %get-tuple-element.209), channel_id=1, source_target_pairs={{0,24},{4,28},{8,16},{12,20},{16,8},{20,12},{24,0},{28,4},{1,25},{... | collective-permute-start | bytes 331784 | tf_op jit(solution)/shard_map/ppermute | solution.py:812
  230.5 10.3 %collective-permute-start.27 = (bf16[72,768]{1,0:T(8,128)(2,1)}, bf16[72,768]{1,0:T(8,128)(2,1)S(1)}, u32[]{:S(2)}, u32[]{:S(2)}) collective-permute-start(bf16[72,768]{1,0:T(8,128)(2,1)} %get-tuple-element.210), channel_id=1, source_target_pairs={{0,28},{4,24},{8,20},{12,16},{16,12},{20,8},{24,4},{28,0},{1,29},{... | collective-permute-start | bytes 331784 | tf_op jit(solution)/shard_map/ppermute | solution.py:812
  246.6 11.0 %collective-permute-start.29 = (bf16[72,768]{1,0:T(8,128)(2,1)}, bf16[72,768]{1,0:T(8,128)(2,1)S(1)}, u32[]{:S(2)}, u32[]{:S(2)}) collective-permute-start(bf16[72,768]{1,0:T(8,128)(2,1)} %get-tuple-element.216), channel_id=1, source_target_pairs={{0,8},{4,12},{8,0},{12,4},{16,24},{20,28},{24,16},{28,20},{1,9},{5... | collective-permute-start | bytes 331784 | tf_op jit(solution)/shard_map/ppermute | solution.py:812
  255.2 15.4 %collective-permute-start.32 = (bf16[72,768]{1,0:T(8,128)(2,1)}, bf16[72,768]{1,0:T(8,128)(2,1)S(1)}, u32[]{:S(2)}, u32[]{:S(2)}) collective-permute-start(bf16[72,768]{1,0:T(8,128)(2,1)} %get-tuple-element.219), channel_id=1, source_target_pairs={{0,20},{4,16},{8,28},{12,24},{16,4},{20,0},{24,12},{28,8},{1,21},{... | collective-permute-start | bytes 331784 | tf_op jit(solution)/shard_map/ppermute | solution.py:812
  255.5 15.0 %collective-permute-start.33 = (bf16[72,768]{1,0:T(8,128)(2,1)}, bf16[72,768]{1,0:T(8,128)(2,1)S(1)}, u32[]{:S(2)}, u32[]{:S(2)}) collective-permute-start(bf16[72,768]{1,0:T(8,128)(2,1)} %get-tuple-element.220), channel_id=1, source_target_pairs={{0,24},{4,28},{8,16},{12,20},{16,8},{20,12},{24,0},{28,4},{1,25},{... | collective-permute-start | bytes 331784 | tf_op jit(solution)/shard_map/ppermute | solution.py:812
  257.6 13.0 %collective-permute-start.34 = (bf16[72,768]{1,0:T(8,128)(2,1)}, bf16[72,768]{1,0:T(8,128)(2,1)S(1)}, u32[]{:S(2)}, u32[]{:S(2)}) collective-permute-start(bf16[72,768]{1,0:T(8,128)(2,1)} %get-tuple-element.221), channel_id=1, source_target_pairs={{0,28},{4,24},{8,20},{12,16},{16,12},{20,8},{24,4},{28,0},{1,29},{... | collective-permute-start | bytes 331784 | tf_op jit(solution)/shard_map/ppermute | solution.py:812
  284.6 169.2 %all-gather.17.cloned.1.call-start = ((), (), s32[]{:S(2)}) async-start(), calls=%async_computation.5 | async-start | bytes 4423680 | tf_op jit(solution)/shard_map/all_gather | solution.py:820
  292.9 15.6 %collective-permute-start.39 = (bf16[72,768]{1,0:T(8,128)(2,1)}, bf16[72,768]{1,0:T(8,128)(2,1)S(1)}, u32[]{:S(2)}, u32[]{:S(2)}) collective-permute-start(bf16[72,768]{1,0:T(8,128)(2,1)} %get-tuple-element.236), channel_id=1, source_target_pairs={{0,20},{4,16},{8,28},{12,24},{16,4},{20,0},{24,12},{28,8},{1,21},{... | collective-permute-start | bytes 331784 | tf_op jit(solution)/shard_map/ppermute | solution.py:812
  293.2 15.2 %collective-permute-start.40 = (bf16[72,768]{1,0:T(8,128)(2,1)}, bf16[72,768]{1,0:T(8,128)(2,1)S(1)}, u32[]{:S(2)}, u32[]{:S(2)}) collective-permute-start(bf16[72,768]{1,0:T(8,128)(2,1)} %get-tuple-element.237), channel_id=1, source_target_pairs={{0,24},{4,28},{8,16},{12,20},{16,8},{20,12},{24,0},{28,4},{1,25},{... | collective-permute-start | bytes 331784 | tf_op jit(solution)/shard_map/ppermute | solution.py:812
  295.3 13.1 %collective-permute-start.41 = (bf16[72,768]{1,0:T(8,128)(2,1)}, bf16[72,768]{1,0:T(8,128)(2,1)S(1)}, u32[]{:S(2)}, u32[]{:S(2)}) collective-permute-start(bf16[72,768]{1,0:T(8,128)(2,1)} %get-tuple-element.238), channel_id=1, source_target_pairs={{0,28},{4,24},{8,20},{12,16},{16,12},{20,8},{24,4},{28,0},{1,29},{... | collective-permute-start | bytes 331784 | tf_op jit(solution)/shard_map/ppermute | solution.py:812
  351.1 11.9 %collective-permute-start.43 = (bf16[72,768]{1,0:T(8,128)(2,1)}, bf16[72,768]{1,0:T(8,128)(2,1)S(1)}, u32[]{:S(2)}, u32[]{:S(2)}) collective-permute-start(bf16[72,768]{1,0:T(8,128)(2,1)} %get-tuple-element.255), channel_id=1, source_target_pairs={{0,8},{4,12},{8,0},{12,4},{16,24},{20,28},{24,16},{28,20},{1,9},{5... | collective-permute-start | bytes 331784 | tf_op jit(solution)/shard_map/ppermute | solution.py:812
  355.7 27.3 %collective-permute-start.44 = (bf16[72,768]{1,0:T(8,128)(2,1)}, bf16[72,768]{1,0:T(8,128)(2,1)S(1)}, u32[]{:S(2)}, u32[]{:S(2)}) collective-permute-start(bf16[72,768]{1,0:T(8,128)(2,1)} %get-tuple-element.256), channel_id=1, source_target_pairs={{0,12},{4,8},{8,4},{12,0},{16,28},{20,24},{24,20},{28,16},{1,13},{... | collective-permute-start | bytes 331784 | tf_op jit(solution)/shard_map/ppermute | solution.py:812
  355.7 27.3 %collective-permute-start.45 = (bf16[72,768]{1,0:T(8,128)(2,1)}, bf16[72,768]{1,0:T(8,128)(2,1)S(1)}, u32[]{:S(2)}, u32[]{:S(2)}) collective-permute-start(bf16[72,768]{1,0:T(8,128)(2,1)} %get-tuple-element.257), channel_id=1, source_target_pairs={{0,16},{4,20},{8,24},{12,28},{16,0},{20,4},{24,8},{28,12},{1,17},{... | collective-permute-start | bytes 331784 | tf_op jit(solution)/shard_map/ppermute | solution.py:812
  357.9 25.1 %collective-permute-start.46 = (bf16[72,768]{1,0:T(8,128)(2,1)}, bf16[72,768]{1,0:T(8,128)(2,1)S(1)}, u32[]{:S(2)}, u32[]{:S(2)}) collective-permute-start(bf16[72,768]{1,0:T(8,128)(2,1)} %get-tuple-element.258), channel_id=1, source_target_pairs={{0,20},{4,16},{8,28},{12,24},{16,4},{20,0},{24,12},{28,8},{1,21},{... | collective-permute-start | bytes 331784 | tf_op jit(solution)/shard_map/ppermute | solution.py:812
  358.2 24.9 %collective-permute-start.47 = (bf16[72,768]{1,0:T(8,128)(2,1)}, bf16[72,768]{1,0:T(8,128)(2,1)S(1)}, u32[]{:S(2)}, u32[]{:S(2)}) collective-permute-start(bf16[72,768]{1,0:T(8,128)(2,1)} %get-tuple-element.259), channel_id=1, source_target_pairs={{0,24},{4,28},{8,16},{12,20},{16,8},{20,12},{24,0},{28,4},{1,25},{... | collective-permute-start | bytes 331784 | tf_op jit(solution)/shard_map/ppermute | solution.py:812
  363.0 20.0 %collective-permute-start.48 = (bf16[72,768]{1,0:T(8,128)(2,1)}, bf16[72,768]{1,0:T(8,128)(2,1)S(1)}, u32[]{:S(2)}, u32[]{:S(2)}) collective-permute-start(bf16[72,768]{1,0:T(8,128)(2,1)} %get-tuple-element.260), channel_id=1, source_target_pairs={{0,28},{4,24},{8,20},{12,16},{16,12},{20,8},{24,4},{28,0},{1,29},{... | collective-permute-start | bytes 331784 | tf_op jit(solution)/shard_map/ppermute | solution.py:812
  399.2 58.2 %collective-permute-start.57 = (bf16[1664,768]{1,0:T(8,128)(2,1)S(1)}, bf16[1664,768]{1,0:T(8,128)(2,1)}, u32[]{:S(2)}, u32[]{:S(2)}) collective-permute-start(bf16[1664,768]{1,0:T(8,128)(2,1)S(1)} %constant_dynamic-slice_fusion.11), channel_id=1, source_target_pairs={{0,4},{4,0},{8,12},{12,8},{16,20},{20,16},{24,28},{28,24},{1,5},{5... | collective-permute-start | bytes 7667720 | tf_op jit(solution)/shard_map/ppermute | solution.py:812
  401.2 9.9 %collective-permute-start.51 = (bf16[72,768]{1,0:T(8,128)(2,1)S(1)}, bf16[72,768]{1,0:T(8,128)(2,1)S(1)}, u32[]{:S(2)}, u32[]{:S(2)}) collective-permute-start(bf16[72,768]{1,0:T(8,128)(2,1)S(1)} %copy-done.74), channel_id=1, source_target_pairs={{0,12},{4,8},{8,4},{12,0},{16,28},{20,24},{24,20},{28,16},{1,13},{... | collective-permute-start | bytes 331784 | tf_op jit(solution)/shard_map/ppermute | solution.py:812
  402.9 10.1 %collective-permute-start.52 = (bf16[72,768]{1,0:T(8,128)(2,1)S(1)}, bf16[72,768]{1,0:T(8,128)(2,1)S(1)}, u32[]{:S(2)}, u32[]{:S(2)}) collective-permute-start(bf16[72,768]{1,0:T(8,128)(2,1)S(1)} %copy-done.73), channel_id=1, source_target_pairs={{0,16},{4,20},{8,24},{12,28},{16,0},{20,4},{24,8},{28,12},{1,17},{... | collective-permute-start | bytes 331784 | tf_op jit(solution)/shard_map/ppermute | solution.py:812
  405.5 15.4 %collective-permute-start.53 = (bf16[72,768]{1,0:T(8,128)(2,1)S(1)}, bf16[72,768]{1,0:T(8,128)(2,1)S(1)}, u32[]{:S(2)}, u32[]{:S(2)}) collective-permute-start(bf16[72,768]{1,0:T(8,128)(2,1)S(1)} %copy-done.72), channel_id=1, source_target_pairs={{0,20},{4,16},{8,28},{12,24},{16,4},{20,0},{24,12},{28,8},{1,21},{... | collective-permute-start | bytes 331784 | tf_op jit(solution)/shard_map/ppermute | solution.py:812
  409.4 11.5 %collective-permute-start.54 = (bf16[72,768]{1,0:T(8,128)(2,1)S(1)}, bf16[72,768]{1,0:T(8,128)(2,1)S(1)}, u32[]{:S(2)}, u32[]{:S(2)}) collective-permute-start(bf16[72,768]{1,0:T(8,128)(2,1)S(1)} %copy-done.71), channel_id=1, source_target_pairs={{0,24},{4,28},{8,16},{12,20},{16,8},{20,12},{24,0},{28,4},{1,25},{... | collective-permute-start | bytes 331784 | tf_op jit(solution)/shard_map/ppermute | solution.py:812
  411.1 9.8 %collective-permute-start.55 = (bf16[72,768]{1,0:T(8,128)(2,1)S(1)}, bf16[72,768]{1,0:T(8,128)(2,1)S(1)}, u32[]{:S(2)}, u32[]{:S(2)}) collective-permute-start(bf16[72,768]{1,0:T(8,128)(2,1)S(1)} %copy-done.70), channel_id=1, source_target_pairs={{0,28},{4,24},{8,20},{12,16},{16,12},{20,8},{24,4},{28,0},{1,29},{... | collective-permute-start | bytes 331784 | tf_op jit(solution)/shard_map/ppermute | solution.py:812
  465.2 28.7 %collective-permute-start.58 = (bf16[280,1536]{1,0:T(8,128)(2,1)S(1)}, bf16[280,1536]{1,0:T(8,128)(2,1)}, u32[]{:S(2)}, u32[]{:S(2)}) collective-permute-start(bf16[280,1536]{1,0:T(8,128)(2,1)S(1)} %constant_dynamic-slice_fusion.10), channel_id=1, source_target_pairs={{0,1},{1,0},{2,3},{3,2},{4,5},{5,4},{6,7},{7,6},{8,9},{9,8},{10,11... | collective-permute-start | bytes 2580488 | tf_op jit(solution)/shard_map/ppermute | solution.py:812
  467.0 27.0 %collective-permute-start.59 = (bf16[280,1536]{1,0:T(8,128)(2,1)}, bf16[280,1536]{1,0:T(8,128)(2,1)}, u32[]{:S(2)}, u32[]{:S(2)}) collective-permute-start(bf16[280,1536]{1,0:T(8,128)(2,1)} %constant_dynamic-slice_fusion.9), channel_id=1, source_target_pairs={{0,2},{1,3},{2,0},{3,1},{4,6},{5,7},{6,4},{7,5},{8,10},{9,11},{10,... | collective-permute-start | bytes 2580488 | tf_op jit(solution)/shard_map/ppermute | solution.py:812
  469.3 24.6 %collective-permute-start.60 = (bf16[272,1536]{1,0:T(8,128)(2,1)}, bf16[272,1536]{1,0:T(8,128)(2,1)}, u32[]{:S(2)}, u32[]{:S(2)}) collective-permute-start(bf16[272,1536]{1,0:T(8,128)(2,1)} %fusion.6), channel_id=1, source_target_pairs={{0,8},{4,12},{8,0},{12,4},{16,24},{20,28},{24,16},{28,20},{1,9},{5... | collective-permute-start | bytes 2506760 | tf_op jit(solution)/shard_map/ppermute | solution.py:812
  498.9 13.5 %collective-permute-start.62 = (bf16[140,1536]{1,0:T(8,128)(2,1)S(1)}, bf16[140,1536]{1,0:T(8,128)(2,1)}, u32[]{:S(2)}, u32[]{:S(2)}) collective-permute-start(bf16[140,1536]{1,0:T(8,128)(2,1)S(1)} %constant_dynamic-slice_fusion.7), channel_id=1, source_target_pairs={{0,8},{4,12},{8,0},{12,4},{16,24},{20,28},{24,16},{28,20},{1,9},{5... | collective-permute-start | bytes 1290248 | tf_op jit(solution)/shard_map/ppermute | solution.py:812
  500.2 12.2 %collective-permute-start.61 = (bf16[140,1536]{1,0:T(8,128)(2,1)}, bf16[140,1536]{1,0:T(8,128)(2,1)}, u32[]{:S(2)}, u32[]{:S(2)}) collective-permute-start(bf16[140,1536]{1,0:T(8,128)(2,1)} %constant_dynamic-slice_fusion.8), channel_id=1, source_target_pairs={{0,2},{1,3},{2,0},{3,1},{4,6},{5,7},{6,4},{7,5},{8,10},{9,11},{10,... | collective-permute-start | bytes 1290248 | tf_op jit(solution)/shard_map/ppermute | solution.py:812
  501.8 10.6 %collective-permute-start.63 = (bf16[136,1536]{1,0:T(8,128)(2,1)}, bf16[136,1536]{1,0:T(8,128)(2,1)}, u32[]{:S(2)}, u32[]{:S(2)}) collective-permute-start(bf16[136,1536]{1,0:T(8,128)(2,1)} %constant_dynamic-slice_fusion.6), channel_id=1, source_target_pairs={{0,1},{1,0},{2,3},{3,2},{4,5},{5,4},{6,7},{7,6},{8,9},{9,8},{10,11... | collective-permute-start | bytes 1253384 | tf_op jit(solution)/shard_map/ppermute | solution.py:812
  525.5 15.8 %collective-permute-start.68 = (bf16[35,1536]{1,0:T(8,128)(2,1)S(1)}, bf16[35,1536]{1,0:T(8,128)(2,1)S(1)}, u32[]{:S(2)}, u32[]{:S(2)}) collective-permute-start(bf16[35,1536]{1,0:T(8,128)(2,1)S(1)} %constant_dynamic-slice_fusion.1), channel_id=1, source_target_pairs={{0,16},{4,20},{8,24},{12,28},{16,0},{20,4},{24,8},{28,12},{1,17},{... | collective-permute-start | bytes 322568 | tf_op jit(solution)/shard_map/ppermute | solution.py:812
  527.1 14.2 %collective-permute-start.67 = (bf16[35,1536]{1,0:T(8,128)(2,1)S(1)}, bf16[35,1536]{1,0:T(8,128)(2,1)S(1)}, u32[]{:S(2)}, u32[]{:S(2)}) collective-permute-start(bf16[35,1536]{1,0:T(8,128)(2,1)S(1)} %constant_dynamic-slice_fusion.2), channel_id=1, source_target_pairs={{0,16},{4,20},{8,24},{12,28},{16,0},{20,4},{24,8},{28,12},{1,17},{... | collective-permute-start | bytes 322568 | tf_op jit(solution)/shard_map/ppermute | solution.py:812
  528.5 12.7 %collective-permute-start.69 = (bf16[34,1536]{1,0:T(8,128)(2,1)S(1)}, bf16[34,1536]{1,0:T(8,128)(2,1)S(1)}, u32[]{:S(2)}, u32[]{:S(2)}) collective-permute-start(bf16[34,1536]{1,0:T(8,128)(2,1)S(1)} %constant_dynamic-slice_fusion), channel_id=1, source_target_pairs={{0,16},{4,20},{8,24},{12,28},{16,0},{20,4},{24,8},{28,12},{1,17},{... | collective-permute-start | bytes 313352 | tf_op jit(solution)/shard_map/ppermute | solution.py:812
  541.4 18.3 %collective-permute-start.70 = (bf16[35,1536]{1,0:T(8,128)(2,1)S(1)}, bf16[35,1536]{1,0:T(8,128)(2,1)S(1)}, u32[]{:S(2)}, u32[]{:S(2)}) collective-permute-start(bf16[35,1536]{1,0:T(8,128)(2,1)S(1)} %add_convert_fusion.13), channel_id=1, source_target_pairs={{0,16},{4,20},{8,24},{12,28},{16,0},{20,4},{24,8},{28,12},{1,17},{... | collective-permute-start | bytes 322568 | tf_op jit(solution)/shard_map/ppermute | solution.py:812
  541.5 18.2 %collective-permute-start.71 = (bf16[35,1536]{1,0:T(8,128)(2,1)S(1)}, bf16[35,1536]{1,0:T(8,128)(2,1)S(1)}, u32[]{:S(2)}, u32[]{:S(2)}) collective-permute-start(bf16[35,1536]{1,0:T(8,128)(2,1)S(1)} %add_convert_fusion.12), channel_id=1, source_target_pairs={{0,16},{4,20},{8,24},{12,28},{16,0},{20,4},{24,8},{28,12},{1,17},{... | collective-permute-start | bytes 322568 | tf_op jit(solution)/shard_map/ppermute | solution.py:812
  544.4 15.3 %collective-permute-start.72 = (bf16[34,1536]{1,0:T(8,128)(2,1)S(1)}, bf16[34,1536]{1,0:T(8,128)(2,1)S(1)}, u32[]{:S(2)}, u32[]{:S(2)}) collective-permute-start(bf16[34,1536]{1,0:T(8,128)(2,1)S(1)} %add_convert_fusion.11), channel_id=1, source_target_pairs={{0,16},{4,20},{8,24},{12,28},{16,0},{20,4},{24,8},{28,12},{1,17},{... | collective-permute-start | bytes 313352 | tf_op jit(solution)/shard_map/ppermute | solution.py:812
  567.6 13.3 %collective-permute-start.77 = (bf16[140,1536]{1,0:T(8,128)(2,1)S(1)}, bf16[140,1536]{1,0:T(8,128)(2,1)S(1)}, u32[]{:S(2)}, u32[]{:S(2)}) collective-permute-start(bf16[140,1536]{1,0:T(8,128)(2,1)S(1)} %maximum_select_fusion.7), channel_id=1, source_target_pairs={{0,8},{4,12},{8,0},{12,4},{16,24},{20,28},{24,16},{28,20},{1,9},{5... | collective-permute-start | bytes 1290248 | tf_op jit(solution)/shard_map/ppermute | solution.py:812
  569.5 11.4 %collective-permute-start.76 = (bf16[140,1536]{1,0:T(8,128)(2,1)S(1)}, bf16[140,1536]{1,0:T(8,128)(2,1)S(1)}, u32[]{:S(2)}, u32[]{:S(2)}) collective-permute-start(bf16[140,1536]{1,0:T(8,128)(2,1)S(1)} %maximum_select_fusion.6), channel_id=1, source_target_pairs={{0,2},{1,3},{2,0},{3,1},{4,6},{5,7},{6,4},{7,5},{8,10},{9,11},{10,... | collective-permute-start | bytes 1290248 | tf_op jit(solution)/shard_map/ppermute | solution.py:812
  581.5 19.1 %collective-permute-start.80 = (bf16[280,1536]{1,0:T(8,128)(2,1)S(1)}, bf16[280,1536]{1,0:T(8,128)(2,1)S(1)}, u32[]{:S(2)}, u32[]{:S(2)}) collective-permute-start(bf16[280,1536]{1,0:T(8,128)(2,1)S(1)} %maximum_select_fusion.4), channel_id=1, source_target_pairs={{0,2},{1,3},{2,0},{3,1},{4,6},{5,7},{6,4},{7,5},{8,10},{9,11},{10,... | collective-permute-start | bytes 2580488 | tf_op jit(solution)/shard_map/ppermute | solution.py:812
  582.1 18.5 %collective-permute-start.79 = (bf16[280,1536]{1,0:T(8,128)(2,1)S(1)}, bf16[280,1536]{1,0:T(8,128)(2,1)S(1)}, u32[]{:S(2)}, u32[]{:S(2)}) collective-permute-start(bf16[280,1536]{1,0:T(8,128)(2,1)S(1)} %maximum_select_fusion.3), channel_id=1, source_target_pairs={{0,1},{1,0},{2,3},{3,2},{4,5},{5,4},{6,7},{7,6},{8,9},{9,8},{10,11... | collective-permute-start | bytes 2580488 | tf_op jit(solution)/shard_map/ppermute | solution.py:812
  583.7 16.9 %collective-permute-start.81 = (bf16[272,1536]{1,0:T(8,128)(2,1)S(1)}, bf16[272,1536]{1,0:T(8,128)(2,1)S(1)}, u32[]{:S(2)}, u32[]{:S(2)}) collective-permute-start(bf16[272,1536]{1,0:T(8,128)(2,1)S(1)} %maximum_select_fusion.5), channel_id=1, source_target_pairs={{0,8},{4,12},{8,0},{12,4},{16,24},{20,28},{24,16},{28,20},{1,9},{5... | collective-permute-start | bytes 2506760 | tf_op jit(solution)/shard_map/ppermute | solution.py:812
  (102 other events, 1085.4 us)
Sparse Core Ops, SparseCore 0:
  11.6 99.0 all-gather.6
  113.1 96.3 all-gather.8
  211.3 47.2 all-gather.10
  260.9 47.2 all-gather.12
  309.8 47.2 all-gather.14
  397.3 47.4 all-gather.16

commit v3 on v2

--- a/solution.py
+++ b/solution.py
@@ -88,6 +88,13 @@
     return lax.dot_general(a, b, dims, preferred_element_type=f32, precision=precision)
 
 
+def pieces_of(values):
+    first = values.astype(bf16)
+    rest = values - first.astype(f32)
+    second = rest.astype(bf16)
+    return first, second, (rest - second.astype(f32)).astype(bf16)
+
+
 def rms_factor(values):
     return lax.rsqrt(jnp.mean(values * values, axis=-1, keepdims=True) + epsilon)
 
@@ -164,7 +171,7 @@
         ref[...] = values[index * count : (index + 1) * count].astype(ref.dtype)
 
 
-QUERY_SPAN = 256
+QUERY_SPAN = 512
 SMALL_ROWS = 128
 
 
@@ -239,7 +246,10 @@
         mid = x_s[...] + acc_s[...]
         middle[...] = mid
         nf = (mid * rms_factor(mid) * gain_ffn[layer : layer + 1, :]).astype(bf16)
-        logits = dot(nf.astype(f32), router[0], precision=highest)
+        spread = dot(nf, jnp.concatenate(pieces_of(router[0]), axis=1))
+        logits = (
+            spread[:, 2 * experts :] + spread[:, experts : 2 * experts] + spread[:, :experts]
+        )
         powers = jnp.exp(logits - jnp.max(logits, axis=-1, keepdims=True))
         prob[...] = powers / jnp.sum(powers, axis=-1, keepdims=True)
         cut(dot(place_matrix(rowid_row[0], experts * buffer[0].shape[0]), nf), buffer)
@@ -371,10 +381,19 @@
         r = rms_factor(mid)
         scaled = mid * r
         gain = gain_ffn[layer : layer + 1, :]
-        nf = (scaled * gain).astype(bf16).astype(f32)
+        nf = (scaled * gain).astype(bf16)
         small_s[...] = jnp.zeros_like(small_s)
-        small_s[:experts] = dot(logit_grad, nf, TN, precision=highest)
-        ffn_in = expert_part + dot(logit_grad, router[0], NT, precision=highest)
+        l1, l2, l3 = pieces_of(logit_grad)
+        w1, w2, w3 = pieces_of(router[0])
+        spread = dot(jnp.concatenate([l1, l2, l3], axis=1), nf, TN)
+        small_s[:experts] = (
+            spread[2 * experts :] + spread[experts : 2 * experts] + spread[:experts]
+        )
+        ffn_in = expert_part + dot(
+            jnp.concatenate([l1, l1, l2, l2, l1, l3], axis=1),
+            jnp.concatenate([w1, w2, w1, w2, w3, w1], axis=1),
+            NT,
+        )
         u = ffn_in * gain
         mg = g + r * (u - scaled * (r * jnp.mean(u * mid, axis=-1, keepdims=True)))
         small_s[experts + 1 : experts + 2] = jnp.sum(ffn_in * scaled, axis=0, keepdims=True)
@@ -954,6 +973,7 @@
     output, gate_grad, *blocks = turn(LAYERS - 1, states[-1], cotangent, common)
     gradient = cotangent
     totals = [None] * LAYERS
+    held = []
     order = jnp.arange(parts, dtype=jnp.int32)
     weight_grads = ()
     for layer in reversed(range(LAYERS)):
@@ -967,12 +987,16 @@
         gback = swap(sent)
         if layer > 0:
             gback, rows_all[layer] = lax.optimization_barrier((gback, rows_all[layer]))
+        else:
+            gback[1], held = lax.optimization_barrier((gback[1], held))
+            totals[1:] = [sum_of_cores(array) for array in held]
+            gback, totals[1:] = lax.optimization_barrier((gback, totals[1:]))
         grads_all = gather_rows(grads)
         results = attend_back(layer, states, gradient, gback, gate_grad, common)
         gradient, payload = results[:2]
         if layer > 0:
             gate_grad, *blocks = results[2:]
-            totals[layer] = sum_of_cores(payload)
+            held.insert(0, payload)
         else:
             payload, grads_all = lax.optimization_barrier((payload, grads_all))
             totals[layer] = sum_of_cores(payload)

time: 643 us -> 636 us (0.989)
  Pallas kernels: 219 us -> 198 us
    pallas_call x2, Pallas kernels: 73.4 us -> 58.5 us  [attend_back(): pl.pallas_call(lambda *refs: attend_back_kernel(layer, experts, refs), gr...]
    ppermute x83, waiting for transfers between devices: 156 us -> 149 us  [partner(): return lax.ppermute(array, axis, pairs)]
  transfers between devices with their start and end apart: 89 -> 89, of which waited for: 27 -> 27; matrix products, arithmetic and copies ran while one was open for 4% -> 4% of each run, Pallas kernels for 30% -> 27%
where the time goes in v3:
time: 636 us; the launch traced here: 628 us
  waiting for transfers between devices  241 us (38%)
  Pallas kernels  198 us (31%)
  starting transfers between devices  115 us (18%)
  other arithmetic  31.4 us (5%)
  local copies, waits for them, and re-layouts  26.5 us (4%)
  between operations  15.6 us (2%)
    ppermute x83, waiting for transfers between devices, partner(): return lax.ppermute(array, axis, pairs)  149 us
    ppermute x83, starting transfers between devices, partner(): return lax.ppermute(array, axis, pairs)  114 us
    all_gather x2, waiting for transfers between devices, gather_weights(): return (lax.all_gather(joined, 'mp', axis=0, tiled=True),)  86.8 us
    pallas_call x2, Pallas kernels, attend_back(): pl.pallas_call(lambda *refs: attend_back_kernel(layer, experts, refs), gr...  58.5 us
    pallas_call x2, Pallas kernels, weight_grad(): pl.pallas_call(weight_grad_kernel, grid_spec=grid_spec, out_shape=[jax.Sh...  38.8 us
    pallas_call x2, Pallas kernels, attend(): pl.pallas_call(lambda *refs: attend_kernel(layer, experts, refs), grid=(g...  34.9 us
    pallas_call x2, Pallas kernels, expert_back(): pl.pallas_call(lambda *refs: expert_back_kernel(experts, refs), grid=(par...  26.5 us
    pallas_call x2, Pallas kernels, expert(): pl.pallas_call(lambda *refs: expert_kernel(experts, refs), grid=(parts,),...  20.7 us
  transfers between devices with their start and end apart: 89, of which 27 were waited for; matrix products, arithmetic and copies ran while one was open for 4% of the time, Pallas kernels for 27%

profile of v3, /device:TPU:0, one launch (start us, length us, event | category | flops | bytes accessed | tf_op | source)
XLA Modules:
  0.0 627.8 jit_solution(15653499170282493203)
XLA Ops:
  7.2 2.6 slice_bitcast_fusion
  17.6 2.3 reduce-window.6
  22.0 16.8 %attend.2 = (bf16[3,512,768]{2,1,0:T(8,128)(2,1)}, bf16[512,768]{1,0:T(8,128)(2,1)}, f32[3,8,512]{2,1,0:T(8,128)}, f32[512,768]{1,0:T(8,128)}, f32[512,8]{1,0:T(...) custom-call(bf16[512,768]{1,0:T(8,128)(2,1)} %refs_16_.3, ...), custom_call_target="tpu_custom_call" | custom-call | flops 1000000 | bytes 1000000 | tf_op jit(solution)/shard_map/attend/pallas_call | solution.py:331
  39.4 2.5 collective-permute-start.1
  41.9 2.8 collective-permute-start.3
  44.7 3.6 collective-permute-start.5
  48.9 2.9 collective-permute-done.2.refs_3_
  51.8 8.6 %collective-permute-done.4.refs_5_ = bf16[72,768]{1,0:T(8,128)(2,1)S(1)} collective-permute-done((bf16[72,768]{1,0:T(8,128)(2,1)}, bf16[72,768]{1,0:T(8,128)(2,1)S(1)}, u32[]{:S(2)}, u32[]{:S(2)}) %collective-permute-start.4) | collective-permute-done | bytes 110624 | tf_op jit(solution)/shard_map/ppermute | solution.py:831
  60.4 50.3 %all-gather.7.cloned.1.call-done.refs_8_.refs_9_.refs_10_ = bf16[6144,768]{1,0:T(8,128)(2,1)} async-done(((bf16[1536,768]{1,0:T(8,128)(2,1)}), bf16[6144,768]{1,0:T(8,128)(2,1)}) %all-gather.7.cloned.1.call-update) | async-done | bytes 9437200 | tf_op jit(solution)/shard_map/all_gather | solution.py:846
  110.7 10.4 %expert.2 = (bf16[576,768]{1,0:T(8,128)(2,1)}, bf16[72,768]{1,0:T(8,128)(2,1)}, bf16[72,768]{1,0:T(8,128)(2,1)}, bf16[72,768]{1,0:T(8,128)(2,1)}, bf16[72,768]{1...) custom-call(bf16[72,768]{1,0:T(8,128)(2,1)} %get-tuple-element.188.r, ...), custom_call_target="tpu_custom_call" | custom-call | flops 1000000 | bytes 1000000 | tf_op jit(solution)/shard_map/expert/pallas_call | solution.py:672
  123.3 2.4 collective-permute-start.10
  125.9 3.3 collective-permute-start.12
  133.1 8.4 %collective-permute-done.11.refs_9_.refs_38_ = bf16[72,768]{1,0:T(8,128)(2,1)S(1)} collective-permute-done((bf16[72,768]{1,0:T(8,128)(2,1)}, bf16[72,768]{1,0:T(8,128)(2,1)S(1)}, u32[]{:S(2)}, u32[]{:S(2)}) %collective-permute-start.11) | collective-permute-done | bytes 110624 | tf_op jit(solution)/shard_map/ppermute | solution.py:831
  142.2 18.1 %attend.3 = (f32[512,768]{1,0:T(8,128)}, bf16[3,512,768]{2,1,0:T(8,128)(2,1)}, bf16[512,768]{1,0:T(8,128)(2,1)}, f32[3,8,512]{2,1,0:T(8,128)}, f32[512,768]{1,0:...) custom-call(f32[512,768]{1,0:T(8,128)} %get-tuple-element.186.refs_0, ...), custom_call_target="tpu_custom_call" | custom-call | flops 1000000 | bytes 1000000 | tf_op jit(solution)/shard_map/attend/pallas_call | solution.py:331
  160.7 5.3 collective-permute-start.15
  166.0 3.2 collective-permute-start.17
  169.6 2.1 collective-permute-start.19
  172.9 36.5 %all-gather.9.cloned.1.call-done.refs_8_.refs_9_.refs_10_ = bf16[6144,768]{1,0:T(8,128)(2,1)} async-done(((bf16[1536,768]{1,0:T(8,128)(2,1)}), bf16[6144,768]{1,0:T(8,128)(2,1)}) %all-gather.9.cloned.1.call-update) | async-done | bytes 9437200 | tf_op jit(solution)/shard_map/all_gather | solution.py:846
  210.2 10.4 %expert.3 = (bf16[576,768]{1,0:T(8,128)(2,1)}, bf16[72,768]{1,0:T(8,128)(2,1)}, bf16[72,768]{1,0:T(8,128)(2,1)}, bf16[72,768]{1,0:T(8,128)(2,1)}, bf16[72,768]{1...) custom-call(bf16[72,768]{1,0:T(8,128)(2,1)} %get-tuple-element.206.r, ...), custom_call_target="tpu_custom_call" | custom-call | flops 1000000 | bytes 1000000 | tf_op jit(solution)/shard_map/expert/pallas_call | solution.py:672
  222.6 2.4 collective-permute-start.24
  225.2 3.3 collective-permute-start.26
  232.4 8.4 %collective-permute-done.25.refs_11_ = bf16[72,768]{1,0:T(8,128)(2,1)S(1)} collective-permute-done((bf16[72,768]{1,0:T(8,128)(2,1)}, bf16[72,768]{1,0:T(8,128)(2,1)S(1)}, u32[]{:S(2)}, u32[]{:S(2)}) %collective-permute-start.25) | collective-permute-done | bytes 110624 | tf_op jit(solution)/shard_map/ppermute | solution.py:831
  241.5 4.8 turn.1
  246.6 5.3 collective-permute-start.29
  251.9 3.2 collective-permute-start.31
  255.5 2.1 collective-permute-start.33
  258.9 2.6 collective-permute-done.30.refs_4_
  261.4 9.1 %collective-permute-done.32.refs_6_ = bf16[72,768]{1,0:T(8,128)(2,1)S(1)} collective-permute-done((bf16[72,768]{1,0:T(8,128)(2,1)}, bf16[72,768]{1,0:T(8,128)(2,1)S(1)}, u32[]{:S(2)}, u32[]{:S(2)}) %collective-permute-start.32) | collective-permute-done | bytes 110624 | tf_op jit(solution)/shard_map/ppermute | solution.py:831
  271.3 13.3 %expert_back.2 = (bf16[576,768]{1,0:T(8,128)(2,1)}, bf16[72,768]{1,0:T(8,128)(2,1)}, bf16[72,768]{1,0:T(8,128)(2,1)}, bf16[72,768]{1,0:T(8,128)(2,1)}, bf16[72,7...) custom-call(bf16[576,768]{1,0:T(8,128)(2,1)} %get-tuple-element.224., ...), custom_call_target="tpu_custom_call" | custom-call | flops 1000000 | bytes 1000000 | tf_op jit(solution)/shard_map/expert_back/pallas_call | solution.py:714
  286.2 5.0 collective-permute-start.36
  291.2 2.1 collective-permute-start.38
  293.6 2.1 collective-permute-start.40
  300.7 8.1 %collective-permute-done.39.refs_13_ = bf16[72,768]{1,0:T(8,128)(2,1)S(1)} collective-permute-done((bf16[72,768]{1,0:T(8,128)(2,1)}, bf16[72,768]{1,0:T(8,128)(2,1)S(1)}, u32[]{:S(2)}, u32[]{:S(2)}) %collective-permute-start.39) | collective-permute-done | bytes 110624 | tf_op jit(solution)/shard_map/ppermute | solution.py:831
  309.6 29.7 %attend_back.2 = (f32[512,768]{1,0:T(8,128)}, bf16[3328,768]{1,0:T(8,128)(2,1)}, f32[512,1]{1,0:T(8,128)}, bf16[72,768]{1,0:T(8,128)(2,1)}, bf16[72,768]{1,0:T(8...) custom-call(bf16[512,768]{1,0:T(8,128)(2,1)} %refs_0_.3, ...), custom_call_target="tpu_custom_call" | custom-call | flops 1000000 | bytes 1000000 | tf_op jit(solution)/shard_map/attend_back/pallas_call | solution.py:560
  340.2 5.2 collective-permute-start.43
  351.6 5.6 all-gather.15.cloned.1.call-done.grads
  357.6 19.4 %weight_grad.2 = (f32[2,1,768,768]{3,2,1,0:T(8,128)}, f32[2,1,768,768]{3,2,1,0:T(8,128)}) custom-call(s32[4]{0:T(128)} %iota.14.order, bf16[2304,768]{1,0:T(8,128)(2,1)} %all-gather.13.cloned.1.call-done.rows, bf16[2304,768]{1,0:T(8,128)(2,1)} %all-gather.15.cloned.1.call-done.grads, bf16[2,1,768,768]{3,2,1,0:T(8,128)(2,1)} %w_in.3, ...), custom_call_target="tpu_custom_call" | custom-call | flops 1000000 | bytes 1000000 | tf_op jit(solution)/shard_map/weight_grad/pallas_call | solution.py:766
  377.8 13.3 %expert_back.3 = (bf16[576,768]{1,0:T(8,128)(2,1)}, bf16[72,768]{1,0:T(8,128)(2,1)}, bf16[72,768]{1,0:T(8,128)(2,1)}, bf16[72,768]{1,0:T(8,128)(2,1)}, bf16[72,7...) custom-call(bf16[576,768]{1,0:T(8,128)(2,1)} %get-tuple-element.233., ...), custom_call_target="tpu_custom_call" | custom-call | flops 1000000 | bytes 1000000 | tf_op jit(solution)/shard_map/expert_back/pallas_call | solution.py:714
  392.8 3.5 constant_dynamic-slice_fusion.13
  398.1 2.4 collective-permute-start.52
  400.8 4.9 collective-permute-done.50.refs_10_
  408.6 3.1 add_convert_fusion.1
  411.8 4.2 collective-permute-done.53.refs_13_
  416.7 28.8 %attend_back.3 = (f32[512,768]{1,0:T(8,128)}, bf16[3328,768]{1,0:T(8,128)(2,1)}) custom-call(f32[512,768]{1,0:T(8,128)} %get-tuple-element.262.refs_0_, s32[2,512,1]{2,1,0:T(8,128)} %get-tuple-element.406.refs_2_.refs_3_.refs_1_.refs_30_, f32[512,1]{1,0:T(8,128)} %get-tuple-element.263.refs_2_, f32[512,8]{1,0:T(8,128)} %get-tuple-element.187.refs_1_.refs_31_.refs_3_, ...), custom_call_target="tpu_custom_call" | custom-call | flops 1000000 | bytes 1000000 | tf_op jit(solution)/shard_map/attend_back/pallas_call | solution.py:560
  445.5 3.4 constant_dynamic-slice_fusion.12
  449.3 4.8 collective-permute-done.57
  454.1 3.1 add_convert_fusion
  463.3 4.8 collective-permute-start.60
  468.6 19.4 %weight_grad.3 = (f32[2,1,768,768]{3,2,1,0:T(8,128)}, f32[2,1,768,768]{3,2,1,0:T(8,128)}) custom-call(s32[4]{0:T(128)} %iota.15.order, bf16[2304,768]{1,0:T(8,128)(2,1)} %all-gather.11.cloned.1.call-done.rows, bf16[2304,768]{1,0:T(8,128)(2,1)} %all-gather.17.cloned.1.call-done.grads, ...), custom_call_target="tpu_custom_call", output_to_operand_aliasing={{0}: (5, {}), {1}: (6, {})} | custom-call | flops 1000000 | bytes 1000000 | tf_op jit(solution)/shard_map/weight_grad/pallas_call | solution.py:766
  496.5 9.9 %collective-permute-done.63 = bf16[136,1536]{1,0:T(8,128)(2,1)} collective-permute-done((bf16[136,1536]{1,0:T(8,128)(2,1)}, bf16[136,1536]{1,0:T(8,128)(2,1)}, u32[]{:S(2)}, u32[]{:S(2)}) %collective-permute-start.63) | collective-permute-done | bytes 417824 | tf_op jit(solution)/shard_map/ppermute | solution.py:831
  513.1 4.5 collective-permute-done.66
  517.9 2.2 collective-permute-start.67
  521.0 2.2 collective-permute-start.69
  523.3 10.5 %collective-permute-done.69 = bf16[34,1536]{1,0:T(8,128)(2,1)S(1)} collective-permute-done((bf16[34,1536]{1,0:T(8,128)(2,1)S(1)}, bf16[34,1536]{1,0:T(8,128)(2,1)S(1)}, u32[]{:S(2)}, u32[]{:S(2)}) %collective-permute-start.69) | collective-permute-done | bytes 104480 | tf_op jit(solution)/shard_map/ppermute | solution.py:831
  534.0 2.9 collective-permute-start.71
  537.0 14.3 %collective-permute-done.72 = bf16[34,1536]{1,0:T(8,128)(2,1)S(1)} collective-permute-done((bf16[34,1536]{1,0:T(8,128)(2,1)S(1)}, bf16[34,1536]{1,0:T(8,128)(2,1)S(1)}, u32[]{:S(2)}, u32[]{:S(2)}) %collective-permute-start.72) | collective-permute-done | bytes 104480 | tf_op jit(solution)/shard_map/ppermute | solution.py:831
  553.9 5.6 collective-permute-done.75
  562.6 2.1 collective-permute-start.78
  564.7 7.3 %collective-permute-done.78 = bf16[136,1536]{1,0:T(8,128)(2,1)S(1)} collective-permute-done((bf16[136,1536]{1,0:T(8,128)(2,1)S(1)}, bf16[136,1536]{1,0:T(8,128)(2,1)S(1)}, u32[]{:S(2)}, u32[]{:S(2)}) %collective-permute-start.78) | collective-permute-done | bytes 417824 | tf_op jit(solution)/shard_map/ppermute | solution.py:831
  572.2 2.5 collective-permute-start.79
  575.4 14.4 %collective-permute-done.81 = bf16[272,1536]{1,0:T(8,128)(2,1)S(1)} collective-permute-done((bf16[272,1536]{1,0:T(8,128)(2,1)S(1)}, bf16[272,1536]{1,0:T(8,128)(2,1)S(1)}, u32[]{:S(2)}, u32[]{:S(2)}) %collective-permute-start.81) | collective-permute-done | bytes 835616 | tf_op jit(solution)/shard_map/ppermute | solution.py:831
  591.9 2.8 pad_maximum_fusion.first
  594.7 8.8 %collective-permute-done.82.second = bf16[1664,1536]{1,0:T(8,128)(2,1)} collective-permute-done((bf16[1664,1536]{1,0:T(8,128)(2,1)}, bf16[1664,1536]{1,0:T(8,128)(2,1)}, u32[]{:S(2)}, u32[]{:S(2)}) %collective-permute-start.82) | collective-permute-done | bytes 5111840 | tf_op jit(solution)/shard_map/ppermute | solution.py:831
  607.1 13.4 %finish.1 = (f32[2,768,2304]{2,1,0:T(8,128)}, f32[2,768,768]{2,1,0:T(8,128)}) custom-call(s32[1]{0:T(128)} %bitcast.11.side, bf16[1664,1536]{1,0:T(8,128)(2,1)} %pad_maximum_fusion.first, bf16[1664,1536]{1,0:T(8,128)(2,1)} %collective-permute-done.82.second), custom_call_target="tpu_custom_call" | custom-call | flops 1000000 | bytes 1000000 | tf_op jit(solution)/shard_map/finish/pallas_call | solution.py:816
  (354 shorter events, 88.8 us)
Async XLA Ops:
  7.2 103.5 %all-gather.7.cloned.1.call-start = ((), (), s32[]{:S(2)}) async-start(), calls=%async_computation | async-start | bytes 11796480 | tf_op jit(solution)/shard_map/all_gather | solution.py:846
  11.5 198.0 %all-gather.9.cloned.1.call-start = ((), (), s32[]{:S(2)}) async-start(), calls=%async_computation.1 | async-start | bytes 11796480 | tf_op jit(solution)/shard_map/all_gather | solution.py:846
  13.1 257.5 %all-gather.11.cloned.1.call-start = ((), (), s32[]{:S(2)}) async-start(), calls=%async_computation.2 | async-start | bytes 4423680 | tf_op jit(solution)/shard_map/all_gather | solution.py:839
  41.8 10.0 %collective-permute-start.2 = (bf16[72,768]{1,0:T(8,128)(2,1)}, bf16[72,768]{1,0:T(8,128)(2,1)S(1)}, u32[]{:S(2)}, u32[]{:S(2)}) collective-permute-start(bf16[72,768]{1,0:T(8,128)(2,1)} %get-tuple-element.191), channel_id=1, source_target_pairs={{0,12},{4,8},{8,4},{12,0},{16,28},{20,24},{24,20},{28,16},{1,13},{... | collective-permute-start | bytes 331784 | tf_op jit(solution)/shard_map/ppermute | solution.py:831
  41.9 9.9 %collective-permute-start.3 = (bf16[72,768]{1,0:T(8,128)(2,1)}, bf16[72,768]{1,0:T(8,128)(2,1)S(1)}, u32[]{:S(2)}, u32[]{:S(2)}) collective-permute-start(bf16[72,768]{1,0:T(8,128)(2,1)} %get-tuple-element.192), channel_id=1, source_target_pairs={{0,16},{4,20},{8,24},{12,28},{16,0},{20,4},{24,8},{28,12},{1,17},{... | collective-permute-start | bytes 331784 | tf_op jit(solution)/shard_map/ppermute | solution.py:831
  44.6 15.7 %collective-permute-start.4 = (bf16[72,768]{1,0:T(8,128)(2,1)}, bf16[72,768]{1,0:T(8,128)(2,1)S(1)}, u32[]{:S(2)}, u32[]{:S(2)}) collective-permute-start(bf16[72,768]{1,0:T(8,128)(2,1)} %get-tuple-element.193), channel_id=1, source_target_pairs={{0,20},{4,16},{8,28},{12,24},{16,4},{20,0},{24,12},{28,8},{1,21},{... | collective-permute-start | bytes 331784 | tf_op jit(solution)/shard_map/ppermute | solution.py:831
  44.7 15.7 %collective-permute-start.5 = (bf16[72,768]{1,0:T(8,128)(2,1)}, bf16[72,768]{1,0:T(8,128)(2,1)S(1)}, u32[]{:S(2)}, u32[]{:S(2)}) collective-permute-start(bf16[72,768]{1,0:T(8,128)(2,1)} %get-tuple-element.194), channel_id=1, source_target_pairs={{0,24},{4,28},{8,16},{12,20},{16,8},{20,12},{24,0},{28,4},{1,25},{... | collective-permute-start | bytes 331784 | tf_op jit(solution)/shard_map/ppermute | solution.py:831
  48.3 12.1 %collective-permute-start.6 = (bf16[72,768]{1,0:T(8,128)(2,1)}, bf16[72,768]{1,0:T(8,128)(2,1)S(1)}, u32[]{:S(2)}, u32[]{:S(2)}) collective-permute-start(bf16[72,768]{1,0:T(8,128)(2,1)} %get-tuple-element.195), channel_id=1, source_target_pairs={{0,28},{4,24},{8,20},{12,16},{16,12},{20,8},{24,4},{28,0},{1,29},{... | collective-permute-start | bytes 331784 | tf_op jit(solution)/shard_map/ppermute | solution.py:831
  121.1 187.8 %all-gather.13.cloned.1.call-start = ((), (), s32[]{:S(2)}) async-start(), calls=%async_computation.3 | async-start | bytes 4423680 | tf_op jit(solution)/shard_map/all_gather | solution.py:839
  121.5 9.7 %collective-permute-start.8 = (bf16[72,768]{1,0:T(8,128)(2,1)}, bf16[72,768]{1,0:T(8,128)(2,1)S(1)}, u32[]{:S(2)}, u32[]{:S(2)}) collective-permute-start(bf16[72,768]{1,0:T(8,128)(2,1)} %get-tuple-element.198), channel_id=1, source_target_pairs={{0,8},{4,12},{8,0},{12,4},{16,24},{20,28},{24,16},{28,20},{1,9},{5... | collective-permute-start | bytes 331784 | tf_op jit(solution)/shard_map/ppermute | solution.py:831
  123.0 10.0 %collective-permute-start.9 = (bf16[72,768]{1,0:T(8,128)(2,1)}, bf16[72,768]{1,0:T(8,128)(2,1)S(1)}, u32[]{:S(2)}, u32[]{:S(2)}) collective-permute-start(bf16[72,768]{1,0:T(8,128)(2,1)} %get-tuple-element.199), channel_id=1, source_target_pairs={{0,12},{4,8},{8,4},{12,0},{16,28},{20,24},{24,20},{28,16},{1,13},{... | collective-permute-start | bytes 331784 | tf_op jit(solution)/shard_map/ppermute | solution.py:831
  123.3 9.7 %collective-permute-start.10 = (bf16[72,768]{1,0:T(8,128)(2,1)}, bf16[72,768]{1,0:T(8,128)(2,1)S(1)}, u32[]{:S(2)}, u32[]{:S(2)}) collective-permute-start(bf16[72,768]{1,0:T(8,128)(2,1)} %get-tuple-element.200), channel_id=1, source_target_pairs={{0,16},{4,20},{8,24},{12,28},{16,0},{20,4},{24,8},{28,12},{1,17},{... | collective-permute-start | bytes 331784 | tf_op jit(solution)/shard_map/ppermute | solution.py:831
  125.7 15.7 %collective-permute-start.11 = (bf16[72,768]{1,0:T(8,128)(2,1)}, bf16[72,768]{1,0:T(8,128)(2,1)S(1)}, u32[]{:S(2)}, u32[]{:S(2)}) collective-permute-start(bf16[72,768]{1,0:T(8,128)(2,1)} %get-tuple-element.201), channel_id=1, source_target_pairs={{0,20},{4,16},{8,28},{12,24},{16,4},{20,0},{24,12},{28,8},{1,21},{... | collective-permute-start | bytes 331784 | tf_op jit(solution)/shard_map/ppermute | solution.py:831
  125.9 15.5 %collective-permute-start.12 = (bf16[72,768]{1,0:T(8,128)(2,1)}, bf16[72,768]{1,0:T(8,128)(2,1)S(1)}, u32[]{:S(2)}, u32[]{:S(2)}) collective-permute-start(bf16[72,768]{1,0:T(8,128)(2,1)} %get-tuple-element.202), channel_id=1, source_target_pairs={{0,24},{4,28},{8,16},{12,20},{16,8},{20,12},{24,0},{28,4},{1,25},{... | collective-permute-start | bytes 331784 | tf_op jit(solution)/shard_map/ppermute | solution.py:831
  131.2 10.3 %collective-permute-start.13 = (bf16[72,768]{1,0:T(8,128)(2,1)}, bf16[72,768]{1,0:T(8,128)(2,1)S(1)}, u32[]{:S(2)}, u32[]{:S(2)}) collective-permute-start(bf16[72,768]{1,0:T(8,128)(2,1)} %get-tuple-element.203), channel_id=1, source_target_pairs={{0,28},{4,24},{8,20},{12,16},{16,12},{20,8},{24,4},{28,0},{1,29},{... | collective-permute-start | bytes 331784 | tf_op jit(solution)/shard_map/ppermute | solution.py:831
  160.7 11.0 %collective-permute-start.15 = (bf16[72,768]{1,0:T(8,128)(2,1)}, bf16[72,768]{1,0:T(8,128)(2,1)S(1)}, u32[]{:S(2)}, u32[]{:S(2)}) collective-permute-start(bf16[72,768]{1,0:T(8,128)(2,1)} %get-tuple-element.208), channel_id=1, source_target_pairs={{0,8},{4,12},{8,0},{12,4},{16,24},{20,28},{24,16},{28,20},{1,9},{5... | collective-permute-start | bytes 331784 | tf_op jit(solution)/shard_map/ppermute | solution.py:831
  166.0 43.4 %collective-permute-start.16 = (bf16[72,768]{1,0:T(8,128)(2,1)}, bf16[72,768]{1,0:T(8,128)(2,1)S(1)}, u32[]{:S(2)}, u32[]{:S(2)}) collective-permute-start(bf16[72,768]{1,0:T(8,128)(2,1)} %get-tuple-element.209), channel_id=1, source_target_pairs={{0,12},{4,8},{8,4},{12,0},{16,28},{20,24},{24,20},{28,16},{1,13},{... | collective-permute-start | bytes 331784 | tf_op jit(solution)/shard_map/ppermute | solution.py:831
  166.0 43.4 %collective-permute-start.17 = (bf16[72,768]{1,0:T(8,128)(2,1)}, bf16[72,768]{1,0:T(8,128)(2,1)S(1)}, u32[]{:S(2)}, u32[]{:S(2)}) collective-permute-start(bf16[72,768]{1,0:T(8,128)(2,1)} %get-tuple-element.210), channel_id=1, source_target_pairs={{0,16},{4,20},{8,24},{12,28},{16,0},{20,4},{24,8},{28,12},{1,17},{... | collective-permute-start | bytes 331784 | tf_op jit(solution)/shard_map/ppermute | solution.py:831
  169.3 40.2 %collective-permute-start.18 = (bf16[72,768]{1,0:T(8,128)(2,1)}, bf16[72,768]{1,0:T(8,128)(2,1)S(1)}, u32[]{:S(2)}, u32[]{:S(2)}) collective-permute-start(bf16[72,768]{1,0:T(8,128)(2,1)} %get-tuple-element.211), channel_id=1, source_target_pairs={{0,20},{4,16},{8,28},{12,24},{16,4},{20,0},{24,12},{28,8},{1,21},{... | collective-permute-start | bytes 331784 | tf_op jit(solution)/shard_map/ppermute | solution.py:831
  169.6 39.9 %collective-permute-start.19 = (bf16[72,768]{1,0:T(8,128)(2,1)}, bf16[72,768]{1,0:T(8,128)(2,1)S(1)}, u32[]{:S(2)}, u32[]{:S(2)}) collective-permute-start(bf16[72,768]{1,0:T(8,128)(2,1)} %get-tuple-element.212), channel_id=1, source_target_pairs={{0,24},{4,28},{8,16},{12,20},{16,8},{20,12},{24,0},{28,4},{1,25},{... | collective-permute-start | bytes 331784 | tf_op jit(solution)/shard_map/ppermute | solution.py:831
  171.7 37.8 %collective-permute-start.20 = (bf16[72,768]{1,0:T(8,128)(2,1)}, bf16[72,768]{1,0:T(8,128)(2,1)S(1)}, u32[]{:S(2)}, u32[]{:S(2)}) collective-permute-start(bf16[72,768]{1,0:T(8,128)(2,1)} %get-tuple-element.213), channel_id=1, source_target_pairs={{0,28},{4,24},{8,20},{12,16},{16,12},{20,8},{24,4},{28,0},{1,29},{... | collective-permute-start | bytes 331784 | tf_op jit(solution)/shard_map/ppermute | solution.py:831
  220.6 136.5 %all-gather.15.cloned.1.call-start = ((), (), s32[]{:S(2)}) async-start(), calls=%async_computation.4 | async-start | bytes 4423680 | tf_op jit(solution)/shard_map/all_gather | solution.py:839
  220.8 9.7 %collective-permute-start.22 = (bf16[72,768]{1,0:T(8,128)(2,1)}, bf16[72,768]{1,0:T(8,128)(2,1)S(1)}, u32[]{:S(2)}, u32[]{:S(2)}) collective-permute-start(bf16[72,768]{1,0:T(8,128)(2,1)} %get-tuple-element.216), channel_id=1, source_target_pairs={{0,8},{4,12},{8,0},{12,4},{16,24},{20,28},{24,16},{28,20},{1,9},{5... | collective-permute-start | bytes 331784 | tf_op jit(solution)/shard_map/ppermute | solution.py:831
  222.3 10.0 %collective-permute-start.23 = (bf16[72,768]{1,0:T(8,128)(2,1)}, bf16[72,768]{1,0:T(8,128)(2,1)S(1)}, u32[]{:S(2)}, u32[]{:S(2)}) collective-permute-start(bf16[72,768]{1,0:T(8,128)(2,1)} %get-tuple-element.217), channel_id=1, source_target_pairs={{0,12},{4,8},{8,4},{12,0},{16,28},{20,24},{24,20},{28,16},{1,13},{... | collective-permute-start | bytes 331784 | tf_op jit(solution)/shard_map/ppermute | solution.py:831
  222.6 9.7 %collective-permute-start.24 = (bf16[72,768]{1,0:T(8,128)(2,1)}, bf16[72,768]{1,0:T(8,128)(2,1)S(1)}, u32[]{:S(2)}, u32[]{:S(2)}) collective-permute-start(bf16[72,768]{1,0:T(8,128)(2,1)} %get-tuple-element.218), channel_id=1, source_target_pairs={{0,16},{4,20},{8,24},{12,28},{16,0},{20,4},{24,8},{28,12},{1,17},{... | collective-permute-start | bytes 331784 | tf_op jit(solution)/shard_map/ppermute | solution.py:831
  225.0 15.7 %collective-permute-start.25 = (bf16[72,768]{1,0:T(8,128)(2,1)}, bf16[72,768]{1,0:T(8,128)(2,1)S(1)}, u32[]{:S(2)}, u32[]{:S(2)}) collective-permute-start(bf16[72,768]{1,0:T(8,128)(2,1)} %get-tuple-element.219), channel_id=1, source_target_pairs={{0,20},{4,16},{8,28},{12,24},{16,4},{20,0},{24,12},{28,8},{1,21},{... | collective-permute-start | bytes 331784 | tf_op jit(solution)/shard_map/ppermute | solution.py:831
  225.2 15.5 %collective-permute-start.26 = (bf16[72,768]{1,0:T(8,128)(2,1)}, bf16[72,768]{1,0:T(8,128)(2,1)S(1)}, u32[]{:S(2)}, u32[]{:S(2)}) collective-permute-start(bf16[72,768]{1,0:T(8,128)(2,1)} %get-tuple-element.220), channel_id=1, source_target_pairs={{0,24},{4,28},{8,16},{12,20},{16,8},{20,12},{24,0},{28,4},{1,25},{... | collective-permute-start | bytes 331784 | tf_op jit(solution)/shard_map/ppermute | solution.py:831
  230.5 10.3 %collective-permute-start.27 = (bf16[72,768]{1,0:T(8,128)(2,1)}, bf16[72,768]{1,0:T(8,128)(2,1)S(1)}, u32[]{:S(2)}, u32[]{:S(2)}) collective-permute-start(bf16[72,768]{1,0:T(8,128)(2,1)} %get-tuple-element.221), channel_id=1, source_target_pairs={{0,28},{4,24},{8,20},{12,16},{16,12},{20,8},{24,4},{28,0},{1,29},{... | collective-permute-start | bytes 331784 | tf_op jit(solution)/shard_map/ppermute | solution.py:831
  246.6 11.0 %collective-permute-start.29 = (bf16[72,768]{1,0:T(8,128)(2,1)}, bf16[72,768]{1,0:T(8,128)(2,1)S(1)}, u32[]{:S(2)}, u32[]{:S(2)}) collective-permute-start(bf16[72,768]{1,0:T(8,128)(2,1)} %get-tuple-element.227), channel_id=1, source_target_pairs={{0,8},{4,12},{8,0},{12,4},{16,24},{20,28},{24,16},{28,20},{1,9},{5... | collective-permute-start | bytes 331784 | tf_op jit(solution)/shard_map/ppermute | solution.py:831
  255.2 15.4 %collective-permute-start.32 = (bf16[72,768]{1,0:T(8,128)(2,1)}, bf16[72,768]{1,0:T(8,128)(2,1)S(1)}, u32[]{:S(2)}, u32[]{:S(2)}) collective-permute-start(bf16[72,768]{1,0:T(8,128)(2,1)} %get-tuple-element.230), channel_id=1, source_target_pairs={{0,20},{4,16},{8,28},{12,24},{16,4},{20,0},{24,12},{28,8},{1,21},{... | collective-permute-start | bytes 331784 | tf_op jit(solution)/shard_map/ppermute | solution.py:831
  255.5 15.0 %collective-permute-start.33 = (bf16[72,768]{1,0:T(8,128)(2,1)}, bf16[72,768]{1,0:T(8,128)(2,1)S(1)}, u32[]{:S(2)}, u32[]{:S(2)}) collective-permute-start(bf16[72,768]{1,0:T(8,128)(2,1)} %get-tuple-element.231), channel_id=1, source_target_pairs={{0,24},{4,28},{8,16},{12,20},{16,8},{20,12},{24,0},{28,4},{1,25},{... | collective-permute-start | bytes 331784 | tf_op jit(solution)/shard_map/ppermute | solution.py:831
  257.6 13.0 %collective-permute-start.34 = (bf16[72,768]{1,0:T(8,128)(2,1)}, bf16[72,768]{1,0:T(8,128)(2,1)S(1)}, u32[]{:S(2)}, u32[]{:S(2)}) collective-permute-start(bf16[72,768]{1,0:T(8,128)(2,1)} %get-tuple-element.232), channel_id=1, source_target_pairs={{0,28},{4,24},{8,20},{12,16},{16,12},{20,8},{24,4},{28,0},{1,29},{... | collective-permute-start | bytes 331784 | tf_op jit(solution)/shard_map/ppermute | solution.py:831
  284.6 160.9 %all-gather.17.cloned.1.call-start = ((), (), s32[]{:S(2)}) async-start(), calls=%async_computation.5 | async-start | bytes 4423680 | tf_op jit(solution)/shard_map/all_gather | solution.py:839
  293.3 15.5 %collective-permute-start.39 = (bf16[72,768]{1,0:T(8,128)(2,1)}, bf16[72,768]{1,0:T(8,128)(2,1)S(1)}, u32[]{:S(2)}, u32[]{:S(2)}) collective-permute-start(bf16[72,768]{1,0:T(8,128)(2,1)} %get-tuple-element.247), channel_id=1, source_target_pairs={{0,20},{4,16},{8,28},{12,24},{16,4},{20,0},{24,12},{28,8},{1,21},{... | collective-permute-start | bytes 331784 | tf_op jit(solution)/shard_map/ppermute | solution.py:831
  293.6 15.2 %collective-permute-start.40 = (bf16[72,768]{1,0:T(8,128)(2,1)}, bf16[72,768]{1,0:T(8,128)(2,1)S(1)}, u32[]{:S(2)}, u32[]{:S(2)}) collective-permute-start(bf16[72,768]{1,0:T(8,128)(2,1)} %get-tuple-element.248), channel_id=1, source_target_pairs={{0,24},{4,28},{8,16},{12,20},{16,8},{20,12},{24,0},{28,4},{1,25},{... | collective-permute-start | bytes 331784 | tf_op jit(solution)/shard_map/ppermute | solution.py:831
  295.7 13.1 %collective-permute-start.41 = (bf16[72,768]{1,0:T(8,128)(2,1)}, bf16[72,768]{1,0:T(8,128)(2,1)S(1)}, u32[]{:S(2)}, u32[]{:S(2)}) collective-permute-start(bf16[72,768]{1,0:T(8,128)(2,1)} %get-tuple-element.249), channel_id=1, source_target_pairs={{0,28},{4,24},{8,20},{12,16},{16,12},{20,8},{24,4},{28,0},{1,29},{... | collective-permute-start | bytes 331784 | tf_op jit(solution)/shard_map/ppermute | solution.py:831
  340.2 9.6 %collective-permute-start.43 = (bf16[72,768]{1,0:T(8,128)(2,1)}, bf16[72,768]{1,0:T(8,128)(2,1)S(1)}, u32[]{:S(2)}, u32[]{:S(2)}) collective-permute-start(bf16[72,768]{1,0:T(8,128)(2,1)} %get-tuple-element.266), channel_id=1, source_target_pairs={{0,8},{4,12},{8,0},{12,4},{16,24},{20,28},{24,16},{28,20},{1,9},{5... | collective-permute-start | bytes 331784 | tf_op jit(solution)/shard_map/ppermute | solution.py:831
  345.4 31.7 %collective-permute-start.44 = (bf16[72,768]{1,0:T(8,128)(2,1)}, bf16[72,768]{1,0:T(8,128)(2,1)S(1)}, u32[]{:S(2)}, u32[]{:S(2)}) collective-permute-start(bf16[72,768]{1,0:T(8,128)(2,1)} %get-tuple-element.267), channel_id=1, source_target_pairs={{0,12},{4,8},{8,4},{12,0},{16,28},{20,24},{24,20},{28,16},{1,13},{... | collective-permute-start | bytes 331784 | tf_op jit(solution)/shard_map/ppermute | solution.py:831
  345.4 31.7 %collective-permute-start.45 = (bf16[72,768]{1,0:T(8,128)(2,1)}, bf16[72,768]{1,0:T(8,128)(2,1)S(1)}, u32[]{:S(2)}, u32[]{:S(2)}) collective-permute-start(bf16[72,768]{1,0:T(8,128)(2,1)} %get-tuple-element.268), channel_id=1, source_target_pairs={{0,16},{4,20},{8,24},{12,28},{16,0},{20,4},{24,8},{28,12},{1,17},{... | collective-permute-start | bytes 331784 | tf_op jit(solution)/shard_map/ppermute | solution.py:831
  347.4 29.7 %collective-permute-start.46 = (bf16[72,768]{1,0:T(8,128)(2,1)}, bf16[72,768]{1,0:T(8,128)(2,1)S(1)}, u32[]{:S(2)}, u32[]{:S(2)}) collective-permute-start(bf16[72,768]{1,0:T(8,128)(2,1)} %get-tuple-element.269), channel_id=1, source_target_pairs={{0,20},{4,16},{8,28},{12,24},{16,4},{20,0},{24,12},{28,8},{1,21},{... | collective-permute-start | bytes 331784 | tf_op jit(solution)/shard_map/ppermute | solution.py:831
  347.8 29.3 %collective-permute-start.47 = (bf16[72,768]{1,0:T(8,128)(2,1)}, bf16[72,768]{1,0:T(8,128)(2,1)S(1)}, u32[]{:S(2)}, u32[]{:S(2)}) collective-permute-start(bf16[72,768]{1,0:T(8,128)(2,1)} %get-tuple-element.270), channel_id=1, source_target_pairs={{0,24},{4,28},{8,16},{12,20},{16,8},{20,12},{24,0},{28,4},{1,25},{... | collective-permute-start | bytes 331784 | tf_op jit(solution)/shard_map/ppermute | solution.py:831
  349.8 27.3 %collective-permute-start.48 = (bf16[72,768]{1,0:T(8,128)(2,1)}, bf16[72,768]{1,0:T(8,128)(2,1)S(1)}, u32[]{:S(2)}, u32[]{:S(2)}) collective-permute-start(bf16[72,768]{1,0:T(8,128)(2,1)} %get-tuple-element.271), channel_id=1, source_target_pairs={{0,28},{4,24},{8,20},{12,16},{16,12},{20,8},{24,4},{28,0},{1,29},{... | collective-permute-start | bytes 331784 | tf_op jit(solution)/shard_map/ppermute | solution.py:831
  396.2 10.9 %collective-permute-start.56 = (bf16[1664,768]{1,0:T(8,128)(2,1)}, bf16[1664,768]{1,0:T(8,128)(2,1)S(1)}, u32[]{:S(2)}, u32[]{:S(2)}) collective-permute-start(bf16[1664,768]{1,0:T(8,128)(2,1)} %constant_dynamic-slice_fusion.13), channel_id=1, source_target_pairs={{0,4},{4,0},{8,12},{12,8},{16,20},{20,16},{24,28},{28,24},{1,5},{5... | collective-permute-start | bytes 7667720 | tf_op jit(solution)/shard_map/ppermute | solution.py:831
  397.9 13.9 %collective-permute-start.51 = (bf16[72,768]{1,0:T(8,128)(2,1)S(1)}, bf16[72,768]{1,0:T(8,128)(2,1)S(1)}, u32[]{:S(2)}, u32[]{:S(2)}) collective-permute-start(bf16[72,768]{1,0:T(8,128)(2,1)S(1)} %copy-done.71), channel_id=1, source_target_pairs={{0,12},{4,8},{8,4},{12,0},{16,28},{20,24},{24,20},{28,16},{1,13},{... | collective-permute-start | bytes 331784 | tf_op jit(solution)/shard_map/ppermute | solution.py:831
  398.1 13.7 %collective-permute-start.52 = (bf16[72,768]{1,0:T(8,128)(2,1)S(1)}, bf16[72,768]{1,0:T(8,128)(2,1)S(1)}, u32[]{:S(2)}, u32[]{:S(2)}) collective-permute-start(bf16[72,768]{1,0:T(8,128)(2,1)S(1)} %copy-done.70), channel_id=1, source_target_pairs={{0,16},{4,20},{8,24},{12,28},{16,0},{20,4},{24,8},{28,12},{1,17},{... | collective-permute-start | bytes 331784 | tf_op jit(solution)/shard_map/ppermute | solution.py:831
  400.5 15.5 %collective-permute-start.53 = (bf16[72,768]{1,0:T(8,128)(2,1)S(1)}, bf16[72,768]{1,0:T(8,128)(2,1)S(1)}, u32[]{:S(2)}, u32[]{:S(2)}) collective-permute-start(bf16[72,768]{1,0:T(8,128)(2,1)S(1)} %copy-done.69), channel_id=1, source_target_pairs={{0,20},{4,16},{8,28},{12,24},{16,4},{20,0},{24,12},{28,8},{1,21},{... | collective-permute-start | bytes 331784 | tf_op jit(solution)/shard_map/ppermute | solution.py:831
  405.7 10.3 %collective-permute-start.54 = (bf16[72,768]{1,0:T(8,128)(2,1)S(1)}, bf16[72,768]{1,0:T(8,128)(2,1)S(1)}, u32[]{:S(2)}, u32[]{:S(2)}) collective-permute-start(bf16[72,768]{1,0:T(8,128)(2,1)S(1)} %copy-done.68), channel_id=1, source_target_pairs={{0,24},{4,28},{8,16},{12,20},{16,8},{20,12},{24,0},{28,4},{1,25},{... | collective-permute-start | bytes 331784 | tf_op jit(solution)/shard_map/ppermute | solution.py:831
  459.0 29.1 %collective-permute-start.58 = (bf16[280,1536]{1,0:T(8,128)(2,1)}, bf16[280,1536]{1,0:T(8,128)(2,1)}, u32[]{:S(2)}, u32[]{:S(2)}) collective-permute-start(bf16[280,1536]{1,0:T(8,128)(2,1)} %constant_dynamic-slice_fusion.11), channel_id=1, source_target_pairs={{0,1},{1,0},{2,3},{3,2},{4,5},{5,4},{6,7},{7,6},{8,9},{9,8},{10,11... | collective-permute-start | bytes 2580488 | tf_op jit(solution)/shard_map/ppermute | solution.py:831
  461.6 26.5 %collective-permute-start.59 = (bf16[280,1536]{1,0:T(8,128)(2,1)}, bf16[280,1536]{1,0:T(8,128)(2,1)}, u32[]{:S(2)}, u32[]{:S(2)}) collective-permute-start(bf16[280,1536]{1,0:T(8,128)(2,1)} %constant_dynamic-slice_fusion.10), channel_id=1, source_target_pairs={{0,2},{1,3},{2,0},{3,1},{4,6},{5,7},{6,4},{7,5},{8,10},{9,11},{10,... | collective-permute-start | bytes 2580488 | tf_op jit(solution)/shard_map/ppermute | solution.py:831
  463.3 24.8 %collective-permute-start.60 = (bf16[272,1536]{1,0:T(8,128)(2,1)}, bf16[272,1536]{1,0:T(8,128)(2,1)}, u32[]{:S(2)}, u32[]{:S(2)}) collective-permute-start(bf16[272,1536]{1,0:T(8,128)(2,1)} %constant_dynamic-slice_fusion.9), channel_id=1, source_target_pairs={{0,8},{4,12},{8,0},{12,4},{16,24},{20,28},{24,16},{28,20},{1,9},{5... | collective-permute-start | bytes 2506760 | tf_op jit(solution)/shard_map/ppermute | solution.py:831
  492.9 13.5 %collective-permute-start.61 = (bf16[140,1536]{1,0:T(8,128)(2,1)S(1)}, bf16[140,1536]{1,0:T(8,128)(2,1)S(1)}, u32[]{:S(2)}, u32[]{:S(2)}) collective-permute-start(bf16[140,1536]{1,0:T(8,128)(2,1)S(1)} %constant_dynamic-slice_fusion.8), channel_id=1, source_target_pairs={{0,2},{1,3},{2,0},{3,1},{4,6},{5,7},{6,4},{7,5},{8,10},{9,11},{10,... | collective-permute-start | bytes 1290248 | tf_op jit(solution)/shard_map/ppermute | solution.py:831
  494.5 11.9 %collective-permute-start.62 = (bf16[140,1536]{1,0:T(8,128)(2,1)S(1)}, bf16[140,1536]{1,0:T(8,128)(2,1)S(1)}, u32[]{:S(2)}, u32[]{:S(2)}) collective-permute-start(bf16[140,1536]{1,0:T(8,128)(2,1)S(1)} %constant_dynamic-slice_fusion.7), channel_id=1, source_target_pairs={{0,8},{4,12},{8,0},{12,4},{16,24},{20,28},{24,16},{28,20},{1,9},{5... | collective-permute-start | bytes 1290248 | tf_op jit(solution)/shard_map/ppermute | solution.py:831
  495.9 10.5 %collective-permute-start.63 = (bf16[136,1536]{1,0:T(8,128)(2,1)}, bf16[136,1536]{1,0:T(8,128)(2,1)}, u32[]{:S(2)}, u32[]{:S(2)}) collective-permute-start(bf16[136,1536]{1,0:T(8,128)(2,1)} %constant_dynamic-slice_fusion.6), channel_id=1, source_target_pairs={{0,1},{1,0},{2,3},{3,2},{4,5},{5,4},{6,7},{7,6},{8,9},{9,8},{10,11... | collective-permute-start | bytes 1253384 | tf_op jit(solution)/shard_map/ppermute | solution.py:831
  517.9 15.9 %collective-permute-start.67 = (bf16[35,1536]{1,0:T(8,128)(2,1)S(1)}, bf16[35,1536]{1,0:T(8,128)(2,1)S(1)}, u32[]{:S(2)}, u32[]{:S(2)}) collective-permute-start(bf16[35,1536]{1,0:T(8,128)(2,1)S(1)} %constant_dynamic-slice_fusion.2), channel_id=1, source_target_pairs={{0,16},{4,20},{8,24},{12,28},{16,0},{20,4},{24,8},{28,12},{1,17},{... | collective-permute-start | bytes 322568 | tf_op jit(solution)/shard_map/ppermute | solution.py:831
  520.2 13.6 %collective-permute-start.68 = (bf16[35,1536]{1,0:T(8,128)(2,1)S(1)}, bf16[35,1536]{1,0:T(8,128)(2,1)S(1)}, u32[]{:S(2)}, u32[]{:S(2)}) collective-permute-start(bf16[35,1536]{1,0:T(8,128)(2,1)S(1)} %constant_dynamic-slice_fusion.1), channel_id=1, source_target_pairs={{0,16},{4,20},{8,24},{12,28},{16,0},{20,4},{24,8},{28,12},{1,17},{... | collective-permute-start | bytes 322568 | tf_op jit(solution)/shard_map/ppermute | solution.py:831
  521.0 12.8 %collective-permute-start.69 = (bf16[34,1536]{1,0:T(8,128)(2,1)S(1)}, bf16[34,1536]{1,0:T(8,128)(2,1)S(1)}, u32[]{:S(2)}, u32[]{:S(2)}) collective-permute-start(bf16[34,1536]{1,0:T(8,128)(2,1)S(1)} %constant_dynamic-slice_fusion), channel_id=1, source_target_pairs={{0,16},{4,20},{8,24},{12,28},{16,0},{20,4},{24,8},{28,12},{1,17},{... | collective-permute-start | bytes 313352 | tf_op jit(solution)/shard_map/ppermute | solution.py:831
  534.0 17.4 %collective-permute-start.70 = (bf16[35,1536]{1,0:T(8,128)(2,1)S(1)}, bf16[35,1536]{1,0:T(8,128)(2,1)S(1)}, u32[]{:S(2)}, u32[]{:S(2)}) collective-permute-start(bf16[35,1536]{1,0:T(8,128)(2,1)S(1)} %add_convert_fusion.13), channel_id=1, source_target_pairs={{0,16},{4,20},{8,24},{12,28},{16,0},{20,4},{24,8},{28,12},{1,17},{... | collective-permute-start | bytes 322568 | tf_op jit(solution)/shard_map/ppermute | solution.py:831
  534.0 17.3 %collective-permute-start.71 = (bf16[35,1536]{1,0:T(8,128)(2,1)S(1)}, bf16[35,1536]{1,0:T(8,128)(2,1)S(1)}, u32[]{:S(2)}, u32[]{:S(2)}) collective-permute-start(bf16[35,1536]{1,0:T(8,128)(2,1)S(1)} %add_convert_fusion.12), channel_id=1, source_target_pairs={{0,16},{4,20},{8,24},{12,28},{16,0},{20,4},{24,8},{28,12},{1,17},{... | collective-permute-start | bytes 322568 | tf_op jit(solution)/shard_map/ppermute | solution.py:831
  537.0 14.4 %collective-permute-start.72 = (bf16[34,1536]{1,0:T(8,128)(2,1)S(1)}, bf16[34,1536]{1,0:T(8,128)(2,1)S(1)}, u32[]{:S(2)}, u32[]{:S(2)}) collective-permute-start(bf16[34,1536]{1,0:T(8,128)(2,1)S(1)} %add_convert_fusion.11), channel_id=1, source_target_pairs={{0,16},{4,20},{8,24},{12,28},{16,0},{20,4},{24,8},{28,12},{1,17},{... | collective-permute-start | bytes 313352 | tf_op jit(solution)/shard_map/ppermute | solution.py:831
  559.7 12.3 %collective-permute-start.76 = (bf16[140,1536]{1,0:T(8,128)(2,1)S(1)}, bf16[140,1536]{1,0:T(8,128)(2,1)S(1)}, u32[]{:S(2)}, u32[]{:S(2)}) collective-permute-start(bf16[140,1536]{1,0:T(8,128)(2,1)S(1)} %maximum_select_fusion.6), channel_id=1, source_target_pairs={{0,2},{1,3},{2,0},{3,1},{4,6},{5,7},{6,4},{7,5},{8,10},{9,11},{10,... | collective-permute-start | bytes 1290248 | tf_op jit(solution)/shard_map/ppermute | solution.py:831
  560.4 11.5 %collective-permute-start.77 = (bf16[140,1536]{1,0:T(8,128)(2,1)S(1)}, bf16[140,1536]{1,0:T(8,128)(2,1)S(1)}, u32[]{:S(2)}, u32[]{:S(2)}) collective-permute-start(bf16[140,1536]{1,0:T(8,128)(2,1)S(1)} %maximum_select_fusion.7), channel_id=1, source_target_pairs={{0,8},{4,12},{8,0},{12,4},{16,24},{20,28},{24,16},{28,20},{1,9},{5... | collective-permute-start | bytes 1290248 | tf_op jit(solution)/shard_map/ppermute | solution.py:831
  572.2 17.6 %collective-permute-start.79 = (bf16[280,1536]{1,0:T(8,128)(2,1)S(1)}, bf16[280,1536]{1,0:T(8,128)(2,1)S(1)}, u32[]{:S(2)}, u32[]{:S(2)}) collective-permute-start(bf16[280,1536]{1,0:T(8,128)(2,1)S(1)} %maximum_select_fusion.3), channel_id=1, source_target_pairs={{0,1},{1,0},{2,3},{3,2},{4,5},{5,4},{6,7},{7,6},{8,9},{9,8},{10,11... | collective-permute-start | bytes 2580488 | tf_op jit(solution)/shard_map/ppermute | solution.py:831
  575.0 14.8 %collective-permute-start.80 = (bf16[280,1536]{1,0:T(8,128)(2,1)S(1)}, bf16[280,1536]{1,0:T(8,128)(2,1)S(1)}, u32[]{:S(2)}, u32[]{:S(2)}) collective-permute-start(bf16[280,1536]{1,0:T(8,128)(2,1)S(1)} %maximum_select_fusion.4), channel_id=1, source_target_pairs={{0,2},{1,3},{2,0},{3,1},{4,6},{5,7},{6,4},{7,5},{8,10},{9,11},{10,... | collective-permute-start | bytes 2580488 | tf_op jit(solution)/shard_map/ppermute | solution.py:831
  575.3 14.5 %collective-permute-start.81 = (bf16[272,1536]{1,0:T(8,128)(2,1)S(1)}, bf16[272,1536]{1,0:T(8,128)(2,1)S(1)}, u32[]{:S(2)}, u32[]{:S(2)}) collective-permute-start(bf16[272,1536]{1,0:T(8,128)(2,1)S(1)} %maximum_select_fusion.5), channel_id=1, source_target_pairs={{0,8},{4,12},{8,0},{12,4},{16,24},{20,28},{24,16},{28,20},{1,9},{5... | collective-permute-start | bytes 2506760 | tf_op jit(solution)/shard_map/ppermute | solution.py:831
  (98 other events, 1056.3 us)
Sparse Core Ops, SparseCore 0:
  11.6 99.0 all-gather.6
  113.1 96.3 all-gather.8
  211.3 47.2 all-gather.10
  260.9 47.2 all-gather.12
  309.8 47.2 all-gather.14
  391.2 47.2 all-gather.16
